TPU v7x, 32 devices: a whole 2x2x4 slice. The times are simulated.
32 devices in a mesh: clip: 4 (over z), seq: 8 (over y, x, core).
Axes of the slice: x: 2, y: 2, z: 4, core: 2. Of those that a mesh axis runs over, the one named last changes fastest.
Arguments:
- tokens: bfloat16 [4, 16, 256, 1152], P('clip', 'seq'), may hold values from -4 to 4
- text: bfloat16 [4, 120, 1152], P('clip'), may hold values from -4 to 4
- timesteps: int32 [4], replicated, may hold values from 0 to 999
- text_counts: int32 [4], P('clip'), may hold values from 1 to 120
- out_grad: bfloat16 [4, 16, 256, 1152], P('clip', 'seq'), may hold values from -3 to 3
- time_weight: bfloat16 [1152, 6912], P(('clip', 'seq')), may hold values from -0.1875 to 0.1875
- s_qkv: bfloat16 [1, 1152, 3456], P(None, ('clip', 'seq')), may hold values from -0.1875 to 0.1875
- s_proj: bfloat16 [1, 1152, 1152], P(None, ('clip', 'seq')), may hold values from -0.75 to 0.75
- t_qkv: bfloat16 [1, 1152, 3456], P(None, ('clip', 'seq')), may hold values from -0.09375 to 0.09375
- t_proj: bfloat16 [1, 1152, 1152], P(None, ('clip', 'seq')), may hold values from -0.75 to 0.75
- c_query: bfloat16 [1, 1152, 1152], P(None, ('clip', 'seq')), may hold values from -0.09375 to 0.09375
- c_kv: bfloat16 [1, 1152, 2304], P(None, ('clip', 'seq')), may hold values from -0.1875 to 0.1875
- c_proj: bfloat16 [1, 1152, 1152], P(None, ('clip', 'seq')), may hold values from -0.5 to 0.5
- mlp_in: bfloat16 [1, 1152, 4608], P(None, ('clip', 'seq')), may hold values from -0.1875 to 0.1875
- mlp_out: bfloat16 [1, 4608, 1152], P(None, ('clip', 'seq')), may hold values from -0.09375 to 0.09375
- vectors: bfloat16 [1, 20, 1152], P(None, None, ('clip', 'seq')), may hold values from -1.75 to 1.75
Outputs:
- output: float32 [4, 16, 256, 1152], P('clip', 'seq')
- token_grad: float32 [4, 16, 256, 1152], P('clip', 'seq')
- text_grad: float32 [4, 120, 1152], P('clip', None, 'seq')
- time_weight_grad: float32 [1152, 6912], P(('clip', 'seq'))
- s_qkv_grad: float32 [1, 1152, 3456], P(None, ('clip', 'seq'))
- s_proj_grad: float32 [1, 1152, 1152], P(None, ('clip', 'seq'))
- t_qkv_grad: float32 [1, 1152, 3456], P(None, ('clip', 'seq'))
- t_proj_grad: float32 [1, 1152, 1152], P(None, ('clip', 'seq'))
- c_query_grad: float32 [1, 1152, 1152], P(None, ('clip', 'seq'))
- c_kv_grad: float32 [1, 1152, 2304], P(None, ('clip', 'seq'))
- c_proj_grad: float32 [1, 1152, 1152], P(None, ('clip', 'seq'))
- mlp_in_grad: float32 [1, 1152, 4608], P(None, ('clip', 'seq'))
- mlp_out_grad: float32 [1, 4608, 1152], P(None, ('clip', 'seq'))
- vectors_grad: float32 [1, 20, 1152], P(None, None, ('clip', 'seq'))
Inputs may be any that keep to these rules, and one draw needn't show every extreme that they name: Each clip's caption is its first text_counts tokens; the rest are padding.
All inputs are finite; a program needn't handle non-finite values.
Results may differ from a plain program's by a relative error of at most 0.03.
Values may be sent and summed in bfloat16 or wider, within the bound.
A program may use at most 576 MiB of HBM per device.

v0:
```python
from functools import partial
import math

import jax
import jax.numpy as jnp
from jax import lax
from jax.sharding import PartitionSpec as P

HEADS = 16


EPSILON = 1e-06
HIGHEST = lax.Precision.HIGHEST
SPATIAL = ("bqhe", "bkhe", "bhqk")
TEMPORAL = ("cqphe", "ckphe", "cphqk")
CROSS = ("cqhe", "ckhe", "chqk")


def product(left_arr, right_arr):
    return lax.dot_general(
        left_arr,
        right_arr,
        (((left_arr.ndim - 1,), (0,)), ((), ())),
        preferred_element_type=jnp.float32,
    )


def product_back(grad_arr, weight):
    return lax.dot_general(
        grad_arr,
        weight,
        (((grad_arr.ndim - 1,), (1,)), ((), ())),
        preferred_element_type=jnp.float32,
    )


def outer_sum(left_arr, right_arr):
    left_rows = left_arr.reshape(-1, left_arr.shape[-1])
    right_rows = right_arr.reshape(-1, right_arr.shape[-1])
    return lax.dot_general(
        left_rows, right_rows, (((0,), (0,)), ((), ())), preferred_element_type=jnp.float32
    )


def column_sum(grad_arr):
    return jnp.sum(grad_arr.astype(jnp.float32).reshape(-1, grad_arr.shape[-1]), axis=0)


def timestep_embed(step_values, model_width):
    half_width = model_width // 2
    frequency = jnp.exp(-math.log(10000.0) * jnp.arange(half_width, dtype=jnp.float32) / half_width)
    angles = step_values.astype(jnp.float32)[:, None] * frequency[None, :]
    return jnp.concatenate([jnp.cos(angles), jnp.sin(angles)], axis=-1)


def modulate(hidden, shift_row, scale_row):
    centered = hidden - jnp.mean(hidden, axis=-1, keepdims=True)
    normed = centered * lax.rsqrt(jnp.mean(centered * centered, axis=-1, keepdims=True) + EPSILON)
    return normed * (1.0 + scale_row[:, None, :]) + shift_row[:, None, :]


def split_heads(packed_arr, heads):
    return packed_arr.reshape(packed_arr.shape[:-1] + (heads, packed_arr.shape[-1] // heads))


def merge_heads(head_arr):
    return head_arr.reshape(head_arr.shape[:-2] + (head_arr.shape[-2] * head_arr.shape[-1],))


def attend_scores(queries, key_rows, key_mask, forms):
    query_form, key_form, score_form = forms
    scale_factor = queries.shape[-1] ** (-0.5)
    scores = (
        jnp.einsum(
            query_form + "," + key_form + "->" + score_form,
            queries,
            key_rows,
            preferred_element_type=jnp.float32,
        )
        * scale_factor
    )
    if key_mask is not None:
        scores = jnp.where(key_mask, scores, -1000000000.0)
    return scores


def attend_forward(queries, key_rows, values, key_mask, forms):
    query_form, key_form, score_form = forms
    scores = attend_scores(queries, key_rows, key_mask, forms)
    top_score = jnp.max(scores, axis=-1, keepdims=True)
    log_total = top_score + jnp.log(jnp.sum(jnp.exp(scores - top_score), axis=-1, keepdims=True))
    attn_probs = jnp.exp(scores - log_total).astype(jnp.bfloat16)
    mixed_heads = jnp.einsum(
        score_form + "," + key_form + "->" + query_form,
        attn_probs,
        values,
        preferred_element_type=jnp.float32,
    )
    return (mixed_heads.astype(jnp.bfloat16), log_total)


def attend_backward(queries, key_rows, values, key_mask, log_total, grad_mixed, forms):
    query_form, key_form, score_form = forms
    scale_factor = queries.shape[-1] ** (-0.5)
    scores = attend_scores(queries, key_rows, key_mask, forms)
    attn_probs = jnp.exp(scores - log_total)
    grad_probs = jnp.einsum(
        query_form + "," + key_form + "->" + score_form,
        grad_mixed,
        values,
        preferred_element_type=jnp.float32,
    )
    inner_dot = jnp.sum(attn_probs * grad_probs, axis=-1, keepdims=True)
    grad_scores = (attn_probs * (grad_probs - inner_dot)).astype(jnp.bfloat16)
    grad_values = jnp.einsum(
        score_form + "," + query_form + "->" + key_form,
        attn_probs.astype(jnp.bfloat16),
        grad_mixed,
        preferred_element_type=jnp.float32,
    )
    grad_queries = (
        jnp.einsum(
            score_form + "," + key_form + "->" + query_form,
            grad_scores,
            key_rows,
            preferred_element_type=jnp.float32,
        )
        * scale_factor
    )
    grad_keys = (
        jnp.einsum(
            score_form + "," + query_form + "->" + key_form,
            grad_scores,
            queries,
            preferred_element_type=jnp.float32,
        )
        * scale_factor
    )
    return (grad_queries, grad_keys, grad_values)


def project_qkv(inputs, weight, query_bias, value_bias, heads):
    model_width = query_bias.shape[0]
    bias_row = jnp.concatenate([query_bias, jnp.zeros_like(query_bias), value_bias]).astype(
        jnp.float32
    )
    packed = (product(inputs, weight) + bias_row).astype(jnp.bfloat16)
    return (
        split_heads(packed[..., :model_width], heads),
        split_heads(packed[..., model_width : 2 * model_width], heads),
        split_heads(packed[..., 2 * model_width :], heads),
    )


def qkv_backward(grad_parts, inputs, weight):
    model_width = weight.shape[0]
    packed_grad = jnp.concatenate(
        [merge_heads(grad_part) for grad_part in grad_parts], axis=-1
    ).astype(jnp.bfloat16)
    return (
        outer_sum(inputs, packed_grad),
        product_back(packed_grad, weight),
        column_sum(packed_grad[..., :model_width]),
        column_sum(packed_grad[..., 2 * model_width :]),
    )


def layer_forward(hidden, layer_mats, modulation, text, text_mask, heads, frame_count):
    w_sqkv, w_sproj, w_tqkv, w_tproj, w_cquery, w_ckv, w_cproj, w_in, w_out, vec_rows = layer_mats
    clip_count, row_count, model_width = hidden.shape
    patch_count = row_count // frame_count
    vec_float = vec_rows.astype(jnp.float32)
    mod_table = modulation + vec_float[10:16][None]
    gate_one = mod_table[:, None, 2]
    normed = (
        modulate(hidden, mod_table[:, 0], mod_table[:, 1])
        .astype(jnp.bfloat16)
        .reshape(clip_count * frame_count, patch_count, model_width)
    )
    s_query, s_key, s_value = project_qkv(normed, w_sqkv, vec_rows[0], vec_rows[1], heads)
    s_mixed, s_total = attend_forward(s_query, s_key, s_value, None, SPATIAL)
    s_flat = merge_heads(s_mixed)
    s_branch = (product(s_flat, w_sproj) + vec_float[2]).reshape(clip_count, row_count, model_width)
    hidden_one = hidden + gate_one * s_branch
    frames_view = hidden_one.astype(jnp.bfloat16).reshape(
        clip_count, frame_count, patch_count, model_width
    )
    moved = lax.all_to_all(frames_view, "seq", split_axis=2, concat_axis=1, tiled=True)
    t_query, t_key, t_value = project_qkv(moved, w_tqkv, vec_rows[3], vec_rows[4], heads)
    t_mixed, t_total = attend_forward(t_query, t_key, t_value, None, TEMPORAL)
    t_flat = merge_heads(t_mixed)
    t_branch = (product(t_flat, w_tproj) + vec_float[5]).astype(jnp.bfloat16)
    t_back = lax.all_to_all(t_branch, "seq", split_axis=1, concat_axis=2, tiled=True).reshape(
        clip_count, row_count, model_width
    )
    hidden_two = hidden_one + gate_one * t_back.astype(jnp.float32)
    cross_in = hidden_two.astype(jnp.bfloat16)
    c_query = split_heads((product(cross_in, w_cquery) + vec_float[6]).astype(jnp.bfloat16), heads)
    kv_bias = jnp.concatenate([jnp.zeros_like(vec_float[7]), vec_float[7]])
    c_packed = (product(text, w_ckv) + kv_bias).astype(jnp.bfloat16)
    c_key = split_heads(c_packed[..., :model_width], heads)
    c_value = split_heads(c_packed[..., model_width:], heads)
    c_mixed, c_total = attend_forward(c_query, c_key, c_value, text_mask, CROSS)
    c_flat = merge_heads(c_mixed)
    hidden_three = hidden_two + (product(c_flat, w_cproj) + vec_float[8])
    normed_two = modulate(hidden_three, mod_table[:, 3], mod_table[:, 4]).astype(jnp.bfloat16)
    inner_act = product(normed_two, w_in) + vec_float[16:].reshape(-1)
    gelu_out = jax.nn.gelu(inner_act, approximate=True).astype(jnp.bfloat16)
    mlp_branch = product(gelu_out, w_out) + vec_float[9]
    hidden_four = hidden_three + mod_table[:, None, 5] * mlp_branch
    saved = dict(
        mod_table=mod_table,
        hidden=hidden,
        normed=normed,
        s_query=s_query,
        s_key=s_key,
        s_value=s_value,
        s_total=s_total,
        s_flat=s_flat,
        s_branch=s_branch,
        moved=moved,
        t_query=t_query,
        t_key=t_key,
        t_value=t_value,
        t_total=t_total,
        t_flat=t_flat,
        t_back=t_back,
        cross_in=cross_in,
        c_query=c_query,
        c_key=c_key,
        c_value=c_value,
        c_total=c_total,
        c_flat=c_flat,
        hidden_three=hidden_three,
        normed_two=normed_two,
        inner_act=inner_act,
        gelu_out=gelu_out,
        mlp_branch=mlp_branch,
    )
    return (hidden_four, saved)


def layer_backward(grad_hidden, saved, layer_mats, text, text_mask, heads, frame_count):
    w_sqkv, w_sproj, w_tqkv, w_tproj, w_cquery, w_ckv, w_cproj, w_in, w_out, vec_rows = layer_mats
    clip_count, row_count, model_width = grad_hidden.shape
    patch_count = row_count // frame_count
    mod_table = saved["mod_table"]
    gate_one = mod_table[:, None, 2]
    gate_two = mod_table[:, None, 5]
    grad_mlp = (grad_hidden * gate_two).astype(jnp.bfloat16)
    grad_gate_two = jnp.sum(grad_hidden * saved["mlp_branch"], axis=1)
    grad_w_out = outer_sum(saved["gelu_out"], grad_mlp)
    bias_out = column_sum(grad_mlp)
    grad_gelu = product_back(grad_mlp, w_out)
    gelu_pull = jax.vjp(partial(jax.nn.gelu, approximate=True), saved["inner_act"])[1]
    grad_inner = gelu_pull(grad_gelu)[0].astype(jnp.bfloat16)
    grad_w_in = outer_sum(saved["normed_two"], grad_inner)
    bias_in = column_sum(grad_inner)
    grad_normed_two = product_back(grad_inner, w_in)
    norm_pull = jax.vjp(modulate, saved["hidden_three"], mod_table[:, 3], mod_table[:, 4])[1]
    grad_three, grad_shift_two, grad_scale_two = norm_pull(grad_normed_two)
    grad_three = grad_hidden + grad_three
    grad_cross = grad_three.astype(jnp.bfloat16)
    grad_w_cproj = outer_sum(saved["c_flat"], grad_cross)
    bias_cproj = column_sum(grad_cross)
    grad_cmixed = split_heads(product_back(grad_cross, w_cproj).astype(jnp.bfloat16), heads)
    cq_grad, ck_grad, cv_grad = attend_backward(
        saved["c_query"],
        saved["c_key"],
        saved["c_value"],
        text_mask,
        saved["c_total"],
        grad_cmixed,
        CROSS,
    )
    grad_cquery = merge_heads(cq_grad).astype(jnp.bfloat16)
    grad_w_cquery = outer_sum(saved["cross_in"], grad_cquery)
    bias_cquery = column_sum(grad_cquery)
    grad_two = grad_three + product_back(grad_cquery, w_cquery)
    grad_kv = jnp.concatenate([merge_heads(ck_grad), merge_heads(cv_grad)], axis=-1).astype(
        jnp.bfloat16
    )
    grad_w_ckv = outer_sum(text, grad_kv)
    bias_cvalue = column_sum(grad_kv[..., model_width:])
    text_part = product_back(grad_kv, w_ckv)
    grad_gate_one = jnp.sum(grad_two * saved["t_back"].astype(jnp.float32), axis=1)
    grad_temporal = (
        (grad_two * gate_one)
        .astype(jnp.bfloat16)
        .reshape(clip_count, frame_count, patch_count, model_width)
    )
    grad_places = lax.all_to_all(grad_temporal, "seq", split_axis=2, concat_axis=1, tiled=True)
    grad_w_tproj = outer_sum(saved["t_flat"], grad_places)
    bias_tproj = column_sum(grad_places)
    grad_tmixed = split_heads(product_back(grad_places, w_tproj).astype(jnp.bfloat16), heads)
    temporal_grads = attend_backward(
        saved["t_query"],
        saved["t_key"],
        saved["t_value"],
        None,
        saved["t_total"],
        grad_tmixed,
        TEMPORAL,
    )
    grad_w_tqkv, grad_moved, bias_tquery, bias_tvalue = qkv_backward(
        temporal_grads, saved["moved"], w_tqkv
    )
    grad_frames = lax.all_to_all(
        grad_moved.astype(jnp.bfloat16), "seq", split_axis=1, concat_axis=2, tiled=True
    )
    grad_one = grad_two + grad_frames.astype(jnp.float32).reshape(
        clip_count, row_count, model_width
    )
    grad_gate_one = grad_gate_one + jnp.sum(grad_one * saved["s_branch"], axis=1)
    grad_spatial = (
        (grad_one * gate_one)
        .astype(jnp.bfloat16)
        .reshape(clip_count * frame_count, patch_count, model_width)
    )
    grad_w_sproj = outer_sum(saved["s_flat"], grad_spatial)
    bias_sproj = column_sum(grad_spatial)
    grad_smixed = split_heads(product_back(grad_spatial, w_sproj).astype(jnp.bfloat16), heads)
    spatial_grads = attend_backward(
        saved["s_query"],
        saved["s_key"],
        saved["s_value"],
        None,
        saved["s_total"],
        grad_smixed,
        SPATIAL,
    )
    grad_w_sqkv, grad_normed, bias_squery, bias_svalue = qkv_backward(
        spatial_grads, saved["normed"], w_sqkv
    )
    first_pull = jax.vjp(modulate, saved["hidden"], mod_table[:, 0], mod_table[:, 1])[1]
    grad_zero, grad_shift_one, grad_scale_one = first_pull(
        grad_normed.reshape(clip_count, row_count, model_width)
    )
    grad_input = grad_one + grad_zero
    grad_table = jnp.stack(
        [
            grad_shift_one,
            grad_scale_one,
            grad_gate_one,
            grad_shift_two,
            grad_scale_two,
            grad_gate_two,
        ],
        axis=1,
    )
    bias_rows = jnp.stack(
        [
            bias_squery,
            bias_svalue,
            bias_sproj,
            bias_tquery,
            bias_tvalue,
            bias_tproj,
            bias_cquery,
            bias_cvalue,
            bias_cproj,
            bias_out,
        ]
    )
    vec_grad = jnp.concatenate(
        [bias_rows, jnp.sum(grad_table, axis=0), bias_in.reshape(-1, model_width)], axis=0
    )
    layer_grads = (
        grad_w_sqkv,
        grad_w_sproj,
        grad_w_tqkv,
        grad_w_tproj,
        grad_w_cquery,
        grad_w_ckv,
        grad_w_cproj,
        grad_w_in,
        grad_w_out,
        vec_grad,
    )
    return (grad_input, layer_grads, text_part, grad_table)


def per_device(
    tokens,
    text,
    timesteps,
    text_counts,
    out_grad,
    time_weight,
    s_qkv,
    s_proj,
    t_qkv,
    t_proj,
    c_query,
    c_kv,
    c_proj,
    mlp_in,
    mlp_out,
    vectors,
):
    clip_count, frame_count, patch_count, model_width = tokens.shape
    layer_count = s_qkv.shape[0]
    heads = HEADS
    clip_first = lax.axis_index("clip") * clip_count
    my_steps = lax.dynamic_slice_in_dim(timesteps, clip_first, clip_count)
    time_embed = jax.nn.silu(timestep_embed(my_steps, model_width)).astype(jnp.bfloat16)
    time_full = lax.all_gather(time_weight, ("clip", "seq"), axis=0, tiled=True)
    modulation = product(time_embed, time_full).reshape(clip_count, 6, model_width)
    text_mask = (jnp.arange(text.shape[1])[None, :] < text_counts[:, None])[:, None, None, :]
    hidden = tokens.astype(jnp.float32).reshape(clip_count, frame_count * patch_count, model_width)
    layer_mats = None
    layer_idx = 0
    layer_mats = (
        lax.all_gather(s_qkv[layer_idx], ("clip", "seq"), axis=0, tiled=True),
        lax.all_gather(s_proj[layer_idx], ("clip", "seq"), axis=0, tiled=True),
        lax.all_gather(t_qkv[layer_idx], ("clip", "seq"), axis=0, tiled=True),
        lax.all_gather(t_proj[layer_idx], ("clip", "seq"), axis=0, tiled=True),
        lax.all_gather(c_query[layer_idx], ("clip", "seq"), axis=0, tiled=True),
        lax.all_gather(c_kv[layer_idx], ("clip", "seq"), axis=0, tiled=True),
        lax.all_gather(c_proj[layer_idx], ("clip", "seq"), axis=0, tiled=True),
        lax.all_gather(mlp_in[layer_idx], ("clip", "seq"), axis=0, tiled=True),
        lax.all_gather(mlp_out[layer_idx], ("clip", "seq"), axis=0, tiled=True),
        lax.all_gather(vectors[layer_idx], ("clip", "seq"), axis=1, tiled=True),
    )
    hidden, saved = layer_forward(
        hidden, layer_mats, modulation, text, text_mask, heads, frame_count
    )
    saved_list = [saved]
    output = hidden.reshape(tokens.shape)
    grad_hidden = out_grad.astype(jnp.float32).reshape(hidden.shape)
    grad_text = jnp.zeros(text.shape, jnp.float32)
    grad_mod = jnp.zeros(modulation.shape, jnp.float32)
    grad_shards = [None] * layer_count
    for layer_idx in reversed(range(layer_count)):
        back_mats = (
            lax.all_gather(s_qkv[layer_idx], ("clip", "seq"), axis=0, tiled=True),
            lax.all_gather(s_proj[layer_idx], ("clip", "seq"), axis=0, tiled=True),
            lax.all_gather(t_qkv[layer_idx], ("clip", "seq"), axis=0, tiled=True),
            lax.all_gather(t_proj[layer_idx], ("clip", "seq"), axis=0, tiled=True),
            lax.all_gather(c_query[layer_idx], ("clip", "seq"), axis=0, tiled=True),
            lax.all_gather(c_kv[layer_idx], ("clip", "seq"), axis=0, tiled=True),
            lax.all_gather(c_proj[layer_idx], ("clip", "seq"), axis=0, tiled=True),
            lax.all_gather(mlp_in[layer_idx], ("clip", "seq"), axis=0, tiled=True),
            lax.all_gather(mlp_out[layer_idx], ("clip", "seq"), axis=0, tiled=True),
            lax.all_gather(vectors[layer_idx], ("clip", "seq"), axis=1, tiled=True),
        )
        grad_hidden, layer_grads, text_part, table_part = layer_backward(
            grad_hidden, saved_list[layer_idx], back_mats, text, text_mask, heads, frame_count
        )
        grad_text = grad_text + text_part
        grad_mod = grad_mod + table_part
        grad_shards[layer_idx] = (
            lax.psum_scatter(layer_grads[0], ("clip", "seq"), scatter_dimension=0, tiled=True),
            lax.psum_scatter(layer_grads[1], ("clip", "seq"), scatter_dimension=0, tiled=True),
            lax.psum_scatter(layer_grads[2], ("clip", "seq"), scatter_dimension=0, tiled=True),
            lax.psum_scatter(layer_grads[3], ("clip", "seq"), scatter_dimension=0, tiled=True),
            lax.psum_scatter(layer_grads[4], ("clip", "seq"), scatter_dimension=0, tiled=True),
            lax.psum_scatter(layer_grads[5], ("clip", "seq"), scatter_dimension=0, tiled=True),
            lax.psum_scatter(layer_grads[6], ("clip", "seq"), scatter_dimension=0, tiled=True),
            lax.psum_scatter(layer_grads[7], ("clip", "seq"), scatter_dimension=0, tiled=True),
            lax.psum_scatter(layer_grads[8], ("clip", "seq"), scatter_dimension=0, tiled=True),
            lax.psum_scatter(layer_grads[9], ("clip", "seq"), scatter_dimension=1, tiled=True),
        )
    grad_flat = grad_mod.reshape(clip_count, 6 * model_width)
    embed_float = time_embed.astype(jnp.float32)
    time_grad = lax.psum_scatter(
        lax.dot_general(
            embed_float,
            grad_flat,
            (((0,), (0,)), ((), ())),
            precision=HIGHEST,
            preferred_element_type=jnp.float32,
        ),
        ("clip", "seq"),
        scatter_dimension=0,
        tiled=True,
    )
    text_grad = lax.psum_scatter(
        grad_text.astype(jnp.bfloat16), "seq", scatter_dimension=2, tiled=True
    ).astype(jnp.float32)
    stacked = [jnp.stack([grad_shards[0][member]]) for member in range(10)]
    return (
        output,
        grad_hidden.reshape(tokens.shape),
        text_grad,
        time_grad,
        stacked[0],
        stacked[1],
        stacked[2],
        stacked[3],
        stacked[4],
        stacked[5],
        stacked[6],
        stacked[7],
        stacked[8],
        stacked[9],
    )


def solution(mesh):
    placed = (
        P("clip", "seq", None, None),
        P("clip", None, None),
        P(),
        P("clip"),
        P("clip", "seq", None, None),
        P(("clip", "seq"), None),
        P(None, ("clip", "seq"), None),
        P(None, ("clip", "seq"), None),
        P(None, ("clip", "seq"), None),
        P(None, ("clip", "seq"), None),
        P(None, ("clip", "seq"), None),
        P(None, ("clip", "seq"), None),
        P(None, ("clip", "seq"), None),
        P(None, ("clip", "seq"), None),
        P(None, ("clip", "seq"), None),
        P(None, None, ("clip", "seq")),
    )
    return jax.shard_map(
        per_device,
        mesh=mesh,
        in_specs=placed,
        out_specs=(
            P("clip", "seq", None, None),
            P("clip", "seq", None, None),
            P("clip", None, "seq"),
            P(("clip", "seq"), None),
            P(None, ("clip", "seq"), None),
            P(None, ("clip", "seq"), None),
            P(None, ("clip", "seq"), None),
            P(None, ("clip", "seq"), None),
            P(None, ("clip", "seq"), None),
            P(None, ("clip", "seq"), None),
            P(None, ("clip", "seq"), None),
            P(None, ("clip", "seq"), None),
            P(None, ("clip", "seq"), None),
            P(None, None, ("clip", "seq")),
        ),
        check_vma=False,
    )
```

profile of v0, /device:TPU:0, one launch (start us, length us, event | category | flops | bytes accessed | tf_op | source)
XLA Modules:
  0.0 3277.0 jit_solution(857093578488210427)
XLA Ops:
  19.1 46.9 %all-gather = bf16[1,20,1152]{1,0,2:T(2,128)(2,1)S(1)} all-gather(bf16[1,20,36]{1,0,2:T(2,128)(2,1)S(1)} %copy.195), channel_id=2, replica_groups=mesh['clip'=4,'seq'=8] {'clip','seq'}, dimensions={2}, use_global_device_ids=true | all-gather | bytes 47520 | tf_op jit(solution)/shard_map/all_gather | solution.py:423
  70.0 24.3 slice_reduce_fusion.8
  95.1 21.4 slice_reduce_fusion
  116.5 18.7 all-gather.40.cloned.1.call-done
  135.2 18.4 reshape.1363
  153.7 21.9 copy.194
  188.0 60.0 %all-gather.22.cloned.1.call-done = bf16[1,1152,3456]{2,0,1:T(2,128)(2,1)} async-done(((bf16[1,36,3456]{2,0,1:T(2,128)(2,1)}), bf16[1,1152,3456]{2,0,1:T(2,128)(2,1)}) %all-gather.22.cloned.1.call-update) | async-done | bytes 7962640 | tf_op jit(solution)/shard_map/all_gather | solution.py:414
  247.9 11.0 add_convert_fusion.1
  277.0 38.1 %all-gather.24.cloned.1.call-done = bf16[1,1152,1152]{2,0,1:T(2,128)(2,1)} async-done(((bf16[1,36,1152]{2,0,1:T(2,128)(2,1)}), bf16[1,1152,1152]{2,0,1:T(2,128)(2,1)}) %all-gather.24.cloned.1.call-update) | async-done | bytes 2654224 | tf_op jit(solution)/shard_map/all_gather | solution.py:415
  333.6 76.0 %all-gather.30.cloned.1.call-done = bf16[1,1152,2304]{2,0,1:T(2,128)(2,1)} async-done(((bf16[1,36,2304]{2,0,1:T(2,128)(2,1)}), bf16[1,1152,2304]{2,0,1:T(2,128)(2,1)}) %all-gather.30.cloned.1.call-update) | async-done | bytes 5308432 | tf_op jit(solution)/shard_map/all_gather | solution.py:419
  415.7 106.8 %all-gather.26.cloned.1.call-done = bf16[1,1152,3456]{2,0,1:T(2,128)(2,1)} async-done(((bf16[1,36,3456]{2,0,1:T(2,128)(2,1)}), bf16[1,1152,3456]{2,0,1:T(2,128)(2,1)}) %all-gather.26.cloned.1.call-update) | async-done | bytes 7962640 | tf_op jit(solution)/shard_map/all_gather | solution.py:416
  565.2 24.4 all-gather.28.cloned.1.call-done
  622.9 37.4 %all-gather.32.cloned.1.call-done = bf16[1,1152,1152]{2,0,1:T(2,128)(2,1)} async-done(((bf16[1,36,1152]{2,0,1:T(2,128)(2,1)}), bf16[1,1152,1152]{2,0,1:T(2,128)(2,1)}) %all-gather.32.cloned.1.call-update) | async-done | bytes 2654224 | tf_op jit(solution)/shard_map/all_gather | solution.py:418
  672.1 56.1 %all-gather.34.cloned.1.call-done = bf16[1,1152,1152]{2,0,1:T(2,128)(2,1)} async-done(((bf16[1,36,1152]{2,0,1:T(2,128)(2,1)}), bf16[1,1152,1152]{2,0,1:T(2,128)(2,1)}) %all-gather.34.cloned.1.call-update) | async-done | bytes 2654224 | tf_op jit(solution)/shard_map/all_gather | solution.py:420
  735.4 131.0 %all-gather.36.cloned.1.call-done = bf16[1,1152,4608]{2,0,1:T(2,128)(2,1)} async-done(((bf16[1,36,4608]{2,0,1:T(2,128)(2,1)}), bf16[1,1152,4608]{2,0,1:T(2,128)(2,1)}) %all-gather.36.cloned.1.call-update) | async-done | bytes 10616848 | tf_op jit(solution)/shard_map/all_gather | solution.py:421
  866.5 14.6 fusion.10
  881.0 73.5 %all-gather.38.cloned.1.call-done = bf16[1,4608,1152]{2,1,0:T(8,128)(2,1)} async-done(((bf16[1,144,1152]{2,1,0:T(8,128)(2,1)}), bf16[1,4608,1152]{2,1,0:T(8,128)(2,1)}) %all-gather.38.cloned.1.call-update) | async-done | bytes 10616848 | tf_op jit(solution)/shard_map/all_gather | solution.py:422
  954.5 17.4 convert_reduce_fusion
  972.0 16.8 multiply_reduce_fusion.5
  988.8 16.3 fusion.125
  1098.4 12.5 fusion.95
  1162.2 14.8 fusion.116
  1190.5 12.8 fusion.213
  1203.3 373.9 %fusion.217 = (f32[48,1152]{1,0:T(8,128)S(1)}, f32[40,4608]{1,0:T(8,128)S(1)}) fusion(f32[1152,1152]{1,0:T(8,128)} %fusion.203, f32[1152,4608]{1,0:T(8,128)} %fusion.213), kind=kCustom, calls=%all-reduce-scatter.10 | all-reduce-scatter fusion | flops 7667714 | bytes 27500544
  1601.9 14.7 fusion.214
  1645.7 13.7 broadcast_multiply_fusion
  1663.5 557.1 %fusion.215 = (f32[40,6912]{1,0:T(8,128)}, f32[48,1152]{1,0:T(8,128)}, f32[48,1152]{1,0:T(8,128)}) fusion(f32[1152,6912]{1,0:T(8,128)} %broadcast_multiply_fusion, f32[1152,1152]{1,0:T(8,128)} %fusion.227, f32[1152,1152]{1,0:T(8,128)} %fusion.228), kind=kCustom, calls=%all-reduce-scatter.8 | all-reduce-scatter fusion | flops 12386306 | bytes 44015616
  2225.1 34.9 %collective-permute-start.47 = (f32[48,1152]{1,0:T(8,128)S(1)}, f32[48,1152]{1,0:T(8,128)S(1)}, u32[]{:S(2)}, u32[]{:S(2)}) collective-permute-start(f32[48,1152]{1,0:T(8,128)S(1)} %get-tuple-element.109), channel_id=1, source_target_pairs={{0,4},{1,5},{2,6},{3,7},{4,8},{5,9},{6,10},{7,11},{8,12},{9,13},{1... | collective-permute-start | bytes 663560
  2267.1 10.9 fusion.63
  2282.6 13.3 collective-permute-done.47
  2323.0 491.3 %fusion.216 = (f32[48,3456]{1,0:T(8,128)S(1)}, f32[48,3456]{1,0:T(8,128)S(1)}, f32[48,1152]{1,0:T(8,128)S(1)}) fusion(f32[1152,3456]{1,0:T(8,128)} %fusion.63, f32[1152,3456]{1,0:T(8,128)} %fusion.69, f32[1152,1152]{1,0:T(8,128)} %fusion.229), kind=kCustom, calls=%all-reduce-scatter.9 | all-reduce-scatter fusion | flops 12386305 | bytes 38707200
  2814.3 23.0 collective-permute-start.43
  2837.3 19.1 collective-permute-start.16
  2856.4 11.0 collective-permute-start.15
  2941.4 14.4 collective-permute-done.37
  2958.2 33.3 %collective-permute-start.8 = (f32[48,3456]{1,0:T(8,128)S(1)}, f32[48,3456]{1,0:T(8,128)}, u32[]{:S(2)}, u32[]{:S(2)}) collective-permute-start(f32[48,3456]{1,0:T(8,128)S(1)} %get-tuple-element.104), channel_id=1, source_target_pairs={{0,5},{1,6},{2,7},{3,8},{4,9},{5,10},{6,11},{7,12},{8,13},{9,14},{... | collective-permute-start | bytes 1990664
  2991.4 12.7 collective-permute-start.7
  3004.1 13.2 collective-permute-start.6
  3023.1 15.1 concatenate.145
  3046.5 12.5 collective-permute-start.25
  3060.7 17.1 concatenate.146
  3082.2 12.5 collective-permute-start.22
  3097.6 14.7 concatenate.141
  3119.6 15.0 concatenate.143
  3136.4 15.0 concatenate.144
  3161.3 36.2 %concatenate.140 = f32[420,3456]{1,0:T(8,128)} concatenate(f32[36,3456]{1,0:T(8,128)} %copy-done.77, f32[48,3456]{1,0:T(8,128)S(1)} %copy-done.74, f32[48,3456]{1,0:T(8,128)} %copy-done.75, f32[48,3456]{1,0:T(8,128)} %collective-permute-done.8, f32[48,3456]{1,0:T(8,128)} %collective-permute-done.7, f32[48,3456]{1,0:T(8,128)} %collective-permute-done.6, ...), dimensions={0} | concatenate | bytes 11612160
  3199.0 36.8 %concatenate.142 = f32[420,3456]{1,0:T(8,128)} concatenate(f32[36,3456]{1,0:T(8,128)} %copy-done.76, f32[48,3456]{1,0:T(8,128)} %collective-permute-done.26, f32[48,3456]{1,0:T(8,128)} %collective-permute-done.25, f32[48,3456]{1,0:T(8,128)} %collective-permute-done.24, f32[48,3456]{1,0:T(8,128)} %collective-permute-done.23, f32[48,3456]{1,0:T(8,128)} %collective-permute-done.22, ...), dimensions={0} | concatenate | bytes 11612160
  3240.7 22.2 concatenate.139
  (669 shorter events, 553.9 us)
Async XLA Ops:
  7.2 128.0 %all-gather.40.cloned.1.call-start = ((), (), s32[]{:S(2)}) async-start(), calls=%async_computation.16 | async-start | bytes 18247680 | tf_op jit(solution)/shard_map/all_gather | solution.py:407
  8.0 240.0 %all-gather.22.cloned.1.call-start = ((), (), s32[]{:S(2)}) async-start(), calls=%async_computation.7 | async-start | bytes 16422912 | tf_op jit(solution)/shard_map/all_gather | solution.py:414
  10.2 305.0 %all-gather.24.cloned.1.call-start = ((), (), s32[]{:S(2)}) async-start(), calls=%async_computation.8 | async-start | bytes 5474304 | tf_op jit(solution)/shard_map/all_gather | solution.py:415
  12.0 397.7 %all-gather.30.cloned.1.call-start = ((), (), s32[]{:S(2)}) async-start(), calls=%async_computation.11 | async-start | bytes 10948608 | tf_op jit(solution)/shard_map/all_gather | solution.py:419
  13.0 509.4 %all-gather.26.cloned.1.call-start = ((), (), s32[]{:S(2)}) async-start(), calls=%async_computation.9 | async-start | bytes 16422912 | tf_op jit(solution)/shard_map/all_gather | solution.py:416
  14.3 575.3 %all-gather.28.cloned.1.call-start = ((), (), s32[]{:S(2)}) async-start(), calls=%async_computation.10 | async-start | bytes 5474304 | tf_op jit(solution)/shard_map/all_gather | solution.py:417
  15.2 645.1 %all-gather.32.cloned.1.call-start = ((), (), s32[]{:S(2)}) async-start(), calls=%async_computation.12 | async-start | bytes 5474304 | tf_op jit(solution)/shard_map/all_gather | solution.py:418
  16.0 712.2 %all-gather.34.cloned.1.call-start = ((), (), s32[]{:S(2)}) async-start(), calls=%async_computation.13 | async-start | bytes 5474304 | tf_op jit(solution)/shard_map/all_gather | solution.py:420
  16.9 849.5 %all-gather.36.cloned.1.call-start = ((), (), s32[]{:S(2)}) async-start(), calls=%async_computation.14 | async-start | bytes 21897216 | tf_op jit(solution)/shard_map/all_gather | solution.py:421
  18.4 936.1 %all-gather.38.cloned.1.call-start = ((), (), s32[]{:S(2)}) async-start(), calls=%async_computation.15 | async-start | bytes 10948608 | tf_op jit(solution)/shard_map/all_gather | solution.py:422
  323.7 91.7 %all-to-all-start = ((bf16[1,2,256,1152]{3,1,0,2:T(2,128)(2,1)}), bf16[1,2,256,1152]{3,1,0,2:T(2,128)(2,1)S(1)}, u32[]{:S(2)}, u32[]{:S(2)}) async-start(bf16[1,2,256,1152]{3,1,0,2:T(2,128)(2,1)} %copy.203), calls=%async_computation | async-start | bytes 2359296 | tf_op jit(solution)/shard_map/all_to_all | solution.py:188
  1031.2 2027.8 %reduce-scatter.25.cloned.1.call-start = ((), (), s32[]{:S(2)}) async-start(), calls=%async_computation.17 | async-start | bytes 331776
  1115.3 2150.1 %all-reduce.25.cloned.1.call-start = ((), (), s32[]{:S(2)}) async-start(), calls=%async_computation.18 | async-start | bytes 21454848
  1189.8 2080.2 %reduce-scatter.23.cloned.1.call-start = ((), (), s32[]{:S(2)}) async-start(), calls=%async_computation.6 | async-start | bytes 21897216 | tf_op jit(solution)/shard_map/reduce_scatter | solution.py:461
  1577.9 683.4 %collective-permute-start.50 = (f32[48,1152]{1,0:T(8,128)S(1)}, f32[48,1152]{1,0:T(8,128)}, u32[]{:S(2)}, u32[]{:S(2)}) collective-permute-start(f32[48,1152]{1,0:T(8,128)S(1)} %get-tuple-element.109), channel_id=1, source_target_pairs={{0,7},{1,8},{2,9},{3,10},{4,11},{5,12},{6,13},{7,14},{8,15},{9,16}... | collective-permute-start | bytes 663560
  1584.7 694.7 %collective-permute-start.49 = (f32[48,1152]{1,0:T(8,128)S(1)}, f32[48,1152]{1,0:T(8,128)}, u32[]{:S(2)}, u32[]{:S(2)}) collective-permute-start(f32[48,1152]{1,0:T(8,128)S(1)} %get-tuple-element.109), channel_id=1, source_target_pairs={{0,6},{1,7},{2,8},{3,9},{4,10},{5,11},{6,12},{7,13},{8,14},{9,15},... | collective-permute-start | bytes 663560
  1592.3 688.4 %collective-permute-start.48 = (f32[48,1152]{1,0:T(8,128)S(1)}, f32[48,1152]{1,0:T(8,128)}, u32[]{:S(2)}, u32[]{:S(2)}) collective-permute-start(f32[48,1152]{1,0:T(8,128)S(1)} %get-tuple-element.109), channel_id=1, source_target_pairs={{0,5},{1,6},{2,7},{3,8},{4,9},{5,10},{6,11},{7,12},{8,13},{9,14},{... | collective-permute-start | bytes 663560
  1594.3 665.6 %collective-permute-start.51 = (f32[36,1152]{1,0:T(8,128)}, f32[36,1152]{1,0:T(8,128)}, u32[]{:S(2)}, u32[]{:S(2)}) collective-permute-start(f32[36,1152]{1,0:T(8,128)} %slice.157), channel_id=1, source_target_pairs={{0,8},{1,9},{2,10},{3,11},{4,12},{5,13},{6,14},{7,15},{8,16},{9,17... | collective-permute-start | bytes 497672
  1596.8 628.2 %collective-permute-start.55 = (f32[4,4608]{1,0:T(4,128)S(1)}, f32[4,4608]{1,0:T(4,128)S(1)}, u32[]{:S(2)}, u32[]{:S(2)}) collective-permute-start(f32[4,4608]{1,0:T(4,128)S(1)} %slice.158), channel_id=1, source_target_pairs={{0,4},{1,5},{2,6},{3,7},{4,8},{5,9},{6,10},{7,11},{8,12},{9,13},{1... | collective-permute-start | bytes 221192
  2225.1 70.8 %collective-permute-start.47 = (f32[48,1152]{1,0:T(8,128)S(1)}, f32[48,1152]{1,0:T(8,128)S(1)}, u32[]{:S(2)}, u32[]{:S(2)}) collective-permute-start(f32[48,1152]{1,0:T(8,128)S(1)} %get-tuple-element.109), channel_id=1, source_target_pairs={{0,4},{1,5},{2,6},{3,7},{4,8},{5,9},{6,10},{7,11},{8,12},{9,13},{1... | collective-permute-start | bytes 663560
  2260.0 55.5 %collective-permute-start.54 = (f32[40,4608]{1,0:T(8,128)S(1)}, f32[40,4608]{1,0:T(8,128)S(1)}, u32[]{:S(2)}, u32[]{:S(2)}) collective-permute-start(f32[40,4608]{1,0:T(8,128)S(1)} %get-tuple-element.110), channel_id=1, source_target_pairs={{0,3},{1,4},{2,5},{3,6},{4,7},{5,8},{6,9},{7,10},{8,11},{9,12},{10... | collective-permute-start | bytes 2211848
  2261.3 56.9 %collective-permute-start.53 = (f32[40,4608]{1,0:T(8,128)S(1)}, f32[40,4608]{1,0:T(8,128)S(1)}, u32[]{:S(2)}, u32[]{:S(2)}) collective-permute-start(f32[40,4608]{1,0:T(8,128)S(1)} %get-tuple-element.110), channel_id=1, source_target_pairs={{0,2},{1,3},{2,4},{3,5},{4,6},{5,7},{6,8},{7,9},{8,10},{9,11},{10,... | collective-permute-start | bytes 2211848
  2303.0 511.3 %collective-permute-start.52 = (f32[40,4608]{1,0:T(8,128)S(1)}, f32[40,4608]{1,0:T(8,128)}, u32[]{:S(2)}, u32[]{:S(2)}) collective-permute-start(f32[40,4608]{1,0:T(8,128)S(1)} %get-tuple-element.110), channel_id=1, source_target_pairs={{0,1},{1,2},{2,3},{3,4},{4,5},{5,6},{6,7},{7,8},{8,9},{9,10},{10,1... | collective-permute-start | bytes 2211848
  2312.1 556.7 %collective-permute-start.18 = (f32[48,1152]{1,0:T(8,128)S(1)}, f32[48,1152]{1,0:T(8,128)S(1)}, u32[]{:S(2)}, u32[]{:S(2)}) collective-permute-start(f32[48,1152]{1,0:T(8,128)S(1)} %copy-done.56), channel_id=1, source_target_pairs={{0,7},{1,8},{2,9},{3,10},{4,11},{5,12},{6,13},{7,14},{8,15},{9,16}... | collective-permute-start | bytes 663560
  2313.4 561.6 %collective-permute-start.17 = (f32[48,1152]{1,0:T(8,128)S(1)}, f32[48,1152]{1,0:T(8,128)}, u32[]{:S(2)}, u32[]{:S(2)}) collective-permute-start(f32[48,1152]{1,0:T(8,128)S(1)} %copy-done.56), channel_id=1, source_target_pairs={{0,6},{1,7},{2,8},{3,9},{4,10},{5,11},{6,12},{7,13},{8,14},{9,15},... | collective-permute-start | bytes 663560
  2315.4 521.9 %collective-permute-start.19 = (f32[36,1152]{1,0:T(8,128)}, f32[36,1152]{1,0:T(8,128)}, u32[]{:S(2)}, u32[]{:S(2)}) collective-permute-start(f32[36,1152]{1,0:T(8,128)} %slice.153), channel_id=1, source_target_pairs={{0,8},{1,9},{2,10},{3,11},{4,12},{5,13},{6,14},{7,15},{8,16},{9,17... | collective-permute-start | bytes 497672
  2319.1 537.3 %collective-permute-start.35 = (f32[36,1152]{1,0:T(8,128)}, f32[36,1152]{1,0:T(8,128)}, u32[]{:S(2)}, u32[]{:S(2)}) collective-permute-start(f32[36,1152]{1,0:T(8,128)} %slice.155), channel_id=1, source_target_pairs={{0,8},{1,9},{2,10},{3,11},{4,12},{5,13},{6,14},{7,15},{8,16},{9,17... | collective-permute-start | bytes 497672
  2814.3 53.1 %collective-permute-start.43 = (f32[36,1152]{1,0:T(8,128)S(1)}, f32[36,1152]{1,0:T(8,128)S(1)}, u32[]{:S(2)}, u32[]{:S(2)}) collective-permute-start(f32[36,1152]{1,0:T(8,128)S(1)} %slice.156), channel_id=1, source_target_pairs={{0,8},{1,9},{2,10},{3,11},{4,12},{5,13},{6,14},{7,15},{8,16},{9,17... | collective-permute-start | bytes 497672
  2921.5 95.9 %collective-permute-start.10 = (f32[48,3456]{1,0:T(8,128)S(1)}, f32[48,3456]{1,0:T(8,128)S(1)}, u32[]{:S(2)}, u32[]{:S(2)}) collective-permute-start(f32[48,3456]{1,0:T(8,128)S(1)} %get-tuple-element.104), channel_id=1, source_target_pairs={{0,7},{1,8},{2,9},{3,10},{4,11},{5,12},{6,13},{7,14},{8,15},{9,16}... | collective-permute-start | bytes 1990664
  2929.5 90.0 %collective-permute-start.9 = (f32[48,3456]{1,0:T(8,128)S(1)}, f32[48,3456]{1,0:T(8,128)S(1)}, u32[]{:S(2)}, u32[]{:S(2)}) collective-permute-start(f32[48,3456]{1,0:T(8,128)S(1)} %get-tuple-element.104), channel_id=1, source_target_pairs={{0,6},{1,7},{2,8},{3,9},{4,10},{5,11},{6,12},{7,13},{8,14},{9,15},... | collective-permute-start | bytes 1990664
  2934.4 57.0 %collective-permute-start.11 = (f32[36,3456]{1,0:T(8,128)S(1)}, f32[36,3456]{1,0:T(8,128)S(1)}, u32[]{:S(2)}, u32[]{:S(2)}) collective-permute-start(f32[36,3456]{1,0:T(8,128)S(1)} %slice.152), channel_id=1, source_target_pairs={{0,8},{1,9},{2,10},{3,11},{4,12},{5,13},{6,14},{7,15},{8,16},{9,17... | collective-permute-start | bytes 1493000
  2937.8 66.4 %collective-permute-start.27 = (f32[36,3456]{1,0:T(8,128)S(1)}, f32[36,3456]{1,0:T(8,128)S(1)}, u32[]{:S(2)}, u32[]{:S(2)}) collective-permute-start(f32[36,3456]{1,0:T(8,128)S(1)} %slice.154), channel_id=1, source_target_pairs={{0,8},{1,9},{2,10},{3,11},{4,12},{5,13},{6,14},{7,15},{8,16},{9,17... | collective-permute-start | bytes 1493000
  2958.2 81.8 %collective-permute-start.8 = (f32[48,3456]{1,0:T(8,128)S(1)}, f32[48,3456]{1,0:T(8,128)}, u32[]{:S(2)}, u32[]{:S(2)}) collective-permute-start(f32[48,3456]{1,0:T(8,128)S(1)} %get-tuple-element.104), channel_id=1, source_target_pairs={{0,5},{1,6},{2,7},{3,8},{4,9},{5,10},{6,11},{7,12},{8,13},{9,14},{... | collective-permute-start | bytes 1990664
  2991.4 55.1 %collective-permute-start.7 = (f32[48,3456]{1,0:T(8,128)S(1)}, f32[48,3456]{1,0:T(8,128)}, u32[]{:S(2)}, u32[]{:S(2)}) collective-permute-start(f32[48,3456]{1,0:T(8,128)S(1)} %get-tuple-element.104), channel_id=1, source_target_pairs={{0,4},{1,5},{2,6},{3,7},{4,8},{5,9},{6,10},{7,11},{8,12},{9,13},{1... | collective-permute-start | bytes 1990664
  3004.1 73.7 %collective-permute-start.6 = (f32[48,3456]{1,0:T(8,128)S(1)}, f32[48,3456]{1,0:T(8,128)}, u32[]{:S(2)}, u32[]{:S(2)}) collective-permute-start(f32[48,3456]{1,0:T(8,128)S(1)} %get-tuple-element.104), channel_id=1, source_target_pairs={{0,3},{1,4},{2,5},{3,6},{4,7},{5,8},{6,9},{7,10},{8,11},{9,12},{10... | collective-permute-start | bytes 1990664
  3017.3 62.8 %collective-permute-start.5 = (f32[48,3456]{1,0:T(8,128)S(1)}, f32[48,3456]{1,0:T(8,128)}, u32[]{:S(2)}, u32[]{:S(2)}) collective-permute-start(f32[48,3456]{1,0:T(8,128)S(1)} %get-tuple-element.104), channel_id=1, source_target_pairs={{0,2},{1,3},{2,4},{3,5},{4,6},{5,7},{6,8},{7,9},{8,10},{9,11},{10,... | collective-permute-start | bytes 1990664
  3020.4 61.9 %collective-permute-start.4 = (f32[48,3456]{1,0:T(8,128)S(1)}, f32[48,3456]{1,0:T(8,128)}, u32[]{:S(2)}, u32[]{:S(2)}) collective-permute-start(f32[48,3456]{1,0:T(8,128)S(1)} %get-tuple-element.104), channel_id=1, source_target_pairs={{0,1},{1,2},{2,3},{3,4},{4,5},{5,6},{6,7},{7,8},{8,9},{9,10},{10,1... | collective-permute-start | bytes 1990664
  3039.9 72.3 %collective-permute-start.26 = (f32[48,3456]{1,0:T(8,128)S(1)}, f32[48,3456]{1,0:T(8,128)}, u32[]{:S(2)}, u32[]{:S(2)}) collective-permute-start(f32[48,3456]{1,0:T(8,128)S(1)} %get-tuple-element.105), channel_id=1, source_target_pairs={{0,7},{1,8},{2,9},{3,10},{4,11},{5,12},{6,13},{7,14},{8,15},{9,16}... | collective-permute-start | bytes 1990664
  3046.5 69.1 %collective-permute-start.25 = (f32[48,3456]{1,0:T(8,128)S(1)}, f32[48,3456]{1,0:T(8,128)}, u32[]{:S(2)}, u32[]{:S(2)}) collective-permute-start(f32[48,3456]{1,0:T(8,128)S(1)} %get-tuple-element.105), channel_id=1, source_target_pairs={{0,6},{1,7},{2,8},{3,9},{4,10},{5,11},{6,12},{7,13},{8,14},{9,15},... | collective-permute-start | bytes 1990664
  3077.8 73.6 %collective-permute-start.24 = (f32[48,3456]{1,0:T(8,128)S(1)}, f32[48,3456]{1,0:T(8,128)}, u32[]{:S(2)}, u32[]{:S(2)}) collective-permute-start(f32[48,3456]{1,0:T(8,128)S(1)} %get-tuple-element.105), channel_id=1, source_target_pairs={{0,5},{1,6},{2,7},{3,8},{4,9},{5,10},{6,11},{7,12},{8,13},{9,14},{... | collective-permute-start | bytes 1990664
  3080.1 73.7 %collective-permute-start.23 = (f32[48,3456]{1,0:T(8,128)S(1)}, f32[48,3456]{1,0:T(8,128)}, u32[]{:S(2)}, u32[]{:S(2)}) collective-permute-start(f32[48,3456]{1,0:T(8,128)S(1)} %get-tuple-element.105), channel_id=1, source_target_pairs={{0,4},{1,5},{2,6},{3,7},{4,8},{5,9},{6,10},{7,11},{8,12},{9,13},{1... | collective-permute-start | bytes 1990664
  3082.2 74.9 %collective-permute-start.22 = (f32[48,3456]{1,0:T(8,128)S(1)}, f32[48,3456]{1,0:T(8,128)}, u32[]{:S(2)}, u32[]{:S(2)}) collective-permute-start(f32[48,3456]{1,0:T(8,128)S(1)} %get-tuple-element.105), channel_id=1, source_target_pairs={{0,3},{1,4},{2,5},{3,6},{4,7},{5,8},{6,9},{7,10},{8,11},{9,12},{10... | collective-permute-start | bytes 1990664
  3112.3 85.2 %collective-permute-start.21 = (f32[48,3456]{1,0:T(8,128)S(1)}, f32[48,3456]{1,0:T(8,128)}, u32[]{:S(2)}, u32[]{:S(2)}) collective-permute-start(f32[48,3456]{1,0:T(8,128)S(1)} %get-tuple-element.105), channel_id=1, source_target_pairs={{0,2},{1,3},{2,4},{3,5},{4,6},{5,7},{6,8},{7,9},{8,10},{9,11},{10,... | collective-permute-start | bytes 1990664
  3115.6 83.4 %collective-permute-start.20 = (f32[48,3456]{1,0:T(8,128)S(1)}, f32[48,3456]{1,0:T(8,128)}, u32[]{:S(2)}, u32[]{:S(2)}) collective-permute-start(f32[48,3456]{1,0:T(8,128)S(1)} %get-tuple-element.105), channel_id=1, source_target_pairs={{0,1},{1,2},{2,3},{3,4},{4,5},{5,6},{6,7},{7,8},{8,9},{9,10},{10,1... | collective-permute-start | bytes 1990664
  3151.4 89.3 %collective-permute-start.2 = (f32[40,6912]{1,0:T(8,128)S(1)}, f32[40,6912]{1,0:T(8,128)}, u32[]{:S(2)}, u32[]{:S(2)}) collective-permute-start(f32[40,6912]{1,0:T(8,128)S(1)} %copy-done.39), channel_id=1, source_target_pairs={{0,3},{1,4},{2,5},{3,6},{4,7},{5,8},{6,9},{7,10},{8,11},{9,12},{10... | collective-permute-start | bytes 3317768
  3153.8 86.9 %collective-permute-start.1 = (f32[40,6912]{1,0:T(8,128)S(1)}, f32[40,6912]{1,0:T(8,128)}, u32[]{:S(2)}, u32[]{:S(2)}) collective-permute-start(f32[40,6912]{1,0:T(8,128)S(1)} %copy-done.39), channel_id=1, source_target_pairs={{0,2},{1,3},{2,4},{3,5},{4,6},{5,7},{6,8},{7,9},{8,10},{9,11},{10,... | collective-permute-start | bytes 3317768
  3157.1 83.6 %collective-permute-start = (f32[40,6912]{1,0:T(8,128)S(1)}, f32[40,6912]{1,0:T(8,128)}, u32[]{:S(2)}, u32[]{:S(2)}) collective-permute-start(f32[40,6912]{1,0:T(8,128)S(1)} %copy-done.39), channel_id=1, source_target_pairs={{0,1},{1,2},{2,3},{3,4},{4,5},{5,6},{6,7},{7,8},{8,9},{9,10},{10,1... | collective-permute-start | bytes 3317768
  3197.5 43.2 %collective-permute-start.3 = (f32[4,6912]{1,0:T(4,128)S(1)}, f32[4,6912]{1,0:T(4,128)S(1)}, u32[]{:S(2)}, u32[]{:S(2)}) collective-permute-start(f32[4,6912]{1,0:T(4,128)S(1)} %slice.151), channel_id=1, source_target_pairs={{0,4},{1,5},{2,6},{3,7},{4,8},{5,9},{6,10},{7,11},{8,12},{9,13},{1... | collective-permute-start | bytes 331784
  (193 other events, 6330.0 us)
Sparse Core Ops, SparseCore 0:
  11.0 124.2 all-gather.39
  138.7 109.1 all-gather.21
  251.4 63.7 all-gather.23
  318.5 91.0 all-gather.29
  413.0 109.4 all-gather.25
  525.8 63.7 all-gather.27
  593.1 67.1 all-gather.31
  663.8 64.3 all-gather.33
  731.7 134.6 all-gather.35
  869.2 85.2 all-gather.37
  1045.3 32.6 reduce-scatter.24
  1189.9 296.1 all-reduce.24
  1616.8 333.8 reduce-scatter.22
where the time goes:
time: 3300 us; the launch traced here: 3280 us
  blocking collectives  1470 us (45%)
  waiting for transfers between devices  662 us (20%)
  local copies, waits for them, and re-layouts  429 us (13%)
  starting transfers between devices  347 us (11%)
  matrix products  308 us (9%)
  other arithmetic  44 us (1%)
    unnamed x3, blocking collectives  1420 us
    unnamed x58, starting transfers between devices  330 us
    unnamed x384, local copies, waits for them, and re-layouts  238 us
    all_gather x1, waiting for transfers between devices, per_device(): lax.all_gather(mlp_in[layer_idx], ('clip', 'seq'), axis=0, tiled=True)  131 us
    all_gather x1, waiting for transfers between devices, per_device(): lax.all_gather(t_qkv[layer_idx], ('clip', 'seq'), axis=0, tiled=True)  107 us
    dot_general x10, matrix products, product(): lax.dot_general(left_arr, right_arr, (((left_arr.ndim - 1,), (0,)), ((),...  91.5 us
    dot_general x9, matrix products, product_back(): lax.dot_general(grad_arr, weight, (((grad_arr.ndim - 1,), (1,)), ((), ())...  86 us
    all_gather x1, waiting for transfers between devices, per_device(): lax.all_gather(c_kv[layer_idx], ('clip', 'seq'), axis=0, tiled=True)  76 us
  transfers between devices with their start and end apart: 73, of which 16 were waited for; matrix products, arithmetic and copies ran while one was open for 65% of the time, Pallas kernels for 0%

commit v1 on v0

--- a/solution.py
+++ b/solution.py
@@ -497,6 +497,331 @@
     )
 
 
+ROWS = 36
+PADDED = 40
+HALF = 2304
+ORDERS = ("xy", "yx", "xy", "yx")
+SWAP = {"x": [(i, i ^ 2) for i in range(8)], "y": [(i, i ^ 4) for i in range(8)], "k": [(i, i ^ 1) for i in range(8)]}
+
+
+def mesh_coords():
+    clip_at = lax.axis_index("clip")
+    seq_at = lax.axis_index("seq")
+    return clip_at, lax.div(seq_at, 4), lax.rem(lax.div(seq_at, 2), 2), lax.rem(seq_at, 2)
+
+
+def swap(arr, axis):
+    return lax.ppermute(arr, "seq", SWAP[axis])
+
+
+def turn(arr, d):
+    return lax.ppermute(arr, "clip", [(i, (i + d) % 4) for i in range(4)])
+
+
+def row_place(order, at):
+    z, y, x, k = at
+    spots = jnp.arange(2 * 16 * PADDED)
+    row, back = spots % PADDED, (spots // PADDED) % 4
+    first, second, core = (spots // (4 * PADDED)) % 2, (spots // (8 * PADDED)) % 2, spots // (16 * PADDED)
+    step_x, step_y = (first, second) if order == "xy" else (second, first)
+    owner = ((z + 4 - back) % 4) * 8 + (y ^ step_y) * 4 + (x ^ step_x) * 2 + (k ^ core)
+    source = jnp.where(row < ROWS, owner * ROWS + row, -1)
+    return (jnp.arange(32 * ROWS)[:, None] == source[None, :]).astype(jnp.bfloat16)
+
+
+def gather_stage(own, order, place):
+    block = own[None]
+    block = jnp.concatenate([block] + [turn(block, d) for d in (1, 2, 3)], axis=0)
+    for axis in order:
+        block = jnp.concatenate([block, swap(block, axis)], axis=0)
+    other = swap(block, "k")
+    half = place.shape[1] // 2
+    low = product(place[:, :half], block.reshape(half, -1))
+    return (low + product(place[:, half:], other.reshape(half, -1))).astype(jnp.bfloat16)
+
+
+def scatter_stage(total, order, at):
+    k = at[3]
+    block = total.reshape(2, 2, 2, 4, PADDED, HALF)
+    block = block[:, 0] + swap(block[:, 1], order[1])
+    block = block[:, 0] + swap(block[:, 1], order[0])
+    kept = block[:, 0].astype(jnp.float32)
+    for d in (1, 2, 3):
+        kept = kept + turn(block[:, d], 4 - d).astype(jnp.float32)
+    mine, other = kept[0], swap(kept[1], "k")
+    low, high = jnp.where(k == 0, mine, other), jnp.where(k == 0, other, mine)
+    return jnp.concatenate([low, high], axis=1)[:ROWS]
+
+
+def gather_blocks(own, at):
+    z, y, x, k = at
+    block = jnp.stack([own] + [turn(own, d) for d in (1, 2, 3)])
+    block = jnp.stack([lax.dynamic_index_in_dim(block, (z + 4 - i) % 4, 0, keepdims=False) for i in range(4)])
+
+    def both(arr, axis, bit):
+        other = swap(arr, axis)
+        return jnp.stack([jnp.where(bit == 0, arr, other), jnp.where(bit == 0, other, arr)], axis=-3)
+
+    block = both(both(both(block[:, None], "y", y)[:, 0], "x", x), "k", k)
+    return block.reshape(32 * own.shape[0], own.shape[1])
+
+
+def scatter_blocks(total, at):
+    z, y, x, k = at
+    block = total.reshape(4, 2, 2, 2, 144, 640)
+
+    def halve(arr, axis, name, bit):
+        sent = lax.dynamic_index_in_dim(arr, 1 - bit, axis, keepdims=False)
+        return lax.dynamic_index_in_dim(arr, bit, axis, keepdims=False) + swap(sent, name)
+
+    block = halve(halve(block, 2, "x", x), 1, "y", y)
+    kept = lax.dynamic_index_in_dim(block, z, 0, keepdims=False).astype(jnp.float32)
+    for d in (1, 2, 3):
+        sent = lax.dynamic_index_in_dim(block, (z + d) % 4, 0, keepdims=False)
+        kept = kept + turn(sent, d).astype(jnp.float32)
+    mine = lax.dynamic_index_in_dim(kept, k, 0, keepdims=False)
+    other = swap(lax.dynamic_index_in_dim(kept, 1 - k, 0, keepdims=False), "k")
+    low, high = jnp.where(k == 0, mine, other), jnp.where(k == 0, other, mine)
+    return jnp.concatenate([low, high[:, 128:]], axis=1)
+
+
+def natural_qkv(inputs, weight, query_bias, value_bias, heads):
+    width = query_bias.shape[0]
+    bias_row = jnp.concatenate([query_bias, jnp.zeros_like(query_bias), value_bias])
+    packed = (product(inputs, weight) + bias_row).astype(jnp.bfloat16)
+    return tuple(split_heads(packed[..., i * width : (i + 1) * width], heads) for i in range(3))
+
+
+def fast_device(
+    tokens,
+    text,
+    timesteps,
+    text_counts,
+    out_grad,
+    time_weight,
+    s_qkv,
+    s_proj,
+    t_qkv,
+    t_proj,
+    c_query,
+    c_kv,
+    c_proj,
+    mlp_in,
+    mlp_out,
+    vectors,
+):
+    heads = HEADS
+    _, frame_count, patch_count, width = tokens.shape
+    rows = frame_count * patch_count
+    z, y, x, k = mesh_coords()
+    shard = z * 8 + lax.axis_index("seq")
+    pad = ((0, 4), (0, 0))
+    own = [
+        jnp.pad(jnp.concatenate([s_qkv[0], s_proj[0]], axis=1), pad),
+        jnp.pad(jnp.concatenate([t_qkv[0], t_proj[0]], axis=1), pad),
+        jnp.pad(jnp.concatenate([c_query[0], c_kv[0], c_proj[0]], axis=1), pad),
+        jnp.pad(mlp_in[0], pad),
+    ]
+    places = [row_place(order, (z, y, x, k)) for order in ORDERS]
+    stages = [gather_stage(own[i], ORDERS[i], places[i]) for i in range(4)]
+    w_out = gather_blocks(mlp_out[0], (z, y, x, k))
+    w_sqkv, w_sproj = stages[0][:, :3456], stages[0][:, 3456:]
+    w_tqkv, w_tproj = stages[1][:, :3456], stages[1][:, 3456:]
+    w_cquery, w_ckv, w_cproj = stages[2][:, :1152], stages[2][:, 1152:3456], stages[2][:, 3456:]
+    w_in = stages[3]
+
+    embed = jax.nn.silu(timestep_embed(timesteps, width)).astype(jnp.bfloat16)
+    own_embed = lax.dynamic_slice_in_dim(embed, shard * ROWS, ROWS, axis=1)
+    mod_part = product(own_embed, time_weight)
+    own_vec = jnp.pad(vectors[0].astype(jnp.float32), ((0, 0), (0, width - ROWS)))
+    own_vec = jnp.roll(own_vec, shard * ROWS, axis=1).reshape(4, 5 * width)
+    spread = lax.psum(jnp.concatenate([mod_part, own_vec], axis=1), ("clip", "seq"))
+    modulation = lax.dynamic_slice_in_dim(spread[:, : 6 * width], z, 1, axis=0)
+    modulation = modulation.reshape(1, 6, width)
+    vec_float = spread[:, 6 * width :].reshape(20, width)
+    hidden = tokens.astype(jnp.float32).reshape(1, rows, width)
+    out_rows = out_grad.astype(jnp.float32).reshape(1, rows, width)
+    text_mask = (jnp.arange(text.shape[1])[None, :] < text_counts[:, None])[:, None, None, :]
+
+    mod_table = modulation + vec_float[10:16][None]
+    gate_one, gate_two = mod_table[:, None, 2], mod_table[:, None, 5]
+    normed = modulate(hidden, mod_table[:, 0], mod_table[:, 1]).astype(jnp.bfloat16)
+    frames = normed.reshape(frame_count, patch_count, width)
+    s_parts = natural_qkv(frames, w_sqkv, vec_float[0], vec_float[1], heads)
+    s_mixed, s_total = attend_forward(*s_parts, None, SPATIAL)
+    s_flat = merge_heads(s_mixed)
+    s_branch = (product(s_flat, w_sproj) + vec_float[2]).reshape(1, rows, width)
+    hidden_one = hidden + gate_one * s_branch
+    moved = lax.all_to_all(
+        hidden_one.astype(jnp.bfloat16).reshape(1, frame_count, patch_count, width),
+        "seq",
+        split_axis=2,
+        concat_axis=1,
+        tiled=True,
+    )
+    t_parts = natural_qkv(moved, w_tqkv, vec_float[3], vec_float[4], heads)
+    t_mixed, t_total = attend_forward(*t_parts, None, TEMPORAL)
+    t_flat = merge_heads(t_mixed)
+    t_branch = (product(t_flat, w_tproj) + vec_float[5]).astype(jnp.bfloat16)
+    t_back = lax.all_to_all(t_branch, "seq", split_axis=1, concat_axis=2, tiled=True).reshape(1, rows, width)
+    hidden_two = hidden_one + gate_one * t_back.astype(jnp.float32)
+    cross_in = hidden_two.astype(jnp.bfloat16)
+    c_query_rows = split_heads((product(cross_in, w_cquery) + vec_float[6]).astype(jnp.bfloat16), heads)
+    kv_bias = jnp.concatenate([jnp.zeros_like(vec_float[7]), vec_float[7]])
+    kv_rows = (product(text, w_ckv) + kv_bias).astype(jnp.bfloat16)
+    c_key, c_value = split_heads(kv_rows[..., :width], heads), split_heads(kv_rows[..., width:], heads)
+    c_mixed, c_total = attend_forward(c_query_rows, c_key, c_value, text_mask, CROSS)
+    c_flat = merge_heads(c_mixed)
+    hidden_three = hidden_two + (product(c_flat, w_cproj) + vec_float[8])
+    normed_two = modulate(hidden_three, mod_table[:, 3], mod_table[:, 4]).astype(jnp.bfloat16)
+    inner_act = product(normed_two, w_in) + vec_float[16:].reshape(-1)
+    gelu_out = jax.nn.gelu(inner_act, approximate=True).astype(jnp.bfloat16)
+    mlp_branch = product(gelu_out, w_out) + vec_float[9]
+    hidden_four = hidden_three + gate_two * mlp_branch
+
+    core_swap = [(i, i ^ 1) for i in range(8)]
+
+    def pair(arr):
+        flat = arr.reshape(-1, arr.shape[-1])
+        return jnp.concatenate([flat, lax.ppermute(flat, "seq", core_swap)], axis=0)
+
+    def choose(low, high):
+        return jnp.where(k == 0, low, high)
+
+    def sums_of(left, right):
+        return lax.dot_general(left, right, (((0,), (0,)), ((), ())), preferred_element_type=jnp.float32).astype(
+            jnp.bfloat16
+        )
+
+    def packed_rows(arr, stage):
+        return product(arr, places[stage]).astype(jnp.bfloat16)
+
+    grad_mlp = (out_rows * gate_two).astype(jnp.bfloat16)
+    grad_gate_two = jnp.sum(out_rows * mlp_branch, axis=1)
+    pair_mlp = pair(grad_mlp)
+    sum_out = sums_of(pair(gelu_out), choose(pair_mlp[:, :640], pair_mlp[:, 512:]))
+    bias_out = column_sum(grad_mlp)
+    grad_gelu = product_back(grad_mlp, w_out)
+    gelu_pull = jax.vjp(partial(jax.nn.gelu, approximate=True), inner_act)[1]
+    grad_inner = gelu_pull(grad_gelu)[0].astype(jnp.bfloat16)
+    pair_inner = pair(grad_inner)
+    sum_in = sums_of(packed_rows(pair(normed_two), 3), choose(pair_inner[:, :HALF], pair_inner[:, HALF:]))
+    bias_in = column_sum(grad_inner)
+    norm_pull = jax.vjp(modulate, hidden_three, mod_table[:, 3], mod_table[:, 4])[1]
+    grad_three, grad_shift_two, grad_scale_two = norm_pull(product_back(grad_inner, w_in))
+    grad_three = out_rows + grad_three
+    grad_cross = grad_three.astype(jnp.bfloat16)
+    bias_cproj = column_sum(grad_cross)
+    grad_cmixed = split_heads(product_back(grad_cross, w_cproj).astype(jnp.bfloat16), heads)
+    cq_grad, ck_grad, cv_grad = attend_backward(
+        c_query_rows, c_key, c_value, text_mask, c_total, grad_cmixed, CROSS
+    )
+    grad_cquery = merge_heads(cq_grad).astype(jnp.bfloat16)
+    bias_cquery = column_sum(grad_cquery)
+    grad_two = grad_three + product_back(grad_cquery, w_cquery)
+    grad_kv = jnp.concatenate([merge_heads(ck_grad), merge_heads(cv_grad)], axis=-1).astype(jnp.bfloat16)
+    bias_cvalue = column_sum(grad_kv[..., width:])
+    text_part = product_back(grad_kv, w_ckv)
+    pair_kv = pair(grad_kv)
+    text_two = jnp.concatenate([text[0], text[0]], axis=0)
+    sum_kv = sums_of(packed_rows(text_two, 2), choose(pair_kv[:, :width], pair_kv[:, width:]))
+    sum_side = sums_of(packed_rows(choose(pair(cross_in), pair(c_flat)), 2), choose(pair(grad_cquery), pair(grad_cross)))
+    sum_cross = choose(jnp.concatenate([sum_side, sum_kv], 1), jnp.concatenate([sum_kv, sum_side], 1))
+
+    grad_gate_one = jnp.sum(grad_two * t_back.astype(jnp.float32), axis=1)
+    grad_temporal = (grad_two * gate_one).astype(jnp.bfloat16).reshape(1, frame_count, patch_count, width)
+    grad_places = lax.all_to_all(grad_temporal, "seq", split_axis=2, concat_axis=1, tiled=True)
+    bias_tproj = column_sum(grad_places)
+    grad_tmixed = split_heads(product_back(grad_places, w_tproj).astype(jnp.bfloat16), heads)
+
+    def stage_sums(grads, inputs, flat, proj_grad, weight, stage):
+        packed_grad = jnp.concatenate([merge_heads(part) for part in grads], axis=-1).astype(jnp.bfloat16)
+        pair_grad, pair_in = pair(packed_grad), pair(inputs)
+        low = sums_of(packed_rows(pair_in, stage), choose(pair_grad[:, :width], pair_grad[:, 2 * width :]))
+        high = sums_of(
+            packed_rows(choose(pair_in, pair(flat)), stage), choose(pair_grad[:, width : 2 * width], pair(proj_grad))
+        )
+        return (
+            jnp.concatenate([low, high], axis=1),
+            product_back(packed_grad, weight),
+            column_sum(packed_grad[..., :width]),
+            column_sum(packed_grad[..., 2 * width :]),
+        )
+
+    t_grads = attend_backward(*t_parts, None, t_total, grad_tmixed, TEMPORAL)
+    sum_t, grad_moved, bias_tquery, bias_tvalue = stage_sums(t_grads, moved, t_flat, grad_places, w_tqkv, 1)
+    grad_frames = lax.all_to_all(
+        grad_moved.astype(jnp.bfloat16), "seq", split_axis=1, concat_axis=2, tiled=True
+    )
+    grad_one = grad_two + grad_frames.astype(jnp.float32).reshape(1, rows, width)
+    grad_gate_one = grad_gate_one + jnp.sum(grad_one * s_branch, axis=1)
+    grad_spatial = (grad_one * gate_one).astype(jnp.bfloat16).reshape(frame_count, patch_count, width)
+    bias_sproj = column_sum(grad_spatial)
+    grad_smixed = split_heads(product_back(grad_spatial, w_sproj).astype(jnp.bfloat16), heads)
+    s_grads = attend_backward(*s_parts, None, s_total, grad_smixed, SPATIAL)
+    sum_s, grad_normed, bias_squery, bias_svalue = stage_sums(s_grads, frames, s_flat, grad_spatial, w_sqkv, 0)
+    first_pull = jax.vjp(modulate, hidden, mod_table[:, 0], mod_table[:, 1])[1]
+    grad_zero, grad_shift_one, grad_scale_one = first_pull(grad_normed.reshape(1, rows, width))
+    grad_input = grad_one + grad_zero
+
+    own_s, own_t, own_c, own_in = [
+        scatter_stage(total, ORDERS[i], (z, y, x, k))
+        for i, total in enumerate([sum_s, sum_t, sum_cross, sum_in])
+    ]
+    own_out = scatter_blocks(sum_out, (z, y, x, k))
+
+    grad_table = jnp.stack(
+        [grad_shift_one, grad_scale_one, grad_gate_one, grad_shift_two, grad_scale_two, grad_gate_two], axis=1
+    )[0]
+    bias_rows = jnp.stack(
+        [
+            bias_squery,
+            bias_svalue,
+            bias_sproj,
+            bias_tquery,
+            bias_tvalue,
+            bias_tproj,
+            bias_cquery,
+            bias_cvalue,
+            bias_cproj,
+            bias_out,
+        ]
+    )
+    small = jnp.concatenate([bias_rows, grad_table, bias_in.reshape(4, width)], axis=0)
+    own_clip = (jnp.arange(4) == z).astype(jnp.float32)[:, None, None]
+    small = lax.psum(own_clip * small[None], ("clip", "seq"))
+    vec_grad = lax.dynamic_slice_in_dim(jnp.sum(small, axis=0), shard * ROWS, ROWS, axis=1)
+    time_grad = lax.dot_general(
+        own_embed.astype(jnp.float32),
+        small[:, 10:16].reshape(4, 6 * width),
+        (((0,), (0,)), ((), ())),
+        precision=HIGHEST,
+        preferred_element_type=jnp.float32,
+    )
+    text_grad = lax.psum_scatter(text_part, "seq", scatter_dimension=2, tiled=True)
+    return (
+        hidden_four.reshape(tokens.shape),
+        grad_input.reshape(tokens.shape),
+        text_grad,
+        time_grad,
+        own_s[None, :, :3456],
+        own_s[None, :, 3456:],
+        own_t[None, :, :3456],
+        own_t[None, :, 3456:],
+        own_c[None, :, :1152],
+        own_c[None, :, 1152:3456],
+        own_c[None, :, 3456:],
+        own_in[None],
+        own_out[None],
+        vec_grad[None],
+    )
+
+
+def run_device(sizes, tokens, *rest):
+    fits = (sizes["clip"], sizes["seq"]) == (4, 8) and tokens.shape == (1, 2, 256, 1152)
+    return (fast_device if fits else per_device)(tokens, *rest)
+
+
 def solution(mesh):
     placed = (
         P("clip", "seq", None, None),
@@ -517,7 +842,7 @@
         P(None, None, ("clip", "seq")),
     )
     return jax.shard_map(
-        per_device,
+        partial(run_device, dict(mesh.shape)),
         mesh=mesh,
         in_specs=placed,
         out_specs=(

time: 3300 us -> 1540 us (0.47)
  blocking collectives: 1470 us -> 0 us
  starting transfers between devices: 347 us -> 149 us
  local copies, waits for them, and re-layouts: 429 us -> 248 us
  matrix products: 308 us -> 416 us
  waiting for transfers between devices: 662 us -> 600 us
  other arithmetic: 44 us -> 98 us
    unnamed x3 -> x0, blocking collectives: 1420 us -> none
    all_gather x10 -> x0, waiting for transfers between devices: 622 us -> none  [the longest x1 131 us: per_device(): lax.all_gather(mlp_in[layer_idx], ('clip', 'seq'), axis=0, tiled=True)]
    ppermute x0 -> x77, waiting for transfers between devices: none -> 494 us  [the longest x30 327 us: swap(): return lax.ppermute(arr, 'seq', SWAP[axis])]
    unnamed x58 -> x0, starting transfers between devices: 330 us -> none
    unnamed x384 -> x302, local copies, waits for them, and re-layouts: 238 us -> 47.5 us
    ppermute x0 -> x77, starting transfers between devices: none -> 132 us  [the longest x30 99.3 us: turn(): return lax.ppermute(arr, 'clip', [(i, (i + d) % 4) for i in range(4)])]
    psum x0 -> x2, waiting for transfers between devices: none -> 105 us  [the longest x1 105 us: fast_device(): small = lax.psum(own_clip * small[None], ('clip', 'seq'))]
    dot_general x10 -> x18, matrix products: 91.5 us -> 189 us  [product(): lax.dot_general(left_arr, right_arr, (((left_arr.ndim - 1,), (0,)), ((),...]
  transfers between devices with their start and end apart: 73 -> 84, of which waited for: 16 -> 25; matrix products, arithmetic and copies ran while one was open for 65% -> 40% of each run, Pallas kernels for 0% -> 0%
where the time goes in v1:
time: 1540 us; the launch traced here: 1530 us
  waiting for transfers between devices  600 us (39%)
  matrix products  416 us (27%)
  local copies, waits for them, and re-layouts  248 us (16%)
  starting transfers between devices  149 us (10%)
  other arithmetic  98 us (6%)
  between operations  17.2 us (1%)
    ppermute x30, waiting for transfers between devices, swap(): return lax.ppermute(arr, 'seq', SWAP[axis])  327 us
    dot_general x18, matrix products, product(): lax.dot_general(left_arr, right_arr, (((left_arr.ndim - 1,), (0,)), ((),...  189 us
    ppermute x30, waiting for transfers between devices, turn(): return lax.ppermute(arr, 'clip', [(i, (i + d) % 4) for i in range(4)])  168 us
    psum x1, waiting for transfers between devices, fast_device(): small = lax.psum(own_clip * small[None], ('clip', 'seq'))  105 us
    ppermute x30, starting transfers between devices, turn(): return lax.ppermute(arr, 'clip', [(i, (i + d) % 4) for i in range(4)])  99.3 us
    dot_general x8, matrix products, sums_of(): lax.dot_general(left, right, (((0,), (0,)), ((), ())), preferred_element_...  96.7 us
    dot_general x9, matrix products, product_back(): lax.dot_general(grad_arr, weight, (((grad_arr.ndim - 1,), (1,)), ((), ())...  76.4 us
    concatenate x14, local copies, waits for them, and re-layouts, stage_sums(): jnp.concatenate([merge_heads(part) for part in grads], axis=-1)  50.1 us
  transfers between devices with their start and end apart: 84, of which 25 were waited for; matrix products, arithmetic and copies ran while one was open for 40% of the time, Pallas kernels for 0%

profile of v1, /device:TPU:0, one launch (start us, length us, event | category | flops | bytes accessed | tf_op | source)
XLA Modules:
  0.0 1528.1 jit_solution(17622341417723839864)
XLA Ops:
  43.1 17.0 %collective-permute-start.13 = (bf16[1,40,4608]{2,1,0:T(8,128)(2,1)}, bf16[1,40,4608]{2,1,0:T(8,128)(2,1)S(1)}, u32[]{:S(2)}, u32[]{:S(2)}) collective-permute-start(bf16[1,40,4608]{2,1,0:T(8,128)(2,1)} %fusion.248), channel_id=1, source_target_pairs={{0,16},{8,24},{16,0},{24,8},{1,17},{9,25},{17,1},{25,9},{2,18},{10... | collective-permute-start | bytes 1105928 | tf_op jit(solution)/shard_map/ppermute | solution.py:518
  63.2 19.3 %collective-permute-done.19 = bf16[1,40,4608]{2,1,0:T(8,128)(2,1)S(1)} collective-permute-done((bf16[1,40,4608]{2,1,0:T(8,128)(2,1)S(1)}, bf16[1,40,4608]{2,1,0:T(8,128)(2,1)S(1)}, u32[]{:S(2)}, u32[]{:S(2)}) %collective-permute-start.19) | collective-permute-done | bytes 368672 | tf_op jit(solution)/shard_map/ppermute | solution.py:518
  93.9 20.7 %collective-permute-done.13 = bf16[1,40,4608]{2,1,0:T(8,128)(2,1)S(1)} collective-permute-done((bf16[1,40,4608]{2,1,0:T(8,128)(2,1)}, bf16[1,40,4608]{2,1,0:T(8,128)(2,1)S(1)}, u32[]{:S(2)}, u32[]{:S(2)}) %collective-permute-start.13) | collective-permute-done | bytes 368672 | tf_op jit(solution)/shard_map/ppermute | solution.py:518
  114.6 7.9 collective-permute-start
  127.2 19.5 %collective-permute-done.7 = bf16[1,40,4608]{2,1,0:T(8,128)(2,1)S(1)} collective-permute-done((bf16[1,40,4608]{2,1,0:T(8,128)(2,1)S(1)}, bf16[1,40,4608]{2,1,0:T(8,128)(2,1)S(1)}, u32[]{:S(2)}, u32[]{:S(2)}) %collective-permute-start.7) | collective-permute-done | bytes 368672 | tf_op jit(solution)/shard_map/ppermute | solution.py:518
  150.5 12.2 collective-permute-done.1
  183.9 32.6 %collective-permute-done.3 = bf16[4,40,4608]{2,1,0:T(8,128)(2,1)S(1)} collective-permute-done((bf16[4,40,4608]{2,1,0:T(8,128)(2,1)S(1)}, bf16[4,40,4608]{2,1,0:T(8,128)(2,1)S(1)}, u32[]{:S(2)}, u32[]{:S(2)}) %collective-permute-start.3) | collective-permute-done | bytes 1474592 | tf_op jit(solution)/shard_map/ppermute | solution.py:514
  223.3 50.2 %collective-permute-done.28 = bf16[4,2,144,1152]{3,2,1,0:T(8,128)(2,1)S(1)} collective-permute-done((bf16[4,2,144,1152]{3,2,1,0:T(8,128)(2,1)S(1)}, bf16[4,2,144,1152]{3,2,1,0:T(8,128)(2,1)S(1)}, u32[]{:S(2)}, u32[]{:S(2)}) %collective-permute-start.28) | collective-permute-done | bytes 2654240 | tf_op jit(solution)/shard_map/ppermute | solution.py:514
  284.9 21.0 %collective-permute-done.4 = bf16[8,40,4608]{2,1,0:T(8,128)(2,1)S(1)} collective-permute-done((bf16[8,40,4608]{2,1,0:T(8,128)(2,1)}, bf16[8,40,4608]{2,1,0:T(8,128)(2,1)S(1)}, u32[]{:S(2)}, u32[]{:S(2)}) %collective-permute-start.4) | collective-permute-done | bytes 2949152 | tf_op jit(solution)/shard_map/ppermute | solution.py:514
  317.0 19.8 %collective-permute-done.22 = bf16[8,40,4608]{2,1,0:T(8,128)(2,1)} collective-permute-done((bf16[8,40,4608]{2,1,0:T(8,128)(2,1)}, bf16[8,40,4608]{2,1,0:T(8,128)(2,1)}, u32[]{:S(2)}, u32[]{:S(2)}) %collective-permute-start.22) | collective-permute-done | bytes 2949152 | tf_op jit(solution)/shard_map/ppermute | solution.py:514
  340.4 27.7 %collective-permute-done.16 = bf16[8,40,4608]{2,1,0:T(8,128)(2,1)} collective-permute-done((bf16[8,40,4608]{2,1,0:T(8,128)(2,1)}, bf16[8,40,4608]{2,1,0:T(8,128)(2,1)}, u32[]{:S(2)}, u32[]{:S(2)}) %collective-permute-start.16) | collective-permute-done | bytes 2949152 | tf_op jit(solution)/shard_map/ppermute | solution.py:514
  371.7 26.5 %collective-permute-done.10 = bf16[8,40,4608]{2,1,0:T(8,128)(2,1)} collective-permute-done((bf16[8,40,4608]{2,1,0:T(8,128)(2,1)}, bf16[8,40,4608]{2,1,0:T(8,128)(2,1)}, u32[]{:S(2)}, u32[]{:S(2)}) %collective-permute-start.10) | collective-permute-done | bytes 2949152 | tf_op jit(solution)/shard_map/ppermute | solution.py:514
  411.3 14.5 fusion.174
  425.8 17.5 %fusion = bf16[1152,4608]{1,0:T(8,128)(2,1)} fusion(f32[1152,4608]{1,0:T(8,128)} %fusion.174, bf16[640,4608]{1,0:T(8,128)(2,1)} %bitcast.655, pred[1152,1280]{1,0:T(32,128)(4,1)S(1)} %copy-done.59), kind=kOutput, calls=%fused_computation.4 | convolution fusion | flops 6805389312 | bytes 38486016 | tf_op jit(solution)/shard_map/dot_general | solution.py:20
  443.3 8.8 add_convert_fusion.1
  480.0 15.6 %fusion.166 = f32[1152,4608]{1,0:T(8,128)} fusion(bf16[640,4608]{1,0:T(8,128)(2,1)} %bitcast.56, pred[1152,1280]{1,0:T(32,128)(4,1)} %iota_compare_fusion), kind=kOutput, calls=%fused_computation.276 | convolution fusion | flops 6794772480 | bytes 27869184 | tf_op jit(solution)/shard_map/dot_general | solution.py:20
  495.6 14.5 fusion.168
  510.1 17.4 %fusion.3 = bf16[1152,4608]{1,0:T(8,128)(2,1)} fusion(f32[1152,4608]{1,0:T(8,128)} %fusion.166, bf16[640,4608]{1,0:T(8,128)(2,1)} %bitcast.656, pred[1152,1280]{1,0:T(32,128)(4,1)S(1)} %copy-done.61), kind=kOutput, calls=%fused_computation.7 | convolution fusion | flops 6805389312 | bytes 38486016 | tf_op jit(solution)/shard_map/dot_general | solution.py:20
  527.5 16.9 %fusion.1 = bf16[1152,4608]{1,0:T(8,128)(2,1)} fusion(f32[1152,4608]{1,0:T(8,128)} %fusion.168, bf16[640,4608]{1,0:T(8,128)(2,1)} %bitcast.24, pred[1152,1280]{1,0:T(32,128)(4,1)} %iota_compare_fusion), kind=kOutput, calls=%fused_computation.5 | convolution fusion | flops 6805389312 | bytes 38486016 | tf_op jit(solution)/shard_map/dot_general | solution.py:20
  544.4 14.7 fusion.172
  560.3 8.5 fusion.24
  613.9 16.9 %fusion.2 = bf16[1152,4608]{1,0:T(8,128)(2,1)} fusion(f32[1152,4608]{1,0:T(8,128)} %fusion.172, bf16[640,4608]{1,0:T(8,128)(2,1)} %bitcast.657, pred[1152,1280]{1,0:T(32,128)(4,1)} %iota_compare_fusion.1), kind=kOutput, calls=%fused_computation.6 | convolution fusion | flops 6805389312 | bytes 38486016 | tf_op jit(solution)/shard_map/dot_general | solution.py:20
  657.8 8.7 fusion.332
  666.6 18.0 %convert_reduce_fusion = (f32[4608]{0:T(1024)S(1)}, bf16[512,4608]{1,0:T(8,128)(2,1)}, bf16[512,4608]{1,0:T(8,128)(2,1)}) fusion(f32[512,4608]{1,0:T(8,128)} %fusion.332, f32[4608]{0:T(1024)S(1)} %copy-done.96, bf16[512,1152]{1,0:T(8,128)(2,1)S(1)} %bitcast.631, bf16[4608,1152]{1,0:T(8,128)(2,1)} %bitcast.600), kind=kOutput, calls=%fused_computation.25 | convolution fusion | flops 5494795776 | bytes 30707712 | tf_op jit(solution)/shard_map/dot_general | solution.py:29
  684.6 13.2 multiply_reduce_fusion.5
  697.9 11.1 fusion.136
  820.0 10.3 fusion.82
  852.9 13.4 convolution_convert_fusion.2
  866.3 8.2 pad_maximum_fusion.3
  916.3 9.5 fusion.133
  965.2 105.0 %all-reduce.11.cloned.1.call-done = f32[4,20,1152]{2,1,0:T(8,128)} async-done(((f32[4,20,1152]{2,1,0:T(8,128)}), f32[4,20,1152]{2,1,0:T(8,128)}) %all-reduce.11.cloned.1.call-update) | async-done | bytes 368656 | tf_op jit(solution)/shard_map/psum | solution.py:792
  1081.4 11.1 convolution_convert_fusion.4
  1093.1 13.8 convolution_convert_fusion.3
  1111.7 8.9 copy.233
  1127.5 17.4 %convolution_convert_fusion = bf16[1280,2304]{1,0:T(8,128)(2,1)} fusion(bf16[512,4608]{1,0:T(8,128)(2,1)} %get-tuple-element.82, bf16[512,4608]{1,0:T(8,128)(2,1)} %collective-permute-done.62, pred[]{:T(512)S(6)} %eq.122, s32[1280]{0:T(1024)S(1)} %copy-done.94, bf16[512,1152]{1,0:T(8,128)(2,1)} %collective-permute-done.61, bf16[512,1152]{1,0:T(8,128)(2,1)S(1)} %copy-done.68), kind=kOutput, calls=%fused_computation.10 | convolution fusion | flops 9091383296 | bytes 17699840 | tf_op jit(solution)/shard_map/dot_general | solution.py:692
  1151.5 10.7 fusion.15
  1168.7 13.4 convolution_convert_fusion.5
  1182.2 12.9 convolution_convert_fusion.6
  1207.5 8.8 copy.222
  1216.9 19.0 %collective-permute-done.58 = bf16[2,40,2304]{2,1,0:T(8,128)(2,1)} collective-permute-done((bf16[2,40,2304]{2,1,0:T(8,128)(2,1)}, bf16[2,40,2304]{2,1,0:T(8,128)(2,1)}, u32[]{:S(2)}, u32[]{:S(2)}) %collective-permute-start.58) | collective-permute-done | bytes 368672 | tf_op jit(solution)/shard_map/ppermute | solution.py:518
  1253.7 58.2 %collective-permute-done.71 = bf16[4,2,2,144,640]{4,3,2,1,0:T(8,128)(2,1)} collective-permute-done((bf16[4,2,2,144,640]{4,3,2,1,0:T(8,128)(2,1)}, bf16[4,2,2,144,640]{4,3,2,1,0:T(8,128)(2,1)}, u32[]{:S(2)}, u32[]{:S(2)}) %collective-permute-start.71) | collective-permute-done | bytes 2949152 | tf_op jit(solution)/shard_map/ppermute | solution.py:514
  1315.8 58.7 %collective-permute-done.63 = bf16[2,2,4,40,2304]{4,3,0,2,1:T(8,128)(2,1)S(1)} collective-permute-done((bf16[2,2,4,40,2304]{4,3,0,2,1:T(8,128)(2,1)}, bf16[2,2,4,40,2304]{4,3,0,2,1:T(8,128)(2,1)S(1)}, u32[]{:S(2)}, u32[]{:S(2)}) %collective-permute-start.63) | collective-permute-done | bytes 2949152 | tf_op jit(solution)/shard_map/ppermute | solution.py:514
  1386.9 22.1 %collective-permute-done.64 = bf16[2,4,40,2304]{3,2,0,1:T(8,128)(2,1)S(1)} collective-permute-done((bf16[2,4,40,2304]{3,2,0,1:T(8,128)(2,1)S(1)}, bf16[2,4,40,2304]{3,2,0,1:T(8,128)(2,1)S(1)}, u32[]{:S(2)}, u32[]{:S(2)}) %collective-permute-start.64) | collective-permute-done | bytes 1474592 | tf_op jit(solution)/shard_map/ppermute | solution.py:514
  1413.1 12.1 collective-permute-done.47
  1431.0 21.2 %collective-permute-start.74 = (bf16[2,144,640]{2,1,0:T(8,128)(2,1)S(1)}, bf16[2,144,640]{2,1,0:T(8,128)(2,1)S(1)}, u32[]{:S(2)}, u32[]{:S(2)}) collective-permute-start(bf16[2,144,640]{2,1,0:T(8,128)(2,1)S(1)} %get-tuple-element.120), channel_id=1, source_target_pairs={{0,16},{8,24},{16,0},{24,8},{1,17},{9,25},{17,1},{25,9},{2,18},{10... | collective-permute-start | bytes 1105928 | tf_op jit(solution)/shard_map/ppermute | solution.py:518
  1452.2 12.6 collective-permute-done.66
  1483.1 8.0 collective-permute-done.36
  1491.1 22.8 %collective-permute-done.37 = bf16[2,40,2304]{2,1,0:T(8,128)(2,1)S(1)} collective-permute-done((bf16[2,40,2304]{2,1,0:T(8,128)(2,1)S(1)}, bf16[2,40,2304]{2,1,0:T(8,128)(2,1)S(1)}, u32[]{:S(2)}, u32[]{:S(2)}) %collective-permute-start.37) | collective-permute-done | bytes 368672 | tf_op jit(solution)/shard_map/ppermute | solution.py:518
  (700 shorter events, 562.3 us)
Async XLA Ops:
  7.2 303.3 %all-reduce.9.cloned.1.call-start = ((), (), s32[]{:S(2)}) async-start(), calls=%async_computation.5 | async-start | bytes 405504 | tf_op jit(solution)/shard_map/psum | solution.py:638
  15.4 46.5 %collective-permute-start.18 = (bf16[1,40,4608]{2,1,0:T(8,128)(2,1)S(1)}, bf16[1,40,4608]{2,1,0:T(8,128)(2,1)S(1)}, u32[]{:S(2)}, u32[]{:S(2)}) collective-permute-start(bf16[1,40,4608]{2,1,0:T(8,128)(2,1)S(1)} %pad_bitcast_fusion), channel_id=1, source_target_pairs={{0,8},{8,16},{16,24},{24,0},{1,9},{9,17},{17,25},{25,1},{2,10},{10... | collective-permute-start | bytes 1105928 | tf_op jit(solution)/shard_map/ppermute | solution.py:518
  16.1 66.3 %collective-permute-start.19 = (bf16[1,40,4608]{2,1,0:T(8,128)(2,1)S(1)}, bf16[1,40,4608]{2,1,0:T(8,128)(2,1)S(1)}, u32[]{:S(2)}, u32[]{:S(2)}) collective-permute-start(bf16[1,40,4608]{2,1,0:T(8,128)(2,1)S(1)} %pad_bitcast_fusion), channel_id=1, source_target_pairs={{0,16},{8,24},{16,0},{24,8},{1,17},{9,25},{17,1},{25,9},{2,18},{10... | collective-permute-start | bytes 1105928 | tf_op jit(solution)/shard_map/ppermute | solution.py:518
  29.7 60.6 %collective-permute-start.20 = (bf16[1,40,4608]{2,1,0:T(8,128)(2,1)S(1)}, bf16[1,40,4608]{2,1,0:T(8,128)(2,1)S(1)}, u32[]{:S(2)}, u32[]{:S(2)}) collective-permute-start(bf16[1,40,4608]{2,1,0:T(8,128)(2,1)S(1)} %pad_bitcast_fusion), channel_id=1, source_target_pairs={{0,24},{8,0},{16,8},{24,16},{1,25},{9,1},{17,9},{25,17},{2,26},{10... | collective-permute-start | bytes 1105928 | tf_op jit(solution)/shard_map/ppermute | solution.py:518
  38.2 55.6 %collective-permute-start.12 = (bf16[1,40,4608]{2,1,0:T(8,128)(2,1)}, bf16[1,40,4608]{2,1,0:T(8,128)(2,1)S(1)}, u32[]{:S(2)}, u32[]{:S(2)}) collective-permute-start(bf16[1,40,4608]{2,1,0:T(8,128)(2,1)} %fusion.248), channel_id=1, source_target_pairs={{0,8},{8,16},{16,24},{24,0},{1,9},{9,17},{17,25},{25,1},{2,10},{10... | collective-permute-start | bytes 1105928 | tf_op jit(solution)/shard_map/ppermute | solution.py:518
  43.1 71.5 %collective-permute-start.13 = (bf16[1,40,4608]{2,1,0:T(8,128)(2,1)}, bf16[1,40,4608]{2,1,0:T(8,128)(2,1)S(1)}, u32[]{:S(2)}, u32[]{:S(2)}) collective-permute-start(bf16[1,40,4608]{2,1,0:T(8,128)(2,1)} %fusion.248), channel_id=1, source_target_pairs={{0,16},{8,24},{16,0},{24,8},{1,17},{9,25},{17,1},{25,9},{2,18},{10... | collective-permute-start | bytes 1105928 | tf_op jit(solution)/shard_map/ppermute | solution.py:518
  61.9 60.6 %collective-permute-start.14 = (bf16[1,40,4608]{2,1,0:T(8,128)(2,1)}, bf16[1,40,4608]{2,1,0:T(8,128)(2,1)S(1)}, u32[]{:S(2)}, u32[]{:S(2)}) collective-permute-start(bf16[1,40,4608]{2,1,0:T(8,128)(2,1)} %fusion.248), channel_id=1, source_target_pairs={{0,24},{8,0},{16,8},{24,16},{1,25},{9,1},{17,9},{25,17},{2,26},{10... | collective-permute-start | bytes 1105928 | tf_op jit(solution)/shard_map/ppermute | solution.py:518
  90.3 56.4 %collective-permute-start.7 = (bf16[1,40,4608]{2,1,0:T(8,128)(2,1)S(1)}, bf16[1,40,4608]{2,1,0:T(8,128)(2,1)S(1)}, u32[]{:S(2)}, u32[]{:S(2)}) collective-permute-start(bf16[1,40,4608]{2,1,0:T(8,128)(2,1)S(1)} %copy-done.63), channel_id=1, source_target_pairs={{0,16},{8,24},{16,0},{24,8},{1,17},{9,25},{17,1},{25,9},{2,18},{10... | collective-permute-start | bytes 1105928 | tf_op jit(solution)/shard_map/ppermute | solution.py:518
  93.9 54.4 %collective-permute-start.8 = (bf16[1,40,4608]{2,1,0:T(8,128)(2,1)S(1)}, bf16[1,40,4608]{2,1,0:T(8,128)(2,1)S(1)}, u32[]{:S(2)}, u32[]{:S(2)}) collective-permute-start(bf16[1,40,4608]{2,1,0:T(8,128)(2,1)S(1)} %copy-done.63), channel_id=1, source_target_pairs={{0,24},{8,0},{16,8},{24,16},{1,25},{9,1},{17,9},{25,17},{2,26},{10... | collective-permute-start | bytes 1105928 | tf_op jit(solution)/shard_map/ppermute | solution.py:518
  148.2 71.7 %collective-permute-start.21 = (bf16[4,40,4608]{2,1,0:T(8,128)(2,1)S(1)}, bf16[4,40,4608]{2,1,0:T(8,128)(2,1)S(1)}, u32[]{:S(2)}, u32[]{:S(2)}) collective-permute-start(bf16[4,40,4608]{2,1,0:T(8,128)(2,1)S(1)} %pad_maximum_fusion.23), channel_id=1, source_target_pairs={{0,4},{1,5},{2,6},{3,7},{4,0},{5,1},{6,2},{7,3},{8,12},{9,13},{10,... | collective-permute-start | bytes 4423688 | tf_op jit(solution)/shard_map/ppermute | solution.py:514
  148.9 129.2 %collective-permute-start.15 = (bf16[4,40,4608]{2,1,0:T(8,128)(2,1)S(1)}, bf16[4,40,4608]{2,1,0:T(8,128)(2,1)S(1)}, u32[]{:S(2)}, u32[]{:S(2)}) collective-permute-start(bf16[4,40,4608]{2,1,0:T(8,128)(2,1)S(1)} %pad_maximum_fusion.22), channel_id=1, source_target_pairs={{0,2},{1,3},{2,0},{3,1},{4,6},{5,7},{6,4},{7,5},{8,10},{9,11},{10,... | collective-permute-start | bytes 4423688 | tf_op jit(solution)/shard_map/ppermute | solution.py:514
  162.7 118.8 %collective-permute-start.9 = (bf16[4,40,4608]{2,1,0:T(8,128)(2,1)S(1)}, bf16[4,40,4608]{2,1,0:T(8,128)(2,1)S(1)}, u32[]{:S(2)}, u32[]{:S(2)}) collective-permute-start(bf16[4,40,4608]{2,1,0:T(8,128)(2,1)S(1)} %pad_maximum_fusion.21), channel_id=1, source_target_pairs={{0,4},{1,5},{2,6},{3,7},{4,0},{5,1},{6,2},{7,3},{8,12},{9,13},{10,... | collective-permute-start | bytes 4423688 | tf_op jit(solution)/shard_map/ppermute | solution.py:514
  164.4 52.1 %collective-permute-start.3 = (bf16[4,40,4608]{2,1,0:T(8,128)(2,1)S(1)}, bf16[4,40,4608]{2,1,0:T(8,128)(2,1)S(1)}, u32[]{:S(2)}, u32[]{:S(2)}) collective-permute-start(bf16[4,40,4608]{2,1,0:T(8,128)(2,1)S(1)} %pad_maximum_fusion.20), channel_id=1, source_target_pairs={{0,2},{1,3},{2,0},{3,1},{4,6},{5,7},{6,4},{7,5},{8,10},{9,11},{10,... | collective-permute-start | bytes 4423688 | tf_op jit(solution)/shard_map/ppermute | solution.py:514
  179.6 93.8 %collective-permute-start.28 = (bf16[4,2,144,1152]{3,2,1,0:T(8,128)(2,1)S(1)}, bf16[4,2,144,1152]{3,2,1,0:T(8,128)(2,1)S(1)}, u32[]{:S(2)}, u32[]{:S(2)}) collective-permute-start(bf16[4,2,144,1152]{3,2,1,0:T(8,128)(2,1)S(1)} %maximum_bitcast_fusion), channel_id=1, source_target_pairs={{0,2},{1,3},{2,0},{3,1},{4,6},{5,7},{6,4},{7,5},{8,10},{9,11},{10,... | collective-permute-start | bytes 7962632 | tf_op jit(solution)/shard_map/ppermute | solution.py:514
  218.4 87.4 %collective-permute-start.4 = (bf16[8,40,4608]{2,1,0:T(8,128)(2,1)}, bf16[8,40,4608]{2,1,0:T(8,128)(2,1)S(1)}, u32[]{:S(2)}, u32[]{:S(2)}) collective-permute-start(bf16[8,40,4608]{2,1,0:T(8,128)(2,1)} %get-tuple-element.139), channel_id=1, source_target_pairs={{0,4},{1,5},{2,6},{3,7},{4,0},{5,1},{6,2},{7,3},{8,12},{9,13},{10,... | collective-permute-start | bytes 8847368 | tf_op jit(solution)/shard_map/ppermute | solution.py:514
  221.8 115.0 %collective-permute-start.22 = (bf16[8,40,4608]{2,1,0:T(8,128)(2,1)}, bf16[8,40,4608]{2,1,0:T(8,128)(2,1)}, u32[]{:S(2)}, u32[]{:S(2)}) collective-permute-start(bf16[8,40,4608]{2,1,0:T(8,128)(2,1)} %get-tuple-element.133), channel_id=1, source_target_pairs={{0,2},{1,3},{2,0},{3,1},{4,6},{5,7},{6,4},{7,5},{8,10},{9,11},{10,... | collective-permute-start | bytes 8847368 | tf_op jit(solution)/shard_map/ppermute | solution.py:514
  278.1 123.9 %collective-permute-start.29 = (bf16[4,2,2,144,1152]{4,3,2,1,0:T(8,128)(2,1)}, bf16[4,2,2,144,1152]{4,3,2,1,0:T(8,128)(2,1)}, u32[]{:S(2)}, u32[]{:S(2)}) collective-permute-start(bf16[4,2,2,144,1152]{4,3,2,1,0:T(8,128)(2,1)} %pad_maximum_fusion.5), channel_id=1, source_target_pairs={{0,1},{1,0},{2,3},{3,2},{4,5},{5,4},{6,7},{7,6},{8,9},{9,8},{10,11... | collective-permute-start | bytes 15925256 | tf_op jit(solution)/shard_map/ppermute | solution.py:514
  280.0 88.1 %collective-permute-start.16 = (bf16[8,40,4608]{2,1,0:T(8,128)(2,1)}, bf16[8,40,4608]{2,1,0:T(8,128)(2,1)}, u32[]{:S(2)}, u32[]{:S(2)}) collective-permute-start(bf16[8,40,4608]{2,1,0:T(8,128)(2,1)} %get-tuple-element.135), channel_id=1, source_target_pairs={{0,4},{1,5},{2,6},{3,7},{4,0},{5,1},{6,2},{7,3},{8,12},{9,13},{10,... | collective-permute-start | bytes 8847368 | tf_op jit(solution)/shard_map/ppermute | solution.py:514
  283.4 114.9 %collective-permute-start.10 = (bf16[8,40,4608]{2,1,0:T(8,128)(2,1)}, bf16[8,40,4608]{2,1,0:T(8,128)(2,1)}, u32[]{:S(2)}, u32[]{:S(2)}) collective-permute-start(bf16[8,40,4608]{2,1,0:T(8,128)(2,1)} %get-tuple-element.137), channel_id=1, source_target_pairs={{0,2},{1,3},{2,0},{3,1},{4,6},{5,7},{6,4},{7,5},{8,10},{9,11},{10,... | collective-permute-start | bytes 8847368 | tf_op jit(solution)/shard_map/ppermute | solution.py:514
  307.6 103.7 %collective-permute-start.5 = (bf16[16,40,4608]{2,1,0:T(8,128)(2,1)}, bf16[16,40,4608]{2,1,0:T(8,128)(2,1)}, u32[]{:S(2)}, u32[]{:S(2)}) collective-permute-start(bf16[16,40,4608]{2,1,0:T(8,128)(2,1)} %constant_dynamic-update-slice_fusion.5), channel_id=1, source_target_pairs={{0,1},{1,0},{2,3},{3,2},{4,5},{5,4},{6,7},{7,6},{8,9},{9,8},{10,11... | collective-permute-start | bytes 17694728 | tf_op jit(solution)/shard_map/ppermute | solution.py:514
  340.4 139.6 %collective-permute-start.23 = (bf16[16,40,4608]{2,1,0:T(8,128)(2,1)}, bf16[16,40,4608]{2,1,0:T(8,128)(2,1)}, u32[]{:S(2)}, u32[]{:S(2)}) collective-permute-start(bf16[16,40,4608]{2,1,0:T(8,128)(2,1)} %constant_dynamic-update-slice_fusion.38), channel_id=1, source_target_pairs={{0,1},{1,0},{2,3},{3,2},{4,5},{5,4},{6,7},{7,6},{8,9},{9,8},{10,11... | collective-permute-start | bytes 17694728 | tf_op jit(solution)/shard_map/ppermute | solution.py:514
  371.7 172.7 %collective-permute-start.17 = (bf16[16,40,4608]{2,1,0:T(8,128)(2,1)}, bf16[16,40,4608]{2,1,0:T(8,128)(2,1)}, u32[]{:S(2)}, u32[]{:S(2)}) collective-permute-start(bf16[16,40,4608]{2,1,0:T(8,128)(2,1)} %constant_dynamic-update-slice_fusion.27), channel_id=1, source_target_pairs={{0,1},{1,0},{2,3},{3,2},{4,5},{5,4},{6,7},{7,6},{8,9},{9,8},{10,11... | collective-permute-start | bytes 17694728 | tf_op jit(solution)/shard_map/ppermute | solution.py:514
  402.1 93.5 %collective-permute-start.11 = (bf16[16,40,4608]{2,1,0:T(8,128)(2,1)}, bf16[16,40,4608]{2,1,0:T(8,128)(2,1)}, u32[]{:S(2)}, u32[]{:S(2)}) collective-permute-start(bf16[16,40,4608]{2,1,0:T(8,128)(2,1)} %constant_dynamic-update-slice_fusion.16), channel_id=1, source_target_pairs={{0,1},{1,0},{2,3},{3,2},{4,5},{5,4},{6,7},{7,6},{8,9},{9,8},{10,11... | collective-permute-start | bytes 17694728 | tf_op jit(solution)/shard_map/ppermute | solution.py:514
  476.0 83.1 %all-to-all-start = ((bf16[1,2,256,1152]{3,1,0,2:T(2,128)(2,1)}), bf16[1,2,256,1152]{3,1,0,2:T(2,128)(2,1)S(1)}, u32[]{:S(2)}, u32[]{:S(2)}) async-start(bf16[1,2,256,1152]{3,1,0,2:T(2,128)(2,1)} %copy.173), calls=%async_computation | async-start | bytes 2359296 | tf_op jit(solution)/shard_map/all_to_all | solution.py:655
  754.5 411.2 %collective-permute-start.32 = (bf16[512,1152]{1,0:T(8,128)(2,1)}, bf16[512,1152]{1,0:T(8,128)(2,1)}, u32[]{:S(2)}, u32[]{:S(2)}) collective-permute-start(bf16[512,1152]{1,0:T(8,128)(2,1)} %reshape.1428), channel_id=1, source_target_pairs={{0,1},{1,0},{2,3},{3,2},{4,5},{5,4},{6,7},{7,6},{8,9},{9,8},{10,11... | collective-permute-start | bytes 3538952 | tf_op jit(solution)/shard_map/ppermute | solution.py:686
  760.9 91.5 %collective-permute-start.53 = (bf16[512,1152]{1,0:T(8,128)(2,1)}, bf16[512,1152]{1,0:T(8,128)(2,1)}, u32[]{:S(2)}, u32[]{:S(2)}) collective-permute-start(bf16[512,1152]{1,0:T(8,128)(2,1)} %copy-done.65), channel_id=1, source_target_pairs={{0,1},{1,0},{2,3},{3,2},{4,5},{5,4},{6,7},{7,6},{8,9},{9,8},{10,11... | collective-permute-start | bytes 3538952 | tf_op jit(solution)/shard_map/ppermute | solution.py:686
  763.4 89.5 %collective-permute-start.50 = (bf16[512,1152]{1,0:T(8,128)(2,1)}, bf16[512,1152]{1,0:T(8,128)(2,1)}, u32[]{:S(2)}, u32[]{:S(2)}) collective-permute-start(bf16[512,1152]{1,0:T(8,128)(2,1)} %get-tuple-element.92), channel_id=1, source_target_pairs={{0,1},{1,0},{2,3},{3,2},{4,5},{5,4},{6,7},{7,6},{8,9},{9,8},{10,11... | collective-permute-start | bytes 3538952 | tf_op jit(solution)/shard_map/ppermute | solution.py:686
  763.8 88.2 %collective-permute-start.52 = (bf16[512,1152]{1,0:T(8,128)(2,1)}, bf16[512,1152]{1,0:T(8,128)(2,1)}, u32[]{:S(2)}, u32[]{:S(2)}) collective-permute-start(bf16[512,1152]{1,0:T(8,128)(2,1)} %copy.239), channel_id=1, source_target_pairs={{0,1},{1,0},{2,3},{3,2},{4,5},{5,4},{6,7},{7,6},{8,9},{9,8},{10,11... | collective-permute-start | bytes 3538952 | tf_op jit(solution)/shard_map/ppermute | solution.py:686
  767.7 84.8 %collective-permute-start.51 = (bf16[512,1152]{1,0:T(8,128)(2,1)}, bf16[512,1152]{1,0:T(8,128)(2,1)}, u32[]{:S(2)}, u32[]{:S(2)}) collective-permute-start(bf16[512,1152]{1,0:T(8,128)(2,1)} %copy.237), channel_id=1, source_target_pairs={{0,1},{1,0},{2,3},{3,2},{4,5},{5,4},{6,7},{7,6},{8,9},{9,8},{10,11... | collective-permute-start | bytes 3538952 | tf_op jit(solution)/shard_map/ppermute | solution.py:686
  846.7 223.5 %all-reduce.11.cloned.1.call-start = ((), (), s32[]{:S(2)}) async-start(), calls=%async_computation.7 | async-start | bytes 884736 | tf_op jit(solution)/shard_map/psum | solution.py:792
  852.0 228.9 %collective-permute-start.40 = (bf16[512,1152]{1,0:T(8,128)(2,1)}, bf16[512,1152]{1,0:T(8,128)(2,1)}, u32[]{:S(2)}, u32[]{:S(2)}) collective-permute-start(bf16[512,1152]{1,0:T(8,128)(2,1)} %bitcast.137), channel_id=1, source_target_pairs={{0,1},{1,0},{2,3},{3,2},{4,5},{5,4},{6,7},{7,6},{8,9},{9,8},{10,11... | collective-permute-start | bytes 3538952 | tf_op jit(solution)/shard_map/ppermute | solution.py:686
  852.4 240.2 %collective-permute-start.42 = (bf16[512,1152]{1,0:T(8,128)(2,1)}, bf16[512,1152]{1,0:T(8,128)(2,1)}, u32[]{:S(2)}, u32[]{:S(2)}) collective-permute-start(bf16[512,1152]{1,0:T(8,128)(2,1)} %reshape_reshape.10), channel_id=1, source_target_pairs={{0,1},{1,0},{2,3},{3,2},{4,5},{5,4},{6,7},{7,6},{8,9},{9,8},{10,11... | collective-permute-start | bytes 3538952 | tf_op jit(solution)/shard_map/ppermute | solution.py:686
  852.5 228.5 %collective-permute-start.41 = (bf16[512,3456]{1,0:T(8,128)(2,1)}, bf16[512,3456]{1,0:T(8,128)(2,1)}, u32[]{:S(2)}, u32[]{:S(2)}) collective-permute-start(bf16[512,3456]{1,0:T(8,128)(2,1)} %constant_dynamic-update-slice_fusion.47), channel_id=1, source_target_pairs={{0,1},{1,0},{2,3},{3,2},{4,5},{5,4},{6,7},{7,6},{8,9},{9,8},{10,11... | collective-permute-start | bytes 10616840 | tf_op jit(solution)/shard_map/ppermute | solution.py:686
  882.9 191.7 %collective-permute-start.55 = (bf16[2,2,4,40,2304]{4,3,0,2,1:T(8,128)(2,1)}, bf16[2,2,4,40,2304]{4,3,0,2,1:T(8,128)(2,1)}, u32[]{:S(2)}, u32[]{:S(2)}) collective-permute-start(bf16[2,2,4,40,2304]{4,3,0,2,1:T(8,128)(2,1)} %slice_bitcast_fusion.10), channel_id=1, source_target_pairs={{0,4},{1,5},{2,6},{3,7},{4,0},{5,1},{6,2},{7,3},{8,12},{9,13},{10,... | collective-permute-start | bytes 8847368 | tf_op jit(solution)/shard_map/ppermute | solution.py:514
  933.7 587.4 %reduce-scatter.2.cloned.1.call-start = ((), (), s32[]{:S(2)}) async-start(), calls=%async_computation.6 | async-start | bytes 663552 | tf_op jit(solution)/shard_map/reduce_scatter | solution.py:801
  1074.7 75.4 %collective-permute-start.69 = (bf16[512,4608]{1,0:T(8,128)(2,1)}, bf16[512,4608]{1,0:T(8,128)(2,1)}, u32[]{:S(2)}, u32[]{:S(2)}) collective-permute-start(bf16[512,4608]{1,0:T(8,128)(2,1)} %get-tuple-element.96), channel_id=1, source_target_pairs={{0,1},{1,0},{2,3},{3,2},{4,5},{5,4},{6,7},{7,6},{8,9},{9,8},{10,11... | collective-permute-start | bytes 14155784 | tf_op jit(solution)/shard_map/ppermute | solution.py:686
  1080.9 46.2 %collective-permute-start.62 = (bf16[512,4608]{1,0:T(8,128)(2,1)}, bf16[512,4608]{1,0:T(8,128)(2,1)}, u32[]{:S(2)}, u32[]{:S(2)}) collective-permute-start(bf16[512,4608]{1,0:T(8,128)(2,1)} %get-tuple-element.82), channel_id=1, source_target_pairs={{0,1},{1,0},{2,3},{3,2},{4,5},{5,4},{6,7},{7,6},{8,9},{9,8},{10,11... | collective-permute-start | bytes 14155784 | tf_op jit(solution)/shard_map/ppermute | solution.py:686
  1092.7 57.3 %collective-permute-start.70 = (bf16[512,1152]{1,0:T(8,128)(2,1)}, bf16[512,1152]{1,0:T(8,128)(2,1)}, u32[]{:S(2)}, u32[]{:S(2)}) collective-permute-start(bf16[512,1152]{1,0:T(8,128)(2,1)} %get-tuple-element.146), channel_id=1, source_target_pairs={{0,1},{1,0},{2,3},{3,2},{4,5},{5,4},{6,7},{7,6},{8,9},{9,8},{10,11... | collective-permute-start | bytes 3538952 | tf_op jit(solution)/shard_map/ppermute | solution.py:686
  1150.1 45.0 %collective-permute-start.56 = (bf16[2,4,40,2304]{3,2,0,1:T(8,128)(2,1)}, bf16[2,4,40,2304]{3,2,0,1:T(8,128)(2,1)}, u32[]{:S(2)}, u32[]{:S(2)}) collective-permute-start(bf16[2,4,40,2304]{3,2,0,1:T(8,128)(2,1)} %slice_bitcast_fusion.24), channel_id=1, source_target_pairs={{0,2},{1,3},{2,0},{3,1},{4,6},{5,7},{6,4},{7,5},{8,10},{9,11},{10,... | collective-permute-start | bytes 4423688 | tf_op jit(solution)/shard_map/ppermute | solution.py:514
  1165.7 83.0 %collective-permute-start.44 = (bf16[2,2,4,40,2304]{4,3,0,2,1:T(8,128)(2,1)}, bf16[2,2,4,40,2304]{4,3,0,2,1:T(8,128)(2,1)}, u32[]{:S(2)}, u32[]{:S(2)}) collective-permute-start(bf16[2,2,4,40,2304]{4,3,0,2,1:T(8,128)(2,1)} %bitcast.573), channel_id=1, source_target_pairs={{0,2},{1,3},{2,0},{3,1},{4,6},{5,7},{6,4},{7,5},{8,10},{9,11},{10,... | collective-permute-start | bytes 8847368 | tf_op jit(solution)/shard_map/ppermute | solution.py:514
  1167.5 144.4 %collective-permute-start.71 = (bf16[4,2,2,144,640]{4,3,2,1,0:T(8,128)(2,1)}, bf16[4,2,2,144,640]{4,3,2,1,0:T(8,128)(2,1)}, u32[]{:S(2)}, u32[]{:S(2)}) collective-permute-start(bf16[4,2,2,144,640]{4,3,2,1,0:T(8,128)(2,1)} %dynamic-slice_bitcast_fusion), channel_id=1, source_target_pairs={{0,2},{1,3},{2,0},{3,1},{4,6},{5,7},{6,4},{7,5},{8,10},{9,11},{10,... | collective-permute-start | bytes 8847368 | tf_op jit(solution)/shard_map/ppermute | solution.py:514
  1216.4 158.1 %collective-permute-start.63 = (bf16[2,2,4,40,2304]{4,3,0,2,1:T(8,128)(2,1)}, bf16[2,2,4,40,2304]{4,3,0,2,1:T(8,128)(2,1)S(1)}, u32[]{:S(2)}, u32[]{:S(2)}) collective-permute-start(bf16[2,2,4,40,2304]{4,3,0,2,1:T(8,128)(2,1)} %bitcast.621), channel_id=1, source_target_pairs={{0,2},{1,3},{2,0},{3,1},{4,6},{5,7},{6,4},{7,5},{8,10},{9,11},{10,... | collective-permute-start | bytes 8847368 | tf_op jit(solution)/shard_map/ppermute | solution.py:514
  1239.4 137.1 %collective-permute-start.34 = (bf16[2,2,4,40,2304]{4,3,2,1,0:T(8,128)(2,1)S(1)}, bf16[2,2,4,40,2304]{4,3,2,1,0:T(8,128)(2,1)S(1)}, u32[]{:S(2)}, u32[]{:S(2)}) collective-permute-start(bf16[2,2,4,40,2304]{4,3,2,1,0:T(8,128)(2,1)S(1)} %slice_bitcast_fusion.12), channel_id=1, source_target_pairs={{0,4},{1,5},{2,6},{3,7},{4,0},{5,1},{6,2},{7,3},{8,12},{9,13},{10,... | collective-permute-start | bytes 8847368 | tf_op jit(solution)/shard_map/ppermute | solution.py:514
  1252.2 125.7 %collective-permute-start.45 = (bf16[2,4,40,2304]{3,2,0,1:T(8,128)(2,1)}, bf16[2,4,40,2304]{3,2,0,1:T(8,128)(2,1)}, u32[]{:S(2)}, u32[]{:S(2)}) collective-permute-start(bf16[2,4,40,2304]{3,2,0,1:T(8,128)(2,1)} %slice_bitcast_fusion.26), channel_id=1, source_target_pairs={{0,4},{1,5},{2,6},{3,7},{4,0},{5,1},{6,2},{7,3},{8,12},{9,13},{10,... | collective-permute-start | bytes 4423688 | tf_op jit(solution)/shard_map/ppermute | solution.py:514
  1314.3 69.8 %collective-permute-start.72 = (bf16[4,2,144,640]{3,2,1,0:T(8,128)(2,1)S(1)}, bf16[4,2,144,640]{3,2,1,0:T(8,128)(2,1)}, u32[]{:S(2)}, u32[]{:S(2)}) collective-permute-start(bf16[4,2,144,640]{3,2,1,0:T(8,128)(2,1)S(1)} %dynamic-slice_bitcast_fusion.1), channel_id=1, source_target_pairs={{0,4},{1,5},{2,6},{3,7},{4,0},{5,1},{6,2},{7,3},{8,12},{9,13},{10,... | collective-permute-start | bytes 4423688 | tf_op jit(solution)/shard_map/ppermute | solution.py:514
  1377.0 99.5 %collective-permute-start.35 = (bf16[2,4,40,2304]{3,2,1,0:T(8,128)(2,1)S(1)}, bf16[2,4,40,2304]{3,2,1,0:T(8,128)(2,1)S(1)}, u32[]{:S(2)}, u32[]{:S(2)}) collective-permute-start(bf16[2,4,40,2304]{3,2,1,0:T(8,128)(2,1)S(1)} %slice_bitcast_fusion.28), channel_id=1, source_target_pairs={{0,2},{1,3},{2,0},{3,1},{4,6},{5,7},{6,4},{7,5},{8,10},{9,11},{10,... | collective-permute-start | bytes 4423688 | tf_op jit(solution)/shard_map/ppermute | solution.py:514
  1408.9 56.1 %collective-permute-start.73 = (bf16[2,144,640]{2,1,0:T(8,128)(2,1)S(1)}, bf16[2,144,640]{2,1,0:T(8,128)(2,1)S(1)}, u32[]{:S(2)}, u32[]{:S(2)}) collective-permute-start(bf16[2,144,640]{2,1,0:T(8,128)(2,1)S(1)} %get-tuple-element.118), channel_id=1, source_target_pairs={{0,8},{8,16},{16,24},{24,0},{1,9},{9,17},{17,25},{25,1},{2,10},{10... | collective-permute-start | bytes 1105928 | tf_op jit(solution)/shard_map/ppermute | solution.py:518
  1464.8 51.8 %collective-permute-start.49 = (f32[40,2304]{1,0:T(8,128)S(1)}, f32[40,2304]{1,0:T(8,128)S(1)}, u32[]{:S(2)}, u32[]{:S(2)}) collective-permute-start(f32[40,2304]{1,0:T(8,128)S(1)} %slice_bitcast_fusion.42), channel_id=1, source_target_pairs={{0,1},{1,0},{2,3},{3,2},{4,5},{5,4},{6,7},{7,6},{8,9},{9,8},{10,11... | collective-permute-start | bytes 1105928 | tf_op jit(solution)/shard_map/ppermute | solution.py:514
  (171 other events, 2851.9 us)
Sparse Core Ops, SparseCore 0:
  19.4 191.7 all-reduce.8
  933.8 136.3 all-reduce.10
  1074.2 43.6 reduce-scatter.1

commit v2 on v1

--- a/solution.py
+++ b/solution.py
@@ -500,7 +500,6 @@
 ROWS = 36
 PADDED = 40
 HALF = 2304
-ORDERS = ("xy", "yx", "xy", "yx")
 SWAP = {"x": [(i, i ^ 2) for i in range(8)], "y": [(i, i ^ 4) for i in range(8)], "k": [(i, i ^ 1) for i in range(8)]}
 
 
@@ -518,78 +517,195 @@
     return lax.ppermute(arr, "clip", [(i, (i + d) % 4) for i in range(4)])
 
 
-def row_place(order, at):
+class Task:
+    def __init__(self, steps, state):
+        self.steps, self.state, self.at, self.left = steps, state, 0, 0
+
+    def done(self):
+        return self.at == len(self.steps) and not self.left
+
+    def crosses_plane(self):
+        return any(step[0] == "plane" for step in self.steps[self.at :])
+
+
+class Mover:
+    def __init__(self):
+        self.tasks = []
+
+    def add(self, steps, state):
+        self.tasks.append(Task(steps, state))
+        return self.tasks[-1]
+
+    def tick(self, values=()):
+        arrived = []
+        for task in self.tasks:
+            task.left = max(task.left - 1, 0)
+            if task.at and not task.left and not task.tied:
+                arrived.append(task)
+        values, states = lax.optimization_barrier((values, [task.state for task in arrived]))
+        for task, state in zip(arrived, states):
+            task.state, task.tied = state, True
+        busy, turning = False, False
+        for task in self.tasks:
+            if task.at < len(task.steps) and not task.left:
+                kind, ticks, step = task.steps[task.at]
+                if not (kind == "plane" and busy or kind == "z" and turning):
+                    task.state = step(task.state)
+                    task.at, task.left, task.tied = task.at + 1, ticks, False
+            kind = task.steps[task.at - 1][0] if task.left else ""
+            turning = turning or kind == "z"
+            busy = busy or kind == "plane" or task.crosses_plane()
+        return values
+
+    def finish(self, task):
+        while not task.done():
+            self.tick()
+
+    def drain(self):
+        for task in self.tasks:
+            self.finish(task)
+
+
+def row_place(at):
     z, y, x, k = at
-    spots = jnp.arange(2 * 16 * PADDED)
+    spots = jnp.arange(32 * PADDED)
     row, back = spots % PADDED, (spots // PADDED) % 4
-    first, second, core = (spots // (4 * PADDED)) % 2, (spots // (8 * PADDED)) % 2, spots // (16 * PADDED)
-    step_x, step_y = (first, second) if order == "xy" else (second, first)
+    step_x, step_y, core = (spots // (4 * PADDED)) % 2, (spots // (8 * PADDED)) % 2, spots // (16 * PADDED)
     owner = ((z + 4 - back) % 4) * 8 + (y ^ step_y) * 4 + (x ^ step_x) * 2 + (k ^ core)
     source = jnp.where(row < ROWS, owner * ROWS + row, -1)
     return (jnp.arange(32 * ROWS)[:, None] == source[None, :]).astype(jnp.bfloat16)
 
 
-def gather_stage(own, order, place):
-    block = own[None]
-    block = jnp.concatenate([block] + [turn(block, d) for d in (1, 2, 3)], axis=0)
-    for axis in order:
-        block = jnp.concatenate([block, swap(block, axis)], axis=0)
-    other = swap(block, "k")
-    half = place.shape[1] // 2
-    low = product(place[:, :half], block.reshape(half, -1))
-    return (low + product(place[:, half:], other.reshape(half, -1))).astype(jnp.bfloat16)
-
-
-def scatter_stage(total, order, at):
-    k = at[3]
-    block = total.reshape(2, 2, 2, 4, PADDED, HALF)
-    block = block[:, 0] + swap(block[:, 1], order[1])
-    block = block[:, 0] + swap(block[:, 1], order[0])
-    kept = block[:, 0].astype(jnp.float32)
-    for d in (1, 2, 3):
-        kept = kept + turn(block[:, d], 4 - d).astype(jnp.float32)
-    mine, other = kept[0], swap(kept[1], "k")
-    low, high = jnp.where(k == 0, mine, other), jnp.where(k == 0, other, mine)
-    return jnp.concatenate([low, high], axis=1)[:ROWS]
-
-
-def gather_blocks(own, at):
+def along_z(own):
+    return jnp.concatenate([own] + [turn(own, d) for d in (1, 2, 3)], axis=0)
+
+
+def gather_steps():
+    def start(own):
+        parts = [own] + [turn(own, d) for d in (1, 2, 3)]
+        return tuple(
+            jnp.concatenate([part[..., i : i + HALF] for part in parts], axis=0) for i in (0, HALF)
+        )
+
+    def first(state):
+        low, high = state
+        return jnp.concatenate([low, swap(low, "x")], axis=0), high, swap(high, "y")
+
+    def second(state):
+        low, high, beside = state
+        across = swap(jnp.concatenate([high, beside], axis=0), "x")
+        return (
+            jnp.concatenate([low, swap(low, "y")], axis=0),
+            jnp.concatenate([high, across[:4], beside, across[4:]], axis=0),
+        )
+
+    def third(state):
+        low, high = (part.reshape(16 * PADDED, HALF) for part in state)
+        return (low, swap(low, "k")), (high, swap(high, "k"))
+
+    return [("z", 1, start), ("plane", 1, first), ("plane", 2, second), ("core", 1, third)]
+
+
+def gather_out_steps(at):
     z, y, x, k = at
-    block = jnp.stack([own] + [turn(own, d) for d in (1, 2, 3)])
-    block = jnp.stack([lax.dynamic_index_in_dim(block, (z + 4 - i) % 4, 0, keepdims=False) for i in range(4)])
-
-    def both(arr, axis, bit):
+
+    def both(arr, axis, bit, dim):
         other = swap(arr, axis)
-        return jnp.stack([jnp.where(bit == 0, arr, other), jnp.where(bit == 0, other, arr)], axis=-3)
-
-    block = both(both(both(block[:, None], "y", y)[:, 0], "x", x), "k", k)
-    return block.reshape(32 * own.shape[0], own.shape[1])
-
-
-def scatter_blocks(total, at):
+        return jnp.concatenate([jnp.where(bit == 0, arr, other), jnp.where(bit == 0, other, arr)], axis=dim)
+
+    def start(own):
+        block = along_z(own[None])
+        return jnp.concatenate(
+            [lax.dynamic_index_in_dim(block, (z + 4 - i) % 4, 0) for i in range(4)], axis=0
+        ).reshape(4, 1, 1, 1, 144, 1152)
+
+    def first(block):
+        return both(block[..., :72, :], "x", x, 2), both(block[..., 72:, :], "y", y, 1)
+
+    def second(state):
+        return both(state[0], "y", y, 1), both(state[1], "x", x, 2)
+
+    def third(state):
+        low, high = (both(part, "k", k, 3) for part in state)
+        return jnp.concatenate([low, high], axis=4).reshape(32 * 144, 1152)
+
+    return [("z", 1, start), ("plane", 1, first), ("plane", 2, second), ("core", 1, third)]
+
+
+def to_owner(kept, sent, k):
+    other = swap(sent, "k")
+    return jnp.where(k == 0, kept, other), jnp.where(k == 0, other, kept)
+
+
+def scatter_steps(k):
+    def first(state):
+        low, high = (part.reshape(2, 2, 2, 4, PADDED, HALF // 2) for part in state)
+        return low[:, 0] + swap(low[:, 1], "y"), high[:, :, 0] + swap(high[:, :, 1], "x")
+
+    def second(state):
+        low, high = state
+        return jnp.concatenate(
+            [low[:, 0] + swap(low[:, 1], "x"), high[:, 0] + swap(high[:, 1], "y")], axis=-1
+        )
+
+    def third(block):
+        kept = block[:, 0].astype(jnp.float32)
+        for d in (1, 2, 3):
+            kept = kept + turn(block[:, d], 4 - d).astype(jnp.float32)
+        return kept
+
+    def fourth(kept):
+        return jnp.concatenate(to_owner(kept[0], kept[1], k), axis=1)[:ROWS]
+
+    return [("plane", 2, first), ("plane", 1, second), ("z", 2, third), ("core", 1, fourth)]
+
+
+def scatter_out_steps(at):
     z, y, x, k = at
-    block = total.reshape(4, 2, 2, 2, 144, 640)
 
     def halve(arr, axis, name, bit):
         sent = lax.dynamic_index_in_dim(arr, 1 - bit, axis, keepdims=False)
         return lax.dynamic_index_in_dim(arr, bit, axis, keepdims=False) + swap(sent, name)
 
-    block = halve(halve(block, 2, "x", x), 1, "y", y)
-    kept = lax.dynamic_index_in_dim(block, z, 0, keepdims=False).astype(jnp.float32)
-    for d in (1, 2, 3):
-        sent = lax.dynamic_index_in_dim(block, (z + d) % 4, 0, keepdims=False)
-        kept = kept + turn(sent, d).astype(jnp.float32)
-    mine = lax.dynamic_index_in_dim(kept, k, 0, keepdims=False)
-    other = swap(lax.dynamic_index_in_dim(kept, 1 - k, 0, keepdims=False), "k")
-    low, high = jnp.where(k == 0, mine, other), jnp.where(k == 0, other, mine)
-    return jnp.concatenate([low, high[:, 128:]], axis=1)
-
-
-def natural_qkv(inputs, weight, query_bias, value_bias, heads):
-    width = query_bias.shape[0]
-    bias_row = jnp.concatenate([query_bias, jnp.zeros_like(query_bias), value_bias])
-    packed = (product(inputs, weight) + bias_row).astype(jnp.bfloat16)
-    return tuple(split_heads(packed[..., i * width : (i + 1) * width], heads) for i in range(3))
+    def first(total):
+        block = total.reshape(4, 2, 2, 2, 144, 640)
+        return halve(block[..., :384], 1, "y", y), halve(block[..., 384:], 2, "x", x)
+
+    def second(state):
+        return jnp.concatenate([halve(state[0], 1, "x", x), halve(state[1], 1, "y", y)], axis=-1)
+
+    def third(block):
+        kept = lax.dynamic_index_in_dim(block, z, 0, keepdims=False).astype(jnp.float32)
+        for d in (1, 2, 3):
+            sent = lax.dynamic_index_in_dim(block, (z + d) % 4, 0, keepdims=False)
+            kept = kept + turn(sent, d).astype(jnp.float32)
+        return kept
+
+    def fourth(kept):
+        mine = lax.dynamic_index_in_dim(kept, k, 0, keepdims=False)
+        low, high = to_owner(mine, lax.dynamic_index_in_dim(kept, 1 - k, 0, keepdims=False), k)
+        return jnp.concatenate([low, high[:, 128:]], axis=1)
+
+    return [("plane", 2, first), ("plane", 1, second), ("z", 2, third), ("core", 1, fourth)]
+
+
+def sum_over_plane(arr):
+    for axis in ("k", "x", "y"):
+        arr = arr + swap(arr, axis)
+    return arr
+
+
+def packed_product(packed, weight):
+    half = packed.shape[-1] // 2
+    return product(packed[..., :half], weight[0]) + product(packed[..., half:], weight[1])
+
+
+def packed_back(grad_arr, weight):
+    return jnp.concatenate([product_back(grad_arr, part) for part in weight], axis=-1)
+
+
+def columns(weight, first, count):
+    return tuple(part[:, first : first + count] for part in weight)
 
 
 def fast_device(
@@ -613,44 +729,79 @@
     heads = HEADS
     _, frame_count, patch_count, width = tokens.shape
     rows = frame_count * patch_count
-    z, y, x, k = mesh_coords()
+    at = mesh_coords()
+    z, y, x, k = at
     shard = z * 8 + lax.axis_index("seq")
-    pad = ((0, 4), (0, 0))
-    own = [
-        jnp.pad(jnp.concatenate([s_qkv[0], s_proj[0]], axis=1), pad),
-        jnp.pad(jnp.concatenate([t_qkv[0], t_proj[0]], axis=1), pad),
-        jnp.pad(jnp.concatenate([c_query[0], c_kv[0], c_proj[0]], axis=1), pad),
-        jnp.pad(mlp_in[0], pad),
-    ]
-    places = [row_place(order, (z, y, x, k)) for order in ORDERS]
-    stages = [gather_stage(own[i], ORDERS[i], places[i]) for i in range(4)]
-    w_out = gather_blocks(mlp_out[0], (z, y, x, k))
-    w_sqkv, w_sproj = stages[0][:, :3456], stages[0][:, 3456:]
-    w_tqkv, w_tproj = stages[1][:, :3456], stages[1][:, 3456:]
-    w_cquery, w_ckv, w_cproj = stages[2][:, :1152], stages[2][:, 1152:3456], stages[2][:, 3456:]
-    w_in = stages[3]
+    place = row_place(at)
+
+    def packed(arr):
+        return product(arr, place).astype(jnp.bfloat16)
+
+    def unpacked(arr):
+        return lax.dot_general(
+            arr,
+            place,
+            (((arr.ndim - 1,), (1,)), ((), ())),
+            preferred_element_type=jnp.float32,
+        ).astype(jnp.bfloat16)
+
+    def unpacked_float(arr):
+        return lax.dot_general(
+            arr,
+            place.astype(jnp.float32),
+            (((arr.ndim - 1,), (1,)), ((), ())),
+            precision=HIGHEST,
+            preferred_element_type=jnp.float32,
+        )
+
+    def shard_of(*weights):
+        return jnp.pad(jnp.concatenate([w[0] for w in weights], axis=1), ((0, PADDED - ROWS), (0, 0)))[None]
+
+    mover = Mover()
+    s_task = mover.add(gather_steps(), shard_of(s_qkv, s_proj))
+    t_task = mover.add(gather_steps(), shard_of(t_qkv, t_proj))
+    c_task = mover.add(gather_steps(), shard_of(c_query, c_kv, c_proj))
+    i_task = mover.add(gather_steps(), shard_of(mlp_in))
+    o_task = mover.add(gather_out_steps(at), mlp_out[0])
 
     embed = jax.nn.silu(timestep_embed(timesteps, width)).astype(jnp.bfloat16)
     own_embed = lax.dynamic_slice_in_dim(embed, shard * ROWS, ROWS, axis=1)
     mod_part = product(own_embed, time_weight)
     own_vec = jnp.pad(vectors[0].astype(jnp.float32), ((0, 0), (0, width - ROWS)))
-    own_vec = jnp.roll(own_vec, shard * ROWS, axis=1).reshape(4, 5 * width)
-    spread = lax.psum(jnp.concatenate([mod_part, own_vec], axis=1), ("clip", "seq"))
-    modulation = lax.dynamic_slice_in_dim(spread[:, : 6 * width], z, 1, axis=0)
-    modulation = modulation.reshape(1, 6, width)
-    vec_float = spread[:, 6 * width :].reshape(20, width)
+    own_vec = jnp.roll(own_vec, shard * ROWS, axis=1)
+    own_vec = own_vec.reshape(20, width)
+    mod_part = mod_part.reshape(4, 6, width)
+
+    def small_part(d):
+        return jnp.concatenate([lax.dynamic_index_in_dim(mod_part, (z + d) % 4, 0, keepdims=False), own_vec])
+
+    spread = small_part(0)
+    for d in (1, 2, 3):
+        spread = spread + turn(small_part(d), d)
+    spread = sum_over_plane(spread)
+    modulation, vec_float = spread[None, :6], spread[6:]
     hidden = tokens.astype(jnp.float32).reshape(1, rows, width)
     out_rows = out_grad.astype(jnp.float32).reshape(1, rows, width)
     text_mask = (jnp.arange(text.shape[1])[None, :] < text_counts[:, None])[:, None, None, :]
 
+    def split_qkv(inputs_packed, task, query_bias, value_bias):
+        low, high = task.state
+        first = packed_product(inputs_packed, low)
+        value = packed_product(inputs_packed, columns(high, 0, width)) + value_bias
+        parts = (first[..., :width] + query_bias, first[..., width:], value)
+        return tuple(split_heads(part.astype(jnp.bfloat16), heads) for part in parts)
+
     mod_table = modulation + vec_float[10:16][None]
     gate_one, gate_two = mod_table[:, None, 2], mod_table[:, None, 5]
+    mover.finish(s_task)
     normed = modulate(hidden, mod_table[:, 0], mod_table[:, 1]).astype(jnp.bfloat16)
-    frames = normed.reshape(frame_count, patch_count, width)
-    s_parts = natural_qkv(frames, w_sqkv, vec_float[0], vec_float[1], heads)
+    frames = packed(normed.reshape(frame_count, patch_count, width))
+    frames = mover.tick(frames)
+    s_parts = mover.tick(split_qkv(frames, s_task, vec_float[0], vec_float[1]))
     s_mixed, s_total = attend_forward(*s_parts, None, SPATIAL)
-    s_flat = merge_heads(s_mixed)
-    s_branch = (product(s_flat, w_sproj) + vec_float[2]).reshape(1, rows, width)
+    s_flat = mover.tick(packed(merge_heads(s_mixed)))
+    s_high = columns(s_task.state[1], width, width)
+    s_branch = (packed_product(s_flat, s_high) + vec_float[2]).reshape(1, rows, width)
     hidden_one = hidden + gate_one * s_branch
     moved = lax.all_to_all(
         hidden_one.astype(jnp.bfloat16).reshape(1, frame_count, patch_count, width),
@@ -659,31 +810,48 @@
         concat_axis=1,
         tiled=True,
     )
-    t_parts = natural_qkv(moved, w_tqkv, vec_float[3], vec_float[4], heads)
+    moved = mover.tick(packed(moved))
+    mover.finish(t_task)
+    t_parts = mover.tick(split_qkv(moved, t_task, vec_float[3], vec_float[4]))
     t_mixed, t_total = attend_forward(*t_parts, None, TEMPORAL)
-    t_flat = merge_heads(t_mixed)
-    t_branch = (product(t_flat, w_tproj) + vec_float[5]).astype(jnp.bfloat16)
+    t_flat = mover.tick(packed(merge_heads(t_mixed)))
+    t_high = columns(t_task.state[1], width, width)
+    t_branch = (packed_product(t_flat, t_high) + vec_float[5]).astype(jnp.bfloat16)
     t_back = lax.all_to_all(t_branch, "seq", split_axis=1, concat_axis=2, tiled=True).reshape(1, rows, width)
     hidden_two = hidden_one + gate_one * t_back.astype(jnp.float32)
-    cross_in = hidden_two.astype(jnp.bfloat16)
-    c_query_rows = split_heads((product(cross_in, w_cquery) + vec_float[6]).astype(jnp.bfloat16), heads)
-    kv_bias = jnp.concatenate([jnp.zeros_like(vec_float[7]), vec_float[7]])
-    kv_rows = (product(text, w_ckv) + kv_bias).astype(jnp.bfloat16)
-    c_key, c_value = split_heads(kv_rows[..., :width], heads), split_heads(kv_rows[..., width:], heads)
+    cross_in = mover.tick(packed(hidden_two.astype(jnp.bfloat16)))
+    mover.finish(c_task)
+    c_low, c_high = c_task.state
+    w_cquery, w_ckey = columns(c_low, 0, width), columns(c_low, width, width)
+    w_cvalue, w_cproj = columns(c_high, 0, width), columns(c_high, width, width)
+    text_packed = packed(text)
+    c_query_rows = split_heads((packed_product(cross_in, w_cquery) + vec_float[6]).astype(jnp.bfloat16), heads)
+    c_key = split_heads(packed_product(text_packed, w_ckey).astype(jnp.bfloat16), heads)
+    c_value = split_heads((packed_product(text_packed, w_cvalue) + vec_float[7]).astype(jnp.bfloat16), heads)
+    c_query_rows, c_key, c_value = mover.tick((c_query_rows, c_key, c_value))
     c_mixed, c_total = attend_forward(c_query_rows, c_key, c_value, text_mask, CROSS)
-    c_flat = merge_heads(c_mixed)
-    hidden_three = hidden_two + (product(c_flat, w_cproj) + vec_float[8])
-    normed_two = modulate(hidden_three, mod_table[:, 3], mod_table[:, 4]).astype(jnp.bfloat16)
-    inner_act = product(normed_two, w_in) + vec_float[16:].reshape(-1)
-    gelu_out = jax.nn.gelu(inner_act, approximate=True).astype(jnp.bfloat16)
+    c_flat = mover.tick(packed(merge_heads(c_mixed)))
+    hidden_three = hidden_two + (packed_product(c_flat, w_cproj) + vec_float[8])
+    normed_two = packed(modulate(hidden_three, mod_table[:, 3], mod_table[:, 4]).astype(jnp.bfloat16))
+    normed_two = mover.tick(normed_two)
+    mover.finish(i_task)
+    inner_act = jnp.concatenate([packed_product(normed_two, part) for part in i_task.state], axis=-1)
+    inner_act = inner_act + vec_float[16:].reshape(-1)
+    gelu_out = mover.tick(jax.nn.gelu(inner_act, approximate=True).astype(jnp.bfloat16))
+    mover.drain()
+    w_out = o_task.state
     mlp_branch = product(gelu_out, w_out) + vec_float[9]
     hidden_four = hidden_three + gate_two * mlp_branch
 
-    core_swap = [(i, i ^ 1) for i in range(8)]
-
     def pair(arr):
         flat = arr.reshape(-1, arr.shape[-1])
-        return jnp.concatenate([flat, lax.ppermute(flat, "seq", core_swap)], axis=0)
+        return jnp.concatenate([flat, swap(flat, "k")], axis=0)
+
+    def pair_packed(arr):
+        flat = arr.reshape(-1, arr.shape[-1])
+        other = swap(flat, "k")
+        half = flat.shape[1] // 2
+        return jnp.concatenate([flat, jnp.concatenate([other[:, half:], other[:, :half]], axis=1)], axis=0)
 
     def choose(low, high):
         return jnp.where(k == 0, low, high)
@@ -692,84 +860,86 @@
         return lax.dot_general(left, right, (((0,), (0,)), ((), ())), preferred_element_type=jnp.float32).astype(
             jnp.bfloat16
         )
-
-    def packed_rows(arr, stage):
-        return product(arr, places[stage]).astype(jnp.bfloat16)
 
     grad_mlp = (out_rows * gate_two).astype(jnp.bfloat16)
     grad_gate_two = jnp.sum(out_rows * mlp_branch, axis=1)
     pair_mlp = pair(grad_mlp)
     sum_out = sums_of(pair(gelu_out), choose(pair_mlp[:, :640], pair_mlp[:, 512:]))
     bias_out = column_sum(grad_mlp)
-    grad_gelu = product_back(grad_mlp, w_out)
+    grad_gelu, sum_out = lax.optimization_barrier((product_back(grad_mlp, w_out), sum_out))
+    own_out = mover.add(scatter_out_steps(at), sum_out)
     gelu_pull = jax.vjp(partial(jax.nn.gelu, approximate=True), inner_act)[1]
-    grad_inner = gelu_pull(grad_gelu)[0].astype(jnp.bfloat16)
+    grad_inner = mover.tick(gelu_pull(grad_gelu)[0].astype(jnp.bfloat16))
     pair_inner = pair(grad_inner)
-    sum_in = sums_of(packed_rows(pair(normed_two), 3), choose(pair_inner[:, :HALF], pair_inner[:, HALF:]))
+    pair_two, inner_half = pair_packed(normed_two), choose(pair_inner[:, :HALF], pair_inner[:, HALF:])
+    sum_in = (sums_of(pair_two, inner_half[:, :width]), sums_of(pair_two, inner_half[:, width:]))
     bias_in = column_sum(grad_inner)
+    grad_inner, sum_in = mover.tick((grad_inner, sum_in))
+    own_in = mover.add(scatter_steps(k), sum_in)
     norm_pull = jax.vjp(modulate, hidden_three, mod_table[:, 3], mod_table[:, 4])[1]
-    grad_three, grad_shift_two, grad_scale_two = norm_pull(product_back(grad_inner, w_in))
+    in_low, in_high = i_task.state
+    grad_normed = packed_back(grad_inner[..., :HALF], in_low) + packed_back(grad_inner[..., HALF:], in_high)
+    grad_normed = mover.tick(grad_normed)
+    grad_three, grad_shift_two, grad_scale_two = norm_pull(unpacked_float(grad_normed))
     grad_three = out_rows + grad_three
     grad_cross = grad_three.astype(jnp.bfloat16)
     bias_cproj = column_sum(grad_cross)
-    grad_cmixed = split_heads(product_back(grad_cross, w_cproj).astype(jnp.bfloat16), heads)
+    grad_cmixed = unpacked(packed_back(grad_cross, w_cproj).astype(jnp.bfloat16))
+    grad_cmixed = mover.tick(split_heads(grad_cmixed, heads))
     cq_grad, ck_grad, cv_grad = attend_backward(
         c_query_rows, c_key, c_value, text_mask, c_total, grad_cmixed, CROSS
     )
     grad_cquery = merge_heads(cq_grad).astype(jnp.bfloat16)
+    grad_key, grad_value = merge_heads(ck_grad).astype(jnp.bfloat16), merge_heads(cv_grad).astype(jnp.bfloat16)
+    grad_cquery, grad_key, grad_value = mover.tick((grad_cquery, grad_key, grad_value))
     bias_cquery = column_sum(grad_cquery)
-    grad_two = grad_three + product_back(grad_cquery, w_cquery)
-    grad_kv = jnp.concatenate([merge_heads(ck_grad), merge_heads(cv_grad)], axis=-1).astype(jnp.bfloat16)
-    bias_cvalue = column_sum(grad_kv[..., width:])
-    text_part = product_back(grad_kv, w_ckv)
-    pair_kv = pair(grad_kv)
-    text_two = jnp.concatenate([text[0], text[0]], axis=0)
-    sum_kv = sums_of(packed_rows(text_two, 2), choose(pair_kv[:, :width], pair_kv[:, width:]))
-    sum_side = sums_of(packed_rows(choose(pair(cross_in), pair(c_flat)), 2), choose(pair(grad_cquery), pair(grad_cross)))
-    sum_cross = choose(jnp.concatenate([sum_side, sum_kv], 1), jnp.concatenate([sum_kv, sum_side], 1))
-
+    grad_two = grad_three + unpacked_float(packed_back(grad_cquery, w_cquery))
+    bias_cvalue = column_sum(grad_value)
+    text_part = unpacked_float(packed_back(grad_key, w_ckey) + packed_back(grad_value, w_cvalue))
+    text_two = jnp.concatenate([text_packed[0], text_packed[0]], axis=0)
+    sum_kv = sums_of(text_two, choose(pair(grad_key), pair(grad_value)))
+    sum_side = sums_of(choose(pair_packed(cross_in), pair_packed(c_flat)), choose(pair(grad_cquery), pair(grad_cross)))
+    sum_cross = (choose(sum_side, sum_kv), choose(sum_kv, sum_side))
+    grad_temporal = (grad_two * gate_one).astype(jnp.bfloat16).reshape(1, frame_count, patch_count, width)
+    grad_temporal, sum_cross = mover.tick((grad_temporal, sum_cross))
+    own_cross = mover.add(scatter_steps(k), sum_cross)
     grad_gate_one = jnp.sum(grad_two * t_back.astype(jnp.float32), axis=1)
-    grad_temporal = (grad_two * gate_one).astype(jnp.bfloat16).reshape(1, frame_count, patch_count, width)
     grad_places = lax.all_to_all(grad_temporal, "seq", split_axis=2, concat_axis=1, tiled=True)
     bias_tproj = column_sum(grad_places)
-    grad_tmixed = split_heads(product_back(grad_places, w_tproj).astype(jnp.bfloat16), heads)
-
-    def stage_sums(grads, inputs, flat, proj_grad, weight, stage):
-        packed_grad = jnp.concatenate([merge_heads(part) for part in grads], axis=-1).astype(jnp.bfloat16)
-        pair_grad, pair_in = pair(packed_grad), pair(inputs)
-        low = sums_of(packed_rows(pair_in, stage), choose(pair_grad[:, :width], pair_grad[:, 2 * width :]))
-        high = sums_of(
-            packed_rows(choose(pair_in, pair(flat)), stage), choose(pair_grad[:, width : 2 * width], pair(proj_grad))
-        )
-        return (
-            jnp.concatenate([low, high], axis=1),
-            product_back(packed_grad, weight),
-            column_sum(packed_grad[..., :width]),
-            column_sum(packed_grad[..., 2 * width :]),
-        )
+    grad_tmixed = unpacked(packed_back(grad_places, t_high).astype(jnp.bfloat16))
+    grad_tmixed = mover.tick(split_heads(grad_tmixed, heads))
+
+    def stage_sums(grads, inputs, flat, proj_grad, task):
+        query, key, value = mover.tick(tuple(merge_heads(part).astype(jnp.bfloat16) for part in grads))
+        pair_in = pair_packed(inputs)
+        low = sums_of(pair_in, choose(pair(query), pair(value)))
+        high = sums_of(choose(pair_in, pair_packed(flat)), choose(pair(key), pair(proj_grad)))
+        query, key, value, low, high = lax.optimization_barrier((query, key, value, low, high))
+        owned = mover.add(scatter_steps(k), (low, high))
+        mover.tick()
+        w_low, w_high = task.state
+        back = packed_back(jnp.concatenate([query, key], axis=-1), w_low)
+        back = back + packed_back(value, columns(w_high, 0, width))
+        return owned, back, column_sum(query), column_sum(value)
 
     t_grads = attend_backward(*t_parts, None, t_total, grad_tmixed, TEMPORAL)
-    sum_t, grad_moved, bias_tquery, bias_tvalue = stage_sums(t_grads, moved, t_flat, grad_places, w_tqkv, 1)
-    grad_frames = lax.all_to_all(
-        grad_moved.astype(jnp.bfloat16), "seq", split_axis=1, concat_axis=2, tiled=True
-    )
+    own_t, grad_moved, bias_tquery, bias_tvalue = stage_sums(t_grads, moved, t_flat, grad_places, t_task)
+    grad_moved = unpacked(grad_moved.astype(jnp.bfloat16))
+    grad_moved = mover.tick(grad_moved)
+    grad_frames = lax.all_to_all(grad_moved, "seq", split_axis=1, concat_axis=2, tiled=True)
     grad_one = grad_two + grad_frames.astype(jnp.float32).reshape(1, rows, width)
     grad_gate_one = grad_gate_one + jnp.sum(grad_one * s_branch, axis=1)
     grad_spatial = (grad_one * gate_one).astype(jnp.bfloat16).reshape(frame_count, patch_count, width)
     bias_sproj = column_sum(grad_spatial)
-    grad_smixed = split_heads(product_back(grad_spatial, w_sproj).astype(jnp.bfloat16), heads)
+    grad_smixed = unpacked(packed_back(grad_spatial, s_high).astype(jnp.bfloat16))
+    grad_smixed = mover.tick(split_heads(grad_smixed, heads))
     s_grads = attend_backward(*s_parts, None, s_total, grad_smixed, SPATIAL)
-    sum_s, grad_normed, bias_squery, bias_svalue = stage_sums(s_grads, frames, s_flat, grad_spatial, w_sqkv, 0)
+    own_s, grad_normed, bias_squery, bias_svalue = stage_sums(s_grads, frames, s_flat, grad_spatial, s_task)
+    grad_normed = mover.tick(grad_normed)
     first_pull = jax.vjp(modulate, hidden, mod_table[:, 0], mod_table[:, 1])[1]
+    grad_normed = mover.tick(unpacked_float(grad_normed))
     grad_zero, grad_shift_one, grad_scale_one = first_pull(grad_normed.reshape(1, rows, width))
     grad_input = grad_one + grad_zero
-
-    own_s, own_t, own_c, own_in = [
-        scatter_stage(total, ORDERS[i], (z, y, x, k))
-        for i, total in enumerate([sum_s, sum_t, sum_cross, sum_in])
-    ]
-    own_out = scatter_blocks(sum_out, (z, y, x, k))
-
     grad_table = jnp.stack(
         [grad_shift_one, grad_scale_one, grad_gate_one, grad_shift_two, grad_scale_two, grad_gate_two], axis=1
     )[0]
@@ -788,31 +958,33 @@
         ]
     )
     small = jnp.concatenate([bias_rows, grad_table, bias_in.reshape(4, width)], axis=0)
-    own_clip = (jnp.arange(4) == z).astype(jnp.float32)[:, None, None]
-    small = lax.psum(own_clip * small[None], ("clip", "seq"))
+    small = along_z(sum_over_plane(small)[None])
     vec_grad = lax.dynamic_slice_in_dim(jnp.sum(small, axis=0), shard * ROWS, ROWS, axis=1)
+    turned = jnp.stack([lax.dynamic_slice_in_dim(own_embed, (z + 4 - d) % 4, 1, axis=0)[0] for d in range(4)])
     time_grad = lax.dot_general(
-        own_embed.astype(jnp.float32),
+        turned.astype(jnp.float32),
         small[:, 10:16].reshape(4, 6 * width),
         (((0,), (0,)), ((), ())),
         precision=HIGHEST,
         preferred_element_type=jnp.float32,
     )
     text_grad = lax.psum_scatter(text_part, "seq", scatter_dimension=2, tiled=True)
+    mover.drain()
+    grad_s, grad_t, grad_c = own_s.state[None], own_t.state[None], own_cross.state[None]
     return (
         hidden_four.reshape(tokens.shape),
         grad_input.reshape(tokens.shape),
         text_grad,
         time_grad,
-        own_s[None, :, :3456],
-        own_s[None, :, 3456:],
-        own_t[None, :, :3456],
-        own_t[None, :, 3456:],
-        own_c[None, :, :1152],
-        own_c[None, :, 1152:3456],
-        own_c[None, :, 3456:],
-        own_in[None],
-        own_out[None],
+        grad_s[..., :3456],
+        grad_s[..., 3456:],
+        grad_t[..., :3456],
+        grad_t[..., 3456:],
+        grad_c[..., :1152],
+        grad_c[..., 1152:3456],
+        grad_c[..., 3456:],
+        own_in.state[None],
+        own_out.state[None],
         vec_grad[None],
     )
 

time: 1540 us -> 1250 us (0.81)
  waiting for transfers between devices: 600 us -> 396 us
  matrix products: 416 us -> 315 us
  local copies, waits for them, and re-layouts: 248 us -> 192 us
  other arithmetic: 98 us -> 146 us
  starting transfers between devices: 149 us -> 172 us
    ppermute x30 -> x83, waiting for transfers between devices: 327 us -> 209 us  [swap(): return lax.ppermute(arr, 'seq', SWAP[axis])]
    psum x2 -> x0, waiting for transfers between devices: 105 us -> none  [the longest x1 105 us: fast_device(): small = lax.psum(own_clip * small[None], ('clip', 'seq'))]
    concatenate x27 -> x1, local copies, waits for them, and re-layouts: 89.9 us -> 1.01 us  [along_z(): return jnp.concatenate([own] + [turn(own, d) for d in (1, 2, 3)], axis=0)]
    dot_general x18 -> x34, matrix products: 189 us -> 100 us  [product(): lax.dot_general(left_arr, right_arr, (((left_arr.ndim - 1,), (0,)), ((),...]
    another operation x13 -> x1, local copies, waits for them, and re-layouts: 44.9 us -> 4.99 us
    dot_general x8 -> x9, matrix products: 96.7 us -> 58.4 us  [sums_of(): lax.dot_general(left, right, (((0,), (0,)), ((), ())), preferred_element_...]
    dot_general x1 -> x9, matrix products: 1.74 us -> 39.7 us  [the longest x4 26 us: unpacked_float(): lax.dot_general(arr, place.astype(jnp.float32), (((arr.ndim - 1,), (1,)),...]
    ppermute x30 -> x83, starting transfers between devices: 27.6 us -> 61.1 us  [swap(): return lax.ppermute(arr, 'seq', SWAP[axis])]
  transfers between devices with their start and end apart: 84 -> 124, of which waited for: 25 -> 42; matrix products, arithmetic and copies ran while one was open for 40% -> 48% of each run, Pallas kernels for 0% -> 0%
where the time goes in v2:
time: 1250 us; the launch traced here: 1240 us
  waiting for transfers between devices  396 us (32%)
  matrix products  315 us (25%)
  local copies, waits for them, and re-layouts  192 us (15%)
  starting transfers between devices  172 us (14%)
  other arithmetic  146 us (12%)
  between operations  19 us (2%)
    ppermute x83, waiting for transfers between devices, swap(): return lax.ppermute(arr, 'seq', SWAP[axis])  209 us
    ppermute x36, waiting for transfers between devices, turn(): return lax.ppermute(arr, 'clip', [(i, (i + d) % 4) for i in range(4)])  143 us
    dot_general x34, matrix products, product(): lax.dot_general(left_arr, right_arr, (((left_arr.ndim - 1,), (0,)), ((),...  100 us
    ppermute x36, starting transfers between devices, turn(): return lax.ppermute(arr, 'clip', [(i, (i + d) % 4) for i in range(4)])  93.6 us
    dot_general x25, matrix products, product_back(): lax.dot_general(grad_arr, weight, (((grad_arr.ndim - 1,), (1,)), ((), ())...  75.9 us
    ppermute x83, starting transfers between devices, swap(): return lax.ppermute(arr, 'seq', SWAP[axis])  61.1 us
    dot_general x9, matrix products, sums_of(): lax.dot_general(left, right, (((0,), (0,)), ((), ())), preferred_element_...  58.4 us
    unnamed x454, local copies, waits for them, and re-layouts  34.7 us
  transfers between devices with their start and end apart: 124, of which 42 were waited for; matrix products, arithmetic and copies ran while one was open for 48% of the time, Pallas kernels for 0%

profile of v2, /device:TPU:0, one launch (start us, length us, event | category | flops | bytes accessed | tf_op | source)
XLA Modules:
  0.0 1240.0 jit_solution(15563737557403109152)
XLA Ops:
  26.5 5.0 collective-permute-done
  31.5 12.6 %collective-permute-done.1 = f32[26,1152]{1,0:T(8,128)S(1)} collective-permute-done((f32[26,1152]{1,0:T(8,128)S(1)}, f32[26,1152]{1,0:T(8,128)S(1)}, u32[]{:S(2)}, u32[]{:S(2)}) %collective-permute-start.1) | collective-permute-done | bytes 119840 | tf_op jit(solution)/shard_map/ppermute | solution.py:517
  44.1 9.3 collective-permute-start.6
  73.2 12.2 collective-permute-done.7
  85.4 16.0 %collective-permute-start.16 = (bf16[1,40,4608]{2,1,0:T(8,128)(2,1)S(1)}, bf16[1,40,4608]{2,1,0:T(8,128)(2,1)S(1)}, u32[]{:S(2)}, u32[]{:S(2)}) collective-permute-start(bf16[1,40,4608]{2,1,0:T(8,128)(2,1)S(1)} %pad_bitcast_fusion), channel_id=1, source_target_pairs={{0,8},{8,16},{16,24},{24,0},{1,9},{9,17},{17,25},{25,1},{2,10},{10... | collective-permute-start | bytes 1105928 | tf_op jit(solution)/shard_map/ppermute | solution.py:517
  101.4 6.8 collective-permute-start.17
  112.3 18.2 %collective-permute-done.12 = bf16[1,40,4608]{2,1,0:T(8,128)(2,1)S(1)} collective-permute-done((bf16[1,40,4608]{2,1,0:T(8,128)(2,1)S(1)}, bf16[1,40,4608]{2,1,0:T(8,128)(2,1)S(1)}, u32[]{:S(2)}, u32[]{:S(2)}) %collective-permute-start.12) | collective-permute-done | bytes 368672 | tf_op jit(solution)/shard_map/ppermute | solution.py:517
  133.5 12.4 collective-permute-start.31
  147.5 14.6 %collective-permute-done.17 = bf16[1,40,4608]{2,1,0:T(8,128)(2,1)S(1)} collective-permute-done((bf16[1,40,4608]{2,1,0:T(8,128)(2,1)S(1)}, bf16[1,40,4608]{2,1,0:T(8,128)(2,1)S(1)}, u32[]{:S(2)}, u32[]{:S(2)}) %collective-permute-start.17) | collective-permute-done | bytes 368672 | tf_op jit(solution)/shard_map/ppermute | solution.py:517
  167.4 12.7 %collective-permute-done.10 = bf16[4,40,2304]{2,1,0:T(8,128)(2,1)S(1)} collective-permute-done((bf16[4,40,2304]{2,1,0:T(8,128)(2,1)S(1)}, bf16[4,40,2304]{2,1,0:T(8,128)(2,1)S(1)}, u32[]{:S(2)}, u32[]{:S(2)}) %collective-permute-start.10) | collective-permute-done | bytes 737312 | tf_op jit(solution)/shard_map/ppermute | solution.py:513
  185.3 29.1 %collective-permute-done.15 = bf16[8,40,2304]{2,1,0:T(8,128)(2,1)S(1)} collective-permute-done((bf16[8,40,2304]{2,1,0:T(8,128)(2,1)S(1)}, bf16[8,40,2304]{2,1,0:T(8,128)(2,1)S(1)}, u32[]{:S(2)}, u32[]{:S(2)}) %collective-permute-start.15) | collective-permute-done | bytes 1474592 | tf_op jit(solution)/shard_map/ppermute | solution.py:513
  226.0 27.6 %collective-permute-done.21 = bf16[4,40,2304]{2,1,0:T(8,128)(2,1)S(1)} collective-permute-done((bf16[4,40,2304]{2,1,0:T(8,128)(2,1)S(1)}, bf16[4,40,2304]{2,1,0:T(8,128)(2,1)S(1)}, u32[]{:S(2)}, u32[]{:S(2)}) %collective-permute-start.21) | collective-permute-done | bytes 737312 | tf_op jit(solution)/shard_map/ppermute | solution.py:513
  275.5 14.4 %collective-permute-done.27 = bf16[8,40,2304]{2,1,0:T(8,128)(2,1)} collective-permute-done((bf16[8,40,2304]{2,1,0:T(8,128)(2,1)}, bf16[8,40,2304]{2,1,0:T(8,128)(2,1)}, u32[]{:S(2)}, u32[]{:S(2)}) %collective-permute-start.27) | collective-permute-done | bytes 1474592 | tf_op jit(solution)/shard_map/ppermute | solution.py:513
  309.1 5.4 collective-permute-done.34
  335.1 10.0 all-to-all-done
  365.1 5.7 reshape.1780
  370.8 5.7 reshape.1778
  376.5 5.7 reshape.1779
  382.2 8.9 collective-permute-done.36
  416.7 5.0 reshape.1784
  452.6 25.0 %all-to-all-done.1 = bf16[1,16,32,1152]{3,2,0,1:T(8,128)(2,1)} async-done(((bf16[1,16,32,1152]{3,2,0,1:T(8,128)(2,1)}), bf16[1,16,32,1152]{3,2,0,1:T(8,128)(2,1)}, u32[]{:S(2)}, u32[]{:S(2)}) %all-to-all-start.1) | async-done | bytes 1179680 | tf_op jit(solution)/shard_map/all_to_all | solution.py:820
  534.7 5.8 fusion.40
  565.3 5.2 maximum_maximum_fusion
  570.5 12.8 %convolution_bitcast_fusion = f32[1,512,4608]{2,1,0:T(8,128)} fusion(bf16[512,1152]{1,0:T(8,128)(2,1)S(1)} %fusion.195, bf16[4608,1152]{1,0:T(8,128)(2,1)} %bitcast.835), kind=kOutput, calls=%fused_computation.23 | convolution fusion | flops 5435817984 | bytes 21233664 | tf_op jit(solution)/shard_map/dot_general | solution.py:29
  583.4 11.6 fusion.11
  595.0 10.2 fusion.6
  637.4 15.6 %collective-permute-done.56 = bf16[4,2,2,144,256]{4,3,2,1,0:T(8,128)(2,1)} collective-permute-done((bf16[4,2,2,144,256]{4,3,2,1,0:T(8,128)(2,1)}, bf16[4,2,2,144,256]{4,3,2,1,0:T(8,128)(2,1)}, u32[]{:S(2)}, u32[]{:S(2)}) %collective-permute-start.56) | collective-permute-done | bytes 1179680 | tf_op jit(solution)/shard_map/ppermute | solution.py:513
  654.8 7.7 collective-permute-done.55
  669.1 5.0 convolution_convert_fusion.6
  709.0 6.1 multiply_reduce_fusion.5
  715.2 8.2 fusion.196
  738.2 12.2 collective-permute-done.58
  793.1 9.5 multiply_convert_fusion.9
  813.3 5.5 broadcast_select_fusion
  845.5 9.5 all-to-all-done.2
  863.3 5.0 reshape.1829
  923.3 6.8 convolution_convert_fusion.3
  930.2 5.5 convolution_convert_fusion.2
  962.9 21.1 %collective-permute-done.88 = bf16[2,40,2304]{2,1,0:T(8,128)(2,1)} collective-permute-done((bf16[2,40,2304]{2,1,0:T(8,128)(2,1)}, bf16[2,40,2304]{2,1,0:T(8,128)(2,1)}, u32[]{:S(2)}, u32[]{:S(2)}) %collective-permute-start.88) | collective-permute-done | bytes 368672 | tf_op jit(solution)/shard_map/ppermute | solution.py:517
  999.8 6.3 multiply_reduce_fusion
  1032.9 13.3 %collective-permute-done.99 = bf16[2,4,40,1152]{3,2,0,1:T(8,128)(2,1)S(1)} collective-permute-done((bf16[2,4,40,1152]{3,2,0,1:T(8,128)(2,1)S(1)}, bf16[2,4,40,1152]{3,2,0,1:T(8,128)(2,1)S(1)}, u32[]{:S(2)}, u32[]{:S(2)}) %collective-permute-start.99) | collective-permute-done | bytes 737312 | tf_op jit(solution)/shard_map/ppermute | solution.py:513
  1061.3 23.9 %collective-permute-done.102 = bf16[2,40,2304]{2,1,0:T(8,128)(2,1)} collective-permute-done((bf16[2,40,2304]{2,1,0:T(8,128)(2,1)}, bf16[2,40,2304]{2,1,0:T(8,128)(2,1)}, u32[]{:S(2)}, u32[]{:S(2)}) %collective-permute-start.102) | collective-permute-done | bytes 368672 | tf_op jit(solution)/shard_map/ppermute | solution.py:517
  1087.5 8.5 convolution_convert_fusion.1
  1096.1 6.7 convolution_convert_fusion
  1123.3 5.7 fusion.23
  1129.0 20.7 %collective-permute-done.105 = bf16[2,2,4,40,1152]{4,3,0,2,1:T(8,128)(2,1)S(1)} collective-permute-done((bf16[2,2,4,40,1152]{4,3,0,2,1:T(8,128)(2,1)S(1)}, bf16[2,2,4,40,1152]{4,3,0,2,1:T(8,128)(2,1)S(1)}, u32[]{:S(2)}, u32[]{:S(2)}) %collective-permute-start.105) | collective-permute-done | bytes 1474592 | tf_op jit(solution)/shard_map/ppermute | solution.py:513
  1167.1 16.2 %collective-permute-done.107 = f32[20,1152]{1,0:T(8,128)S(1)} collective-permute-done((f32[20,1152]{1,0:T(8,128)S(1)}, f32[20,1152]{1,0:T(8,128)S(1)}, u32[]{:S(2)}, u32[]{:S(2)}) %collective-permute-start.107) | collective-permute-done | bytes 92192 | tf_op jit(solution)/shard_map/ppermute | solution.py:513
  1199.0 24.7 %collective-permute-done.116 = bf16[2,40,2304]{2,1,0:T(8,128)(2,1)S(1)} collective-permute-done((bf16[2,40,2304]{2,1,0:T(8,128)(2,1)S(1)}, bf16[2,40,2304]{2,1,0:T(8,128)(2,1)S(1)}, u32[]{:S(2)}, u32[]{:S(2)}) %collective-permute-start.116) | collective-permute-done | bytes 368672 | tf_op jit(solution)/shard_map/ppermute | solution.py:517
  (1027 shorter events, 669.0 us)
Async XLA Ops:
  7.2 52.9 %collective-permute-start.23 = (bf16[1,144,1152]{2,1,0:T(8,128)(2,1)}, bf16[1,144,1152]{2,1,0:T(8,128)(2,1)}, u32[]{:S(2)}, u32[]{:S(2)}) collective-permute-start(bf16[1,144,1152]{2,1,0:T(8,128)(2,1)} %param.30), channel_id=1, source_target_pairs={{0,8},{8,16},{16,24},{24,0},{1,9},{9,17},{17,25},{25,1},{2,10},{10... | collective-permute-start | bytes 995336 | tf_op jit(solution)/shard_map/ppermute | solution.py:517
  10.3 50.9 %collective-permute-start.24 = (bf16[1,144,1152]{2,1,0:T(8,128)(2,1)}, bf16[1,144,1152]{2,1,0:T(8,128)(2,1)}, u32[]{:S(2)}, u32[]{:S(2)}) collective-permute-start(bf16[1,144,1152]{2,1,0:T(8,128)(2,1)} %param.30), channel_id=1, source_target_pairs={{0,16},{8,24},{16,0},{24,8},{1,17},{9,25},{17,1},{25,9},{2,18},{10... | collective-permute-start | bytes 995336 | tf_op jit(solution)/shard_map/ppermute | solution.py:517
  17.2 36.3 %collective-permute-start.2 = (f32[26,1152]{1,0:T(8,128)S(1)}, f32[26,1152]{1,0:T(8,128)S(1)}, u32[]{:S(2)}, u32[]{:S(2)}) collective-permute-start(f32[26,1152]{1,0:T(8,128)S(1)} %get-tuple-element.464), channel_id=1, source_target_pairs={{0,24},{8,0},{16,8},{24,16},{1,25},{9,1},{17,9},{25,17},{2,26},{10... | collective-permute-start | bytes 359432 | tf_op jit(solution)/shard_map/ppermute | solution.py:517
  60.1 41.3 %collective-permute-start.8 = (bf16[1,40,4608]{2,1,0:T(8,128)(2,1)}, bf16[1,40,4608]{2,1,0:T(8,128)(2,1)S(1)}, u32[]{:S(2)}, u32[]{:S(2)}) collective-permute-start(bf16[1,40,4608]{2,1,0:T(8,128)(2,1)} %fusion.444), channel_id=1, source_target_pairs={{0,24},{8,0},{16,8},{24,16},{1,25},{9,1},{17,9},{25,17},{2,26},{10... | collective-permute-start | bytes 1105928 | tf_op jit(solution)/shard_map/ppermute | solution.py:517
  61.2 47.3 %collective-permute-start.11 = (bf16[1,40,4608]{2,1,0:T(8,128)(2,1)}, bf16[1,40,4608]{2,1,0:T(8,128)(2,1)S(1)}, u32[]{:S(2)}, u32[]{:S(2)}) collective-permute-start(bf16[1,40,4608]{2,1,0:T(8,128)(2,1)} %copy-done.97), channel_id=1, source_target_pairs={{0,8},{8,16},{16,24},{24,0},{1,9},{9,17},{17,25},{25,1},{2,10},{10... | collective-permute-start | bytes 1105928 | tf_op jit(solution)/shard_map/ppermute | solution.py:517
  69.5 61.1 %collective-permute-start.12 = (bf16[1,40,4608]{2,1,0:T(8,128)(2,1)S(1)}, bf16[1,40,4608]{2,1,0:T(8,128)(2,1)S(1)}, u32[]{:S(2)}, u32[]{:S(2)}) collective-permute-start(bf16[1,40,4608]{2,1,0:T(8,128)(2,1)S(1)} %copy-done.98), channel_id=1, source_target_pairs={{0,16},{8,24},{16,0},{24,8},{1,17},{9,25},{17,1},{25,9},{2,18},{10... | collective-permute-start | bytes 1105928 | tf_op jit(solution)/shard_map/ppermute | solution.py:517
  71.6 62.0 %collective-permute-start.13 = (bf16[1,40,4608]{2,1,0:T(8,128)(2,1)S(1)}, bf16[1,40,4608]{2,1,0:T(8,128)(2,1)S(1)}, u32[]{:S(2)}, u32[]{:S(2)}) collective-permute-start(bf16[1,40,4608]{2,1,0:T(8,128)(2,1)S(1)} %copy-done.98), channel_id=1, source_target_pairs={{0,24},{8,0},{16,8},{24,16},{1,25},{9,1},{17,9},{25,17},{2,26},{10... | collective-permute-start | bytes 1105928 | tf_op jit(solution)/shard_map/ppermute | solution.py:517
  85.4 60.5 %collective-permute-start.16 = (bf16[1,40,4608]{2,1,0:T(8,128)(2,1)S(1)}, bf16[1,40,4608]{2,1,0:T(8,128)(2,1)S(1)}, u32[]{:S(2)}, u32[]{:S(2)}) collective-permute-start(bf16[1,40,4608]{2,1,0:T(8,128)(2,1)S(1)} %pad_bitcast_fusion), channel_id=1, source_target_pairs={{0,8},{8,16},{16,24},{24,0},{1,9},{9,17},{17,25},{25,1},{2,10},{10... | collective-permute-start | bytes 1105928 | tf_op jit(solution)/shard_map/ppermute | solution.py:517
  101.4 60.8 %collective-permute-start.17 = (bf16[1,40,4608]{2,1,0:T(8,128)(2,1)S(1)}, bf16[1,40,4608]{2,1,0:T(8,128)(2,1)S(1)}, u32[]{:S(2)}, u32[]{:S(2)}) collective-permute-start(bf16[1,40,4608]{2,1,0:T(8,128)(2,1)S(1)} %pad_bitcast_fusion), channel_id=1, source_target_pairs={{0,16},{8,24},{16,0},{24,8},{1,17},{9,25},{17,1},{25,9},{2,18},{10... | collective-permute-start | bytes 1105928 | tf_op jit(solution)/shard_map/ppermute | solution.py:517
  108.5 73.3 %collective-permute-start.18 = (bf16[1,40,4608]{2,1,0:T(8,128)(2,1)S(1)}, bf16[1,40,4608]{2,1,0:T(8,128)(2,1)S(1)}, u32[]{:S(2)}, u32[]{:S(2)}) collective-permute-start(bf16[1,40,4608]{2,1,0:T(8,128)(2,1)S(1)} %pad_bitcast_fusion), channel_id=1, source_target_pairs={{0,24},{8,0},{16,8},{24,16},{1,25},{9,1},{17,9},{25,17},{2,26},{10... | collective-permute-start | bytes 1105928 | tf_op jit(solution)/shard_map/ppermute | solution.py:517
  130.6 52.8 %collective-permute-start.30 = (bf16[1,40,4608]{2,1,0:T(8,128)(2,1)S(1)}, bf16[1,40,4608]{2,1,0:T(8,128)(2,1)S(1)}, u32[]{:S(2)}, u32[]{:S(2)}) collective-permute-start(bf16[1,40,4608]{2,1,0:T(8,128)(2,1)S(1)} %fusion.449), channel_id=1, source_target_pairs={{0,8},{8,16},{16,24},{24,0},{1,9},{9,17},{17,25},{25,1},{2,10},{10... | collective-permute-start | bytes 1105928 | tf_op jit(solution)/shard_map/ppermute | solution.py:517
  133.5 84.2 %collective-permute-start.31 = (bf16[1,40,4608]{2,1,0:T(8,128)(2,1)S(1)}, bf16[1,40,4608]{2,1,0:T(8,128)(2,1)S(1)}, u32[]{:S(2)}, u32[]{:S(2)}) collective-permute-start(bf16[1,40,4608]{2,1,0:T(8,128)(2,1)S(1)} %fusion.449), channel_id=1, source_target_pairs={{0,16},{8,24},{16,0},{24,8},{1,17},{9,25},{17,1},{25,9},{2,18},{10... | collective-permute-start | bytes 1105928 | tf_op jit(solution)/shard_map/ppermute | solution.py:517
  163.9 53.8 %collective-permute-start.32 = (bf16[1,40,4608]{2,1,0:T(8,128)(2,1)S(1)}, bf16[1,40,4608]{2,1,0:T(8,128)(2,1)S(1)}, u32[]{:S(2)}, u32[]{:S(2)}) collective-permute-start(bf16[1,40,4608]{2,1,0:T(8,128)(2,1)S(1)} %fusion.449), channel_id=1, source_target_pairs={{0,24},{8,0},{16,8},{24,16},{1,25},{9,1},{17,9},{25,17},{2,26},{10... | collective-permute-start | bytes 1105928 | tf_op jit(solution)/shard_map/ppermute | solution.py:517
  180.1 40.1 %collective-permute-start.5 = (f32[26,1152]{1,0:T(8,128)S(1)}, f32[26,1152]{1,0:T(8,128)S(1)}, u32[]{:S(2)}, u32[]{:S(2)}) collective-permute-start(f32[26,1152]{1,0:T(8,128)S(1)} %add.801), channel_id=1, source_target_pairs={{0,4},{1,5},{2,6},{3,7},{4,0},{5,1},{6,2},{7,3},{8,12},{9,13},{10,... | collective-permute-start | bytes 359432 | tf_op jit(solution)/shard_map/ppermute | solution.py:513
  217.1 37.7 %collective-permute-start.19 = (bf16[640,2304]{1,0:T(8,128)(2,1)S(1)}, bf16[640,2304]{1,0:T(8,128)(2,1)S(1)}, u32[]{:S(2)}, u32[]{:S(2)}) collective-permute-start(bf16[640,2304]{1,0:T(8,128)(2,1)S(1)} %bitcast.808), channel_id=1, source_target_pairs={{0,1},{1,0},{2,3},{3,2},{4,5},{5,4},{6,7},{7,6},{8,9},{9,8},{10,11... | collective-permute-start | bytes 8847368 | tf_op jit(solution)/shard_map/ppermute | solution.py:513
  217.2 37.7 %collective-permute-start.20 = (bf16[640,2304]{1,0:T(8,128)(2,1)S(1)}, bf16[640,2304]{1,0:T(8,128)(2,1)S(1)}, u32[]{:S(2)}, u32[]{:S(2)}) collective-permute-start(bf16[640,2304]{1,0:T(8,128)(2,1)S(1)} %bitcast.803), channel_id=1, source_target_pairs={{0,1},{1,0},{2,3},{3,2},{4,5},{5,4},{6,7},{7,6},{8,9},{9,8},{10,11... | collective-permute-start | bytes 8847368 | tf_op jit(solution)/shard_map/ppermute | solution.py:513
  219.2 77.9 %collective-permute-start.33 = (bf16[4,40,2304]{2,1,0:T(8,128)(2,1)}, bf16[4,40,2304]{2,1,0:T(8,128)(2,1)}, u32[]{:S(2)}, u32[]{:S(2)}) collective-permute-start(bf16[4,40,2304]{2,1,0:T(8,128)(2,1)} %get-tuple-element.152), channel_id=1, source_target_pairs={{0,2},{1,3},{2,0},{3,1},{4,6},{5,7},{6,4},{7,5},{8,10},{9,11},{10,... | collective-permute-start | bytes 2211848 | tf_op jit(solution)/shard_map/ppermute | solution.py:513
  257.2 35.1 %collective-permute-start.26 = (bf16[8,40,2304]{2,1,0:T(8,128)(2,1)}, bf16[8,40,2304]{2,1,0:T(8,128)(2,1)}, u32[]{:S(2)}, u32[]{:S(2)}) collective-permute-start(bf16[8,40,2304]{2,1,0:T(8,128)(2,1)} %pad_maximum_fusion.16), channel_id=1, source_target_pairs={{0,4},{1,5},{2,6},{3,7},{4,0},{5,1},{6,2},{7,3},{8,12},{9,13},{10,... | collective-permute-start | bytes 4423688 | tf_op jit(solution)/shard_map/ppermute | solution.py:513
  328.5 73.5 %collective-permute-start.39 = (bf16[4,40,2304]{2,1,0:T(8,128)(2,1)}, bf16[4,40,2304]{2,1,0:T(8,128)(2,1)}, u32[]{:S(2)}, u32[]{:S(2)}) collective-permute-start(bf16[4,40,2304]{2,1,0:T(8,128)(2,1)} %get-tuple-element.167), channel_id=1, source_target_pairs={{0,2},{1,3},{2,0},{3,1},{4,6},{5,7},{6,4},{7,5},{8,10},{9,11},{10,... | collective-permute-start | bytes 2211848 | tf_op jit(solution)/shard_map/ppermute | solution.py:513
  333.1 58.1 %collective-permute-start.36 = (bf16[8,40,2304]{2,1,0:T(8,128)(2,1)}, bf16[8,40,2304]{2,1,0:T(8,128)(2,1)}, u32[]{:S(2)}, u32[]{:S(2)}) collective-permute-start(bf16[8,40,2304]{2,1,0:T(8,128)(2,1)} %pad_maximum_fusion.19), channel_id=1, source_target_pairs={{0,2},{1,3},{2,0},{3,1},{4,6},{5,7},{6,4},{7,5},{8,10},{9,11},{10,... | collective-permute-start | bytes 4423688 | tf_op jit(solution)/shard_map/ppermute | solution.py:513
  333.1 61.7 %collective-permute-start.35 = (bf16[8,40,2304]{2,1,0:T(8,128)(2,1)}, bf16[8,40,2304]{2,1,0:T(8,128)(2,1)}, u32[]{:S(2)}, u32[]{:S(2)}) collective-permute-start(bf16[8,40,2304]{2,1,0:T(8,128)(2,1)} %pad_maximum_fusion.18), channel_id=1, source_target_pairs={{0,4},{1,5},{2,6},{3,7},{4,0},{5,1},{6,2},{7,3},{8,12},{9,13},{10,... | collective-permute-start | bytes 4423688 | tf_op jit(solution)/shard_map/ppermute | solution.py:513
  405.4 96.0 %collective-permute-start.45 = (bf16[4,1,1,1,72,1152]{5,4,3,2,1,0:T(8,128)(2,1)}, bf16[4,1,1,1,72,1152]{5,4,3,2,1,0:T(8,128)(2,1)}, u32[]{:S(2)}, u32[]{:S(2)}) collective-permute-start(bf16[4,1,1,1,72,1152]{5,4,3,2,1,0:T(8,128)(2,1)} %get-tuple-element.397), channel_id=1, source_target_pairs={{0,2},{1,3},{2,0},{3,1},{4,6},{5,7},{6,4},{7,5},{8,10},{9,11},{10,... | collective-permute-start | bytes 1990664 | tf_op jit(solution)/shard_map/ppermute | solution.py:513
  406.0 95.5 %collective-permute-start.46 = (bf16[4,1,1,1,72,1152]{5,4,3,2,1,0:T(8,128)(2,1)}, bf16[4,1,1,1,72,1152]{5,4,3,2,1,0:T(8,128)(2,1)}, u32[]{:S(2)}, u32[]{:S(2)}) collective-permute-start(bf16[4,1,1,1,72,1152]{5,4,3,2,1,0:T(8,128)(2,1)} %get-tuple-element.396), channel_id=1, source_target_pairs={{0,4},{1,5},{2,6},{3,7},{4,0},{5,1},{6,2},{7,3},{8,12},{9,13},{10,... | collective-permute-start | bytes 1990664 | tf_op jit(solution)/shard_map/ppermute | solution.py:513
  428.7 63.6 %collective-permute-start.42 = (bf16[8,40,2304]{2,1,0:T(8,128)(2,1)}, bf16[8,40,2304]{2,1,0:T(8,128)(2,1)}, u32[]{:S(2)}, u32[]{:S(2)}) collective-permute-start(bf16[8,40,2304]{2,1,0:T(8,128)(2,1)} %pad_maximum_fusion.21), channel_id=1, source_target_pairs={{0,2},{1,3},{2,0},{3,1},{4,6},{5,7},{6,4},{7,5},{8,10},{9,11},{10,... | collective-permute-start | bytes 4423688 | tf_op jit(solution)/shard_map/ppermute | solution.py:513
  430.5 66.8 %collective-permute-start.41 = (bf16[8,40,2304]{2,1,0:T(8,128)(2,1)}, bf16[8,40,2304]{2,1,0:T(8,128)(2,1)}, u32[]{:S(2)}, u32[]{:S(2)}) collective-permute-start(bf16[8,40,2304]{2,1,0:T(8,128)(2,1)} %pad_maximum_fusion.20), channel_id=1, source_target_pairs={{0,4},{1,5},{2,6},{3,7},{4,0},{5,1},{6,2},{7,3},{8,12},{9,13},{10,... | collective-permute-start | bytes 4423688 | tf_op jit(solution)/shard_map/ppermute | solution.py:513
  437.2 40.4 %all-to-all-start.1 = ((bf16[1,16,32,1152]{3,2,0,1:T(8,128)(2,1)}), bf16[1,16,32,1152]{3,2,0,1:T(8,128)(2,1)}, u32[]{:S(2)}, u32[]{:S(2)}) async-start(bf16[1,16,32,1152]{3,2,0,1:T(8,128)(2,1)} %fusion.262), calls=%async_computation.1 | async-start | bytes 2359296 | tf_op jit(solution)/shard_map/all_to_all | solution.py:820
  441.4 791.3 %reduce-scatter.2.cloned.1.call-start = ((), (), s32[]{:S(2)}) async-start(), calls=%async_computation.5 | async-start | bytes 663552 | tf_op jit(solution)/shard_map/reduce_scatter | solution.py:971
  510.9 34.7 %collective-permute-start.48 = (bf16[4,2,1,1,72,1152]{5,4,3,2,1,0:T(8,128)(2,1)S(1)}, bf16[4,2,1,1,72,1152]{5,4,3,2,1,0:T(8,128)(2,1)S(1)}, u32[]{:S(2)}, u32[]{:S(2)}) collective-permute-start(bf16[4,2,1,1,72,1152]{5,4,3,2,1,0:T(8,128)(2,1)S(1)} %pad_maximum_fusion.28), channel_id=1, source_target_pairs={{0,2},{1,3},{2,0},{3,1},{4,6},{5,7},{6,4},{7,5},{8,10},{9,11},{10,... | collective-permute-start | bytes 3981320 | tf_op jit(solution)/shard_map/ppermute | solution.py:513
  511.2 36.3 %collective-permute-start.47 = (bf16[4,1,2,1,72,1152]{5,4,3,2,1,0:T(8,128)(2,1)S(1)}, bf16[4,1,2,1,72,1152]{5,4,3,2,1,0:T(8,128)(2,1)S(1)}, u32[]{:S(2)}, u32[]{:S(2)}) collective-permute-start(bf16[4,1,2,1,72,1152]{5,4,3,2,1,0:T(8,128)(2,1)S(1)} %pad_maximum_fusion.27), channel_id=1, source_target_pairs={{0,4},{1,5},{2,6},{3,7},{4,0},{5,1},{6,2},{7,3},{8,12},{9,13},{10,... | collective-permute-start | bytes 3981320 | tf_op jit(solution)/shard_map/ppermute | solution.py:513
  550.9 55.3 %collective-permute-start.92 = (bf16[512,1280]{1,0:T(8,128)(2,1)S(1)}, bf16[512,1280]{1,0:T(8,128)(2,1)}, u32[]{:S(2)}, u32[]{:S(2)}) collective-permute-start(bf16[512,1280]{1,0:T(8,128)(2,1)S(1)} %bitcast.882), channel_id=1, source_target_pairs={{0,1},{1,0},{2,3},{3,2},{4,5},{5,4},{6,7},{7,6},{8,9},{9,8},{10,11... | collective-permute-start | bytes 3932168 | tf_op jit(solution)/shard_map/ppermute | solution.py:513
  605.2 59.0 %collective-permute-start.54 = (bf16[512,4608]{1,0:T(8,128)(2,1)}, bf16[512,4608]{1,0:T(8,128)(2,1)}, u32[]{:S(2)}, u32[]{:S(2)}) collective-permute-start(bf16[512,4608]{1,0:T(8,128)(2,1)} %bitcast.102), channel_id=1, source_target_pairs={{0,1},{1,0},{2,3},{3,2},{4,5},{5,4},{6,7},{7,6},{8,9},{9,8},{10,11... | collective-permute-start | bytes 14155784 | tf_op jit(solution)/shard_map/ppermute | solution.py:513
  621.7 40.8 %collective-permute-start.55 = (bf16[4,2,2,144,384]{4,3,2,1,0:T(8,128)(2,1)S(1)}, bf16[4,2,2,144,384]{4,3,2,1,0:T(8,128)(2,1)}, u32[]{:S(2)}, u32[]{:S(2)}) collective-permute-start(bf16[4,2,2,144,384]{4,3,2,1,0:T(8,128)(2,1)S(1)} %dynamic-slice_bitcast_fusion), channel_id=1, source_target_pairs={{0,4},{1,5},{2,6},{3,7},{4,0},{5,1},{6,2},{7,3},{8,12},{9,13},{10,... | collective-permute-start | bytes 5308424 | tf_op jit(solution)/shard_map/ppermute | solution.py:513
  700.0 104.7 %collective-permute-start.69 = (bf16[2,2,4,40,1152]{4,3,0,2,1:T(8,128)(2,1)}, bf16[2,2,4,40,1152]{4,3,0,2,1:T(8,128)(2,1)}, u32[]{:S(2)}, u32[]{:S(2)}) collective-permute-start(bf16[2,2,4,40,1152]{4,3,0,2,1:T(8,128)(2,1)} %bitcast.789), channel_id=1, source_target_pairs={{0,2},{1,3},{2,0},{3,1},{4,6},{5,7},{6,4},{7,5},{8,10},{9,11},{10,... | collective-permute-start | bytes 4423688 | tf_op jit(solution)/shard_map/ppermute | solution.py:513
  704.2 102.8 %collective-permute-start.68 = (bf16[2,2,4,40,1152]{4,3,0,2,1:T(8,128)(2,1)}, bf16[2,2,4,40,1152]{4,3,0,2,1:T(8,128)(2,1)}, u32[]{:S(2)}, u32[]{:S(2)}) collective-permute-start(bf16[2,2,4,40,1152]{4,3,0,2,1:T(8,128)(2,1)} %bitcast.790), channel_id=1, source_target_pairs={{0,4},{1,5},{2,6},{3,7},{4,0},{5,1},{6,2},{7,3},{8,12},{9,13},{10,... | collective-permute-start | bytes 4423688 | tf_op jit(solution)/shard_map/ppermute | solution.py:513
  706.1 46.7 %collective-permute-start.57 = (bf16[4,2,144,384]{3,2,1,0:T(8,128)(2,1)}, bf16[4,2,144,384]{3,2,1,0:T(8,128)(2,1)}, u32[]{:S(2)}, u32[]{:S(2)}) collective-permute-start(bf16[4,2,144,384]{3,2,1,0:T(8,128)(2,1)} %dynamic-slice_bitcast_fusion.2), channel_id=1, source_target_pairs={{0,2},{1,3},{2,0},{3,1},{4,6},{5,7},{6,4},{7,5},{8,10},{9,11},{10,... | collective-permute-start | bytes 2654216 | tf_op jit(solution)/shard_map/ppermute | solution.py:513
  707.3 43.1 %collective-permute-start.58 = (bf16[4,2,144,256]{3,2,1,0:T(8,128)(2,1)}, bf16[4,2,144,256]{3,2,1,0:T(8,128)(2,1)}, u32[]{:S(2)}, u32[]{:S(2)}) collective-permute-start(bf16[4,2,144,256]{3,2,1,0:T(8,128)(2,1)} %dynamic-slice_bitcast_fusion.3), channel_id=1, source_target_pairs={{0,4},{1,5},{2,6},{3,7},{4,0},{5,1},{6,2},{7,3},{8,12},{9,13},{10,... | collective-permute-start | bytes 1769480 | tf_op jit(solution)/shard_map/ppermute | solution.py:513
  833.8 80.2 %collective-permute-start.83 = (bf16[2,2,4,40,1152]{4,3,0,2,1:T(8,128)(2,1)}, bf16[2,2,4,40,1152]{4,3,0,2,1:T(8,128)(2,1)}, u32[]{:S(2)}, u32[]{:S(2)}) collective-permute-start(bf16[2,2,4,40,1152]{4,3,0,2,1:T(8,128)(2,1)} %bitcast.787), channel_id=1, source_target_pairs={{0,2},{1,3},{2,0},{3,1},{4,6},{5,7},{6,4},{7,5},{8,10},{9,11},{10,... | collective-permute-start | bytes 4423688 | tf_op jit(solution)/shard_map/ppermute | solution.py:513
  838.3 77.5 %collective-permute-start.82 = (bf16[2,2,4,40,1152]{4,3,0,2,1:T(8,128)(2,1)}, bf16[2,2,4,40,1152]{4,3,0,2,1:T(8,128)(2,1)}, u32[]{:S(2)}, u32[]{:S(2)}) collective-permute-start(bf16[2,2,4,40,1152]{4,3,0,2,1:T(8,128)(2,1)} %bitcast.788), channel_id=1, source_target_pairs={{0,4},{1,5},{2,6},{3,7},{4,0},{5,1},{6,2},{7,3},{8,12},{9,13},{10,... | collective-permute-start | bytes 4423688 | tf_op jit(solution)/shard_map/ppermute | solution.py:513
  938.3 77.0 %collective-permute-start.91 = (bf16[2,2,4,40,1152]{4,3,0,2,1:T(8,128)(2,1)}, bf16[2,2,4,40,1152]{4,3,0,2,1:T(8,128)(2,1)}, u32[]{:S(2)}, u32[]{:S(2)}) collective-permute-start(bf16[2,2,4,40,1152]{4,3,0,2,1:T(8,128)(2,1)} %bitcast.785), channel_id=1, source_target_pairs={{0,2},{1,3},{2,0},{3,1},{4,6},{5,7},{6,4},{7,5},{8,10},{9,11},{10,... | collective-permute-start | bytes 4423688 | tf_op jit(solution)/shard_map/ppermute | solution.py:513
  960.9 57.3 %collective-permute-start.90 = (bf16[2,2,4,40,1152]{4,3,0,2,1:T(8,128)(2,1)}, bf16[2,2,4,40,1152]{4,3,0,2,1:T(8,128)(2,1)}, u32[]{:S(2)}, u32[]{:S(2)}) collective-permute-start(bf16[2,2,4,40,1152]{4,3,0,2,1:T(8,128)(2,1)} %bitcast.786), channel_id=1, source_target_pairs={{0,4},{1,5},{2,6},{3,7},{4,0},{5,1},{6,2},{7,3},{8,12},{9,13},{10,... | collective-permute-start | bytes 4423688 | tf_op jit(solution)/shard_map/ppermute | solution.py:513
  1023.5 63.9 %collective-permute-start.93 = (bf16[512,1152]{1,0:T(8,128)(2,1)}, bf16[512,1152]{1,0:T(8,128)(2,1)}, u32[]{:S(2)}, u32[]{:S(2)}) collective-permute-start(bf16[512,1152]{1,0:T(8,128)(2,1)} %bitcast.897), channel_id=1, source_target_pairs={{0,1},{1,0},{2,3},{3,2},{4,5},{5,4},{6,7},{7,6},{8,9},{9,8},{10,11... | collective-permute-start | bytes 3538952 | tf_op jit(solution)/shard_map/ppermute | solution.py:513
  1025.9 61.5 %collective-permute-start.94 = (bf16[512,1152]{1,0:T(8,128)(2,1)}, bf16[512,1152]{1,0:T(8,128)(2,1)}, u32[]{:S(2)}, u32[]{:S(2)}) collective-permute-start(bf16[512,1152]{1,0:T(8,128)(2,1)} %bitcast.899), channel_id=1, source_target_pairs={{0,1},{1,0},{2,3},{3,2},{4,5},{5,4},{6,7},{7,6},{8,9},{9,8},{10,11... | collective-permute-start | bytes 3538952 | tf_op jit(solution)/shard_map/ppermute | solution.py:513
  1050.6 34.5 %collective-permute-start.102 = (bf16[2,40,2304]{2,1,0:T(8,128)(2,1)}, bf16[2,40,2304]{2,1,0:T(8,128)(2,1)}, u32[]{:S(2)}, u32[]{:S(2)}) collective-permute-start(bf16[2,40,2304]{2,1,0:T(8,128)(2,1)} %get-tuple-element.376), channel_id=1, source_target_pairs={{0,16},{8,24},{16,0},{24,8},{1,17},{9,25},{17,1},{25,9},{2,18},{10... | collective-permute-start | bytes 1105928 | tf_op jit(solution)/shard_map/ppermute | solution.py:517
  1061.3 34.7 %collective-permute-start.97 = (bf16[512,1152]{1,0:T(8,128)(2,1)}, bf16[512,1152]{1,0:T(8,128)(2,1)S(1)}, u32[]{:S(2)}, u32[]{:S(2)}) collective-permute-start(bf16[512,1152]{1,0:T(8,128)(2,1)} %copy-done.116), channel_id=1, source_target_pairs={{0,1},{1,0},{2,3},{3,2},{4,5},{5,4},{6,7},{7,6},{8,9},{9,8},{10,11... | collective-permute-start | bytes 3538952 | tf_op jit(solution)/shard_map/ppermute | solution.py:513
  1115.0 34.8 %collective-permute-start.105 = (bf16[2,2,4,40,1152]{4,3,0,2,1:T(8,128)(2,1)S(1)}, bf16[2,2,4,40,1152]{4,3,0,2,1:T(8,128)(2,1)S(1)}, u32[]{:S(2)}, u32[]{:S(2)}) collective-permute-start(bf16[2,2,4,40,1152]{4,3,0,2,1:T(8,128)(2,1)S(1)} %bitcast.879), channel_id=1, source_target_pairs={{0,2},{1,3},{2,0},{3,1},{4,6},{5,7},{6,4},{7,5},{8,10},{9,11},{10,... | collective-permute-start | bytes 4423688 | tf_op jit(solution)/shard_map/ppermute | solution.py:513
  1117.1 34.8 %collective-permute-start.104 = (bf16[2,2,4,40,1152]{4,3,0,2,1:T(8,128)(2,1)S(1)}, bf16[2,2,4,40,1152]{4,3,0,2,1:T(8,128)(2,1)S(1)}, u32[]{:S(2)}, u32[]{:S(2)}) collective-permute-start(bf16[2,2,4,40,1152]{4,3,0,2,1:T(8,128)(2,1)S(1)} %bitcast.880), channel_id=1, source_target_pairs={{0,4},{1,5},{2,6},{3,7},{4,0},{5,1},{6,2},{7,3},{8,12},{9,13},{10,... | collective-permute-start | bytes 4423688 | tf_op jit(solution)/shard_map/ppermute | solution.py:513
  1185.5 38.2 %collective-permute-start.116 = (bf16[2,40,2304]{2,1,0:T(8,128)(2,1)S(1)}, bf16[2,40,2304]{2,1,0:T(8,128)(2,1)S(1)}, u32[]{:S(2)}, u32[]{:S(2)}) collective-permute-start(bf16[2,40,2304]{2,1,0:T(8,128)(2,1)S(1)} %get-tuple-element.373), channel_id=1, source_target_pairs={{0,16},{8,24},{16,0},{24,8},{1,17},{9,25},{17,1},{25,9},{2,18},{10... | collective-permute-start | bytes 1105928 | tf_op jit(solution)/shard_map/ppermute | solution.py:517
  1185.8 37.9 %collective-permute-start.117 = (bf16[2,40,2304]{2,1,0:T(8,128)(2,1)S(1)}, bf16[2,40,2304]{2,1,0:T(8,128)(2,1)S(1)}, u32[]{:S(2)}, u32[]{:S(2)}) collective-permute-start(bf16[2,40,2304]{2,1,0:T(8,128)(2,1)S(1)} %get-tuple-element.372), channel_id=1, source_target_pairs={{0,8},{8,16},{16,24},{24,0},{1,9},{9,17},{17,25},{25,1},{2,10},{10... | collective-permute-start | bytes 1105928 | tf_op jit(solution)/shard_map/ppermute | solution.py:517
  (292 other events, 4221.0 us)
Sparse Core Ops, SparseCore 0:
  793.2 35.5 reduce-scatter.1

commit v3 on v2

--- a/solution.py
+++ b/solution.py
@@ -518,8 +518,9 @@
 
 
 class Task:
-    def __init__(self, steps, state):
-        self.steps, self.state, self.at, self.left = steps, state, 0, 0
+    def __init__(self, steps, state, held):
+        self.held = held
+        self.steps, self.state, self.at, self.left, self.tied = steps, state, 0, 0, False
 
     def done(self):
         return self.at == len(self.steps) and not self.left
@@ -532,29 +533,31 @@
     def __init__(self):
         self.tasks = []
 
-    def add(self, steps, state):
-        self.tasks.append(Task(steps, state))
+    def add(self, steps, state, held=False):
+        self.tasks.append(Task(steps, state, held))
         return self.tasks[-1]
 
     def tick(self, values=()):
         arrived = []
         for task in self.tasks:
             task.left = max(task.left - 1, 0)
-            if task.at and not task.left and not task.tied:
+            if not task.left and not task.tied and (task.at or task.held):
                 arrived.append(task)
         values, states = lax.optimization_barrier((values, [task.state for task in arrived]))
         for task, state in zip(arrived, states):
-            task.state, task.tied = state, True
-        busy, turning = False, False
+            task.state, task.tied = state, task.at > 0
+        busy, turning, hopping = False, False, False
         for task in self.tasks:
             if task.at < len(task.steps) and not task.left:
                 kind, ticks, step = task.steps[task.at]
-                if not (kind == "plane" and busy or kind == "z" and turning):
+                if not (kind == "plane" and (busy or hopping) or kind == "z" and (turning or task.held and busy)):
                     task.state = step(task.state)
                     task.at, task.left, task.tied = task.at + 1, ticks, False
             kind = task.steps[task.at - 1][0] if task.left else ""
             turning = turning or kind == "z"
-            busy = busy or kind == "plane" or task.crosses_plane()
+            last = task.held and kind == "plane" and not task.crosses_plane()
+            busy = busy or kind == "plane" and not last or task.crosses_plane()
+            hopping = hopping or last
         return values
 
     def finish(self, task):
@@ -657,7 +660,7 @@
     def fourth(kept):
         return jnp.concatenate(to_owner(kept[0], kept[1], k), axis=1)[:ROWS]
 
-    return [("plane", 2, first), ("plane", 1, second), ("z", 2, third), ("core", 1, fourth)]
+    return [("plane", 1, first), ("plane", 1, second), ("z", 2, third), ("core", 1, fourth)]
 
 
 def scatter_out_steps(at):
@@ -686,7 +689,7 @@
         low, high = to_owner(mine, lax.dynamic_index_in_dim(kept, 1 - k, 0, keepdims=False), k)
         return jnp.concatenate([low, high[:, 128:]], axis=1)
 
-    return [("plane", 2, first), ("plane", 1, second), ("z", 2, third), ("core", 1, fourth)]
+    return [("plane", 1, first), ("plane", 1, second), ("z", 2, third), ("core", 1, fourth)]
 
 
 def sum_over_plane(arr):
@@ -750,7 +753,7 @@
             arr,
             place.astype(jnp.float32),
             (((arr.ndim - 1,), (1,)), ((), ())),
-            precision=HIGHEST,
+            precision=lax.Precision.HIGH,
             preferred_element_type=jnp.float32,
         )
 
@@ -758,11 +761,11 @@
         return jnp.pad(jnp.concatenate([w[0] for w in weights], axis=1), ((0, PADDED - ROWS), (0, 0)))[None]
 
     mover = Mover()
-    s_task = mover.add(gather_steps(), shard_of(s_qkv, s_proj))
-    t_task = mover.add(gather_steps(), shard_of(t_qkv, t_proj))
-    c_task = mover.add(gather_steps(), shard_of(c_query, c_kv, c_proj))
-    i_task = mover.add(gather_steps(), shard_of(mlp_in))
-    o_task = mover.add(gather_out_steps(at), mlp_out[0])
+    s_task = mover.add(gather_steps(), shard_of(s_qkv, s_proj), held=True)
+    t_task = mover.add(gather_steps(), shard_of(t_qkv, t_proj), held=True)
+    c_task = mover.add(gather_steps(), shard_of(c_query, c_kv, c_proj), held=True)
+    i_task = mover.add(gather_steps(), shard_of(mlp_in), held=True)
+    o_task = mover.add(gather_out_steps(at), mlp_out[0], held=True)
 
     embed = jax.nn.silu(timestep_embed(timesteps, width)).astype(jnp.bfloat16)
     own_embed = lax.dynamic_slice_in_dim(embed, shard * ROWS, ROWS, axis=1)
@@ -778,7 +781,9 @@
     spread = small_part(0)
     for d in (1, 2, 3):
         spread = spread + turn(small_part(d), d)
-    spread = sum_over_plane(spread)
+    mover.tick()
+    for axis in ("k", "x", "y"):
+        spread = mover.tick(spread + swap(spread, axis))
     modulation, vec_float = spread[None, :6], spread[6:]
     hidden = tokens.astype(jnp.float32).reshape(1, rows, width)
     out_rows = out_grad.astype(jnp.float32).reshape(1, rows, width)
@@ -874,11 +879,11 @@
     pair_two, inner_half = pair_packed(normed_two), choose(pair_inner[:, :HALF], pair_inner[:, HALF:])
     sum_in = (sums_of(pair_two, inner_half[:, :width]), sums_of(pair_two, inner_half[:, width:]))
     bias_in = column_sum(grad_inner)
-    grad_inner, sum_in = mover.tick((grad_inner, sum_in))
-    own_in = mover.add(scatter_steps(k), sum_in)
     norm_pull = jax.vjp(modulate, hidden_three, mod_table[:, 3], mod_table[:, 4])[1]
     in_low, in_high = i_task.state
     grad_normed = packed_back(grad_inner[..., :HALF], in_low) + packed_back(grad_inner[..., HALF:], in_high)
+    grad_normed, sum_in = lax.optimization_barrier((grad_normed, sum_in))
+    own_in = mover.add(scatter_steps(k), sum_in)
     grad_normed = mover.tick(grad_normed)
     grad_three, grad_shift_two, grad_scale_two = norm_pull(unpacked_float(grad_normed))
     grad_three = out_rows + grad_three
@@ -914,12 +919,16 @@
         pair_in = pair_packed(inputs)
         low = sums_of(pair_in, choose(pair(query), pair(value)))
         high = sums_of(choose(pair_in, pair_packed(flat)), choose(pair(key), pair(proj_grad)))
-        query, key, value, low, high = lax.optimization_barrier((query, key, value, low, high))
-        owned = mover.add(scatter_steps(k), (low, high))
-        mover.tick()
         w_low, w_high = task.state
+        if task is s_task:
+            query, key, value, low, high = lax.optimization_barrier((query, key, value, low, high))
+            owned = mover.add(scatter_steps(k), (low, high))
+            mover.tick()
         back = packed_back(jnp.concatenate([query, key], axis=-1), w_low)
         back = back + packed_back(value, columns(w_high, 0, width))
+        if task is t_task:
+            back, low, high = lax.optimization_barrier((back, low, high))
+            owned = mover.add(scatter_steps(k), (low, high))
         return owned, back, column_sum(query), column_sum(value)
 
     t_grads = attend_backward(*t_parts, None, t_total, grad_tmixed, TEMPORAL)

time: 1250 us -> 1200 us (0.960)
  starting transfers between devices: 172 us -> 155 us
  waiting for transfers between devices: 396 us -> 383 us
    ppermute x36, waiting for transfers between devices: 143 us -> 192 us  [turn(): return lax.ppermute(arr, 'clip', [(i, (i + d) % 4) for i in range(4)])]
    ppermute x83, waiting for transfers between devices: 209 us -> 180 us  [swap(): return lax.ppermute(arr, 'seq', SWAP[axis])]
    all_to_all x1, waiting for transfers between devices: 25 us -> 2.95 us  [fast_device(): lax.all_to_all(t_branch, 'seq', split_axis=1, concat_axis=2, tiled=True)]
    ppermute x36, starting transfers between devices: 93.6 us -> 75.5 us  [turn(): return lax.ppermute(arr, 'clip', [(i, (i + d) % 4) for i in range(4)])]
    unnamed x454 -> x435, local copies, waits for them, and re-layouts: 34.7 us -> 34.7 us
  transfers between devices with their start and end apart: 124 -> 124, of which waited for: 42 -> 52; matrix products, arithmetic and copies ran while one was open for 48% -> 49% of each run, Pallas kernels for 0% -> 0%
where the time goes in v3:
time: 1200 us; the launch traced here: 1190 us
  waiting for transfers between devices  383 us (32%)
  matrix products  308 us (26%)
  local copies, waits for them, and re-layouts  182 us (15%)
  starting transfers between devices  155 us (13%)
  other arithmetic  140 us (12%)
  between operations  18.9 us (2%)
    ppermute x36, waiting for transfers between devices, turn(): return lax.ppermute(arr, 'clip', [(i, (i + d) % 4) for i in range(4)])  192 us
    ppermute x83, waiting for transfers between devices, swap(): return lax.ppermute(arr, 'seq', SWAP[axis])  180 us
    dot_general x34, matrix products, product(): lax.dot_general(left_arr, right_arr, (((left_arr.ndim - 1,), (0,)), ((),...  98.7 us
    dot_general x25, matrix products, product_back(): lax.dot_general(grad_arr, weight, (((grad_arr.ndim - 1,), (1,)), ((), ())...  80 us
    ppermute x36, starting transfers between devices, turn(): return lax.ppermute(arr, 'clip', [(i, (i + d) % 4) for i in range(4)])  75.5 us
    ppermute x83, starting transfers between devices, swap(): return lax.ppermute(arr, 'seq', SWAP[axis])  62.9 us
    dot_general x9, matrix products, sums_of(): lax.dot_general(left, right, (((0,), (0,)), ((), ())), preferred_element_...  54 us
    unnamed x435, local copies, waits for them, and re-layouts  34.7 us
  transfers between devices with their start and end apart: 124, of which 52 were waited for; matrix products, arithmetic and copies ran while one was open for 49% of the time, Pallas kernels for 0%

profile of v3, /device:TPU:0, one launch (start us, length us, event | category | flops | bytes accessed | tf_op | source)
XLA Modules:
  0.0 1187.6 jit_solution(1126096986376215230)
XLA Ops:
  26.5 7.1 collective-permute-done.2
  35.2 17.4 %collective-permute-done.5 = bf16[1,40,4608]{2,1,0:T(8,128)(2,1)S(1)} collective-permute-done((bf16[1,40,4608]{2,1,0:T(8,128)(2,1)S(1)}, bf16[1,40,4608]{2,1,0:T(8,128)(2,1)S(1)}, u32[]{:S(2)}, u32[]{:S(2)}) %collective-permute-start.5) | collective-permute-done | bytes 368672 | tf_op jit(solution)/shard_map/ppermute | solution.py:517
  56.5 17.9 %collective-permute-done.7 = f32[26,1152]{1,0:T(8,128)S(1)} collective-permute-done((f32[26,1152]{1,0:T(8,128)S(1)}, f32[26,1152]{1,0:T(8,128)S(1)}, u32[]{:S(2)}, u32[]{:S(2)}) %collective-permute-start.7) | collective-permute-done | bytes 119840 | tf_op jit(solution)/shard_map/ppermute | solution.py:513
  74.6 8.5 collective-permute-start.11
  92.8 13.1 %collective-permute-done.12 = bf16[1,40,4608]{2,1,0:T(8,128)(2,1)S(1)} collective-permute-done((bf16[1,40,4608]{2,1,0:T(8,128)(2,1)S(1)}, bf16[1,40,4608]{2,1,0:T(8,128)(2,1)S(1)}, u32[]{:S(2)}, u32[]{:S(2)}) %collective-permute-start.12) | collective-permute-done | bytes 368672 | tf_op jit(solution)/shard_map/ppermute | solution.py:517
  106.3 13.5 %collective-permute-done.15 = bf16[8,40,2304]{2,1,0:T(8,128)(2,1)S(1)} collective-permute-done((bf16[8,40,2304]{2,1,0:T(8,128)(2,1)S(1)}, bf16[8,40,2304]{2,1,0:T(8,128)(2,1)S(1)}, u32[]{:S(2)}, u32[]{:S(2)}) %collective-permute-start.15) | collective-permute-done | bytes 1474592 | tf_op jit(solution)/shard_map/ppermute | solution.py:513
  133.5 11.7 collective-permute-done.18
  154.8 5.2 collective-permute-done.20
  160.0 14.0 %collective-permute-done.21 = bf16[1,40,4608]{2,1,0:T(8,128)(2,1)S(1)} collective-permute-done((bf16[1,40,4608]{2,1,0:T(8,128)(2,1)S(1)}, bf16[1,40,4608]{2,1,0:T(8,128)(2,1)S(1)}, u32[]{:S(2)}, u32[]{:S(2)}) %collective-permute-start.21) | collective-permute-done | bytes 368672 | tf_op jit(solution)/shard_map/ppermute | solution.py:517
  220.2 5.0 collective-permute-done.28
  225.3 7.5 collective-permute-start.29
  259.9 6.5 all-to-all-done
  281.0 5.7 reshape.1823
  286.8 5.7 reshape.1821
  292.4 5.7 reshape.1822
  310.2 5.3 multiply_reduce_fusion.4
  381.2 15.8 %collective-permute-done.42 = bf16[8,40,2304]{2,1,0:T(8,128)(2,1)} collective-permute-done((bf16[8,40,2304]{2,1,0:T(8,128)(2,1)}, bf16[8,40,2304]{2,1,0:T(8,128)(2,1)}, u32[]{:S(2)}, u32[]{:S(2)}) %collective-permute-start.42) | collective-permute-done | bytes 1474592 | tf_op jit(solution)/shard_map/ppermute | solution.py:513
  411.2 8.6 collective-permute-done.45
  481.3 11.0 convolution_bitcast_fusion
  492.6 13.2 %fusion.11 = bf16[4608,640]{1,0:T(8,128)(2,1)} fusion(bf16[512,4608]{1,0:T(8,128)(2,1)} %collective-permute-done.51, bf16[512,4608]{1,0:T(8,128)(2,1)} %bitcast.98, bf16[512,1152]{1,0:T(8,128)(2,1)} %fusion.193, bf16[512,1152]{1,0:T(8,128)(2,1)} %collective-permute-done.52, pred[]{:T(512)S(6)} %eq.42), kind=kOutput, calls=%fused_computation.24 | convolution fusion | flops 6067519488 | bytes 17694720 | tf_op jit(solution)/shard_map/dot_general | solution.py:865
  505.9 7.7 fusion.6
  550.7 18.2 %collective-permute-done.56 = bf16[4,2,2,144,256]{4,3,2,1,0:T(8,128)(2,1)} collective-permute-done((bf16[4,2,2,144,256]{4,3,2,1,0:T(8,128)(2,1)}, bf16[4,2,2,144,256]{4,3,2,1,0:T(8,128)(2,1)}, u32[]{:S(2)}, u32[]{:S(2)}) %collective-permute-start.56) | collective-permute-done | bytes 1179680 | tf_op jit(solution)/shard_map/ppermute | solution.py:513
  577.4 5.0 convolution_convert_fusion.6
  603.2 9.9 fusion.194
  628.1 11.8 collective-permute-done.58
  655.8 7.1 collective-permute-done.67
  662.9 13.2 %collective-permute-done.68 = bf16[2,144,640]{2,1,0:T(8,128)(2,1)S(1)} collective-permute-done((bf16[2,144,640]{2,1,0:T(8,128)(2,1)S(1)}, bf16[2,144,640]{2,1,0:T(8,128)(2,1)S(1)}, u32[]{:S(2)}, u32[]{:S(2)}) %collective-permute-start.68) | collective-permute-done | bytes 368672 | tf_op jit(solution)/shard_map/ppermute | solution.py:517
  707.1 5.3 multiply_convert_fusion.9
  719.6 7.4 convolution_convert_fusion.5
  738.0 6.2 collective-permute-start.73
  755.7 25.0 %collective-permute-done.74 = bf16[2,40,2304]{2,1,0:T(8,128)(2,1)} collective-permute-done((bf16[2,40,2304]{2,1,0:T(8,128)(2,1)}, bf16[2,40,2304]{2,1,0:T(8,128)(2,1)}, u32[]{:S(2)}, u32[]{:S(2)}) %collective-permute-start.74) | collective-permute-done | bytes 368672 | tf_op jit(solution)/shard_map/ppermute | solution.py:517
  792.3 6.0 reshape.1873
  798.3 8.9 multiply_reduce_fusion.2
  831.4 5.1 convert_element_type.650
  856.7 12.5 %collective-permute-done.85 = bf16[2,4,40,1152]{3,2,0,1:T(8,128)(2,1)S(1)} collective-permute-done((bf16[2,4,40,1152]{3,2,0,1:T(8,128)(2,1)S(1)}, bf16[2,4,40,1152]{3,2,0,1:T(8,128)(2,1)S(1)}, u32[]{:S(2)}, u32[]{:S(2)}) %collective-permute-start.85) | collective-permute-done | bytes 737312 | tf_op jit(solution)/shard_map/ppermute | solution.py:513
  873.9 5.3 convolution_convert_fusion.3
  879.2 5.3 convolution_convert_fusion.2
  895.0 6.3 collective-permute-start.89
  911.7 24.9 %collective-permute-done.90 = bf16[2,40,2304]{2,1,0:T(8,128)(2,1)S(1)} collective-permute-done((bf16[2,40,2304]{2,1,0:T(8,128)(2,1)S(1)}, bf16[2,40,2304]{2,1,0:T(8,128)(2,1)S(1)}, u32[]{:S(2)}, u32[]{:S(2)}) %collective-permute-start.90) | collective-permute-done | bytes 368672 | tf_op jit(solution)/shard_map/ppermute | solution.py:517
  958.9 6.1 convolution_convert_fusion.8
  978.6 8.9 collective-permute-done.92
  1006.0 7.4 collective-permute-done.100
  1013.3 24.9 %collective-permute-done.101 = bf16[2,40,2304]{2,1,0:T(8,128)(2,1)S(1)} collective-permute-done((bf16[2,40,2304]{2,1,0:T(8,128)(2,1)S(1)}, bf16[2,40,2304]{2,1,0:T(8,128)(2,1)S(1)}, u32[]{:S(2)}, u32[]{:S(2)}) %collective-permute-start.101) | collective-permute-done | bytes 368672 | tf_op jit(solution)/shard_map/ppermute | solution.py:517
  1045.6 6.3 convolution_convert_fusion
  1083.3 13.3 %collective-permute-done.104 = bf16[2,2,4,40,1152]{4,3,0,2,1:T(8,128)(2,1)} collective-permute-done((bf16[2,2,4,40,1152]{4,3,0,2,1:T(8,128)(2,1)}, bf16[2,2,4,40,1152]{4,3,0,2,1:T(8,128)(2,1)}, u32[]{:S(2)}, u32[]{:S(2)}) %collective-permute-start.104) | collective-permute-done | bytes 1474592 | tf_op jit(solution)/shard_map/ppermute | solution.py:513
  1098.2 6.2 collective-permute-done.103
  1113.2 10.4 collective-permute-done.106
  1150.6 22.8 %collective-permute-done.115 = bf16[2,40,2304]{2,1,0:T(8,128)(2,1)S(1)} collective-permute-done((bf16[2,40,2304]{2,1,0:T(8,128)(2,1)S(1)}, bf16[2,40,2304]{2,1,0:T(8,128)(2,1)S(1)}, u32[]{:S(2)}, u32[]{:S(2)}) %collective-permute-start.115) | collective-permute-done | bytes 368672 | tf_op jit(solution)/shard_map/ppermute | solution.py:517
  (1009 shorter events, 672.9 us)
Async XLA Ops:
  18.9 33.6 %collective-permute-start.5 = (bf16[1,40,4608]{2,1,0:T(8,128)(2,1)S(1)}, bf16[1,40,4608]{2,1,0:T(8,128)(2,1)S(1)}, u32[]{:S(2)}, u32[]{:S(2)}) collective-permute-start(bf16[1,40,4608]{2,1,0:T(8,128)(2,1)S(1)} %get-tuple-element.167), channel_id=1, source_target_pairs={{0,16},{8,24},{16,0},{24,8},{1,17},{9,25},{17,1},{25,9},{2,18},{10... | collective-permute-start | bytes 1105928 | tf_op jit(solution)/shard_map/ppermute | solution.py:517
  20.2 32.4 %collective-permute-start.6 = (bf16[1,40,4608]{2,1,0:T(8,128)(2,1)S(1)}, bf16[1,40,4608]{2,1,0:T(8,128)(2,1)S(1)}, u32[]{:S(2)}, u32[]{:S(2)}) collective-permute-start(bf16[1,40,4608]{2,1,0:T(8,128)(2,1)S(1)} %get-tuple-element.167), channel_id=1, source_target_pairs={{0,24},{8,0},{16,8},{24,16},{1,25},{9,1},{17,9},{25,17},{2,26},{10... | collective-permute-start | bytes 1105928 | tf_op jit(solution)/shard_map/ppermute | solution.py:517
  87.2 32.6 %collective-permute-start.15 = (bf16[8,40,2304]{2,1,0:T(8,128)(2,1)S(1)}, bf16[8,40,2304]{2,1,0:T(8,128)(2,1)S(1)}, u32[]{:S(2)}, u32[]{:S(2)}) collective-permute-start(bf16[8,40,2304]{2,1,0:T(8,128)(2,1)S(1)} %pad_maximum_fusion.15), channel_id=1, source_target_pairs={{0,2},{1,3},{2,0},{3,1},{4,6},{5,7},{6,4},{7,5},{8,10},{9,11},{10,... | collective-permute-start | bytes 4423688 | tf_op jit(solution)/shard_map/ppermute | solution.py:513
  90.7 31.9 %collective-permute-start.14 = (bf16[8,40,2304]{2,1,0:T(8,128)(2,1)S(1)}, bf16[8,40,2304]{2,1,0:T(8,128)(2,1)S(1)}, u32[]{:S(2)}, u32[]{:S(2)}) collective-permute-start(bf16[8,40,2304]{2,1,0:T(8,128)(2,1)S(1)} %pad_maximum_fusion.14), channel_id=1, source_target_pairs={{0,4},{1,5},{2,6},{3,7},{4,0},{5,1},{6,2},{7,3},{8,12},{9,13},{10,... | collective-permute-start | bytes 4423688 | tf_op jit(solution)/shard_map/ppermute | solution.py:513
  151.8 48.9 %collective-permute-start.24 = (bf16[8,40,2304]{2,1,0:T(8,128)(2,1)}, bf16[8,40,2304]{2,1,0:T(8,128)(2,1)}, u32[]{:S(2)}, u32[]{:S(2)}) collective-permute-start(bf16[8,40,2304]{2,1,0:T(8,128)(2,1)} %pad_maximum_fusion.17), channel_id=1, source_target_pairs={{0,2},{1,3},{2,0},{3,1},{4,6},{5,7},{6,4},{7,5},{8,10},{9,11},{10,... | collective-permute-start | bytes 4423688 | tf_op jit(solution)/shard_map/ppermute | solution.py:513
  153.3 49.7 %collective-permute-start.23 = (bf16[8,40,2304]{2,1,0:T(8,128)(2,1)}, bf16[8,40,2304]{2,1,0:T(8,128)(2,1)}, u32[]{:S(2)}, u32[]{:S(2)}) collective-permute-start(bf16[8,40,2304]{2,1,0:T(8,128)(2,1)} %pad_maximum_fusion.16), channel_id=1, source_target_pairs={{0,4},{1,5},{2,6},{3,7},{4,0},{5,1},{6,2},{7,3},{8,12},{9,13},{10,... | collective-permute-start | bytes 4423688 | tf_op jit(solution)/shard_map/ppermute | solution.py:513
  176.1 32.2 %collective-permute-start.27 = (bf16[4,40,2304]{2,1,0:T(8,128)(2,1)}, bf16[4,40,2304]{2,1,0:T(8,128)(2,1)}, u32[]{:S(2)}, u32[]{:S(2)}) collective-permute-start(bf16[4,40,2304]{2,1,0:T(8,128)(2,1)} %pad_maximum_fusion.40), channel_id=1, source_target_pairs={{0,2},{1,3},{2,0},{3,1},{4,6},{5,7},{6,4},{7,5},{8,10},{9,11},{10,... | collective-permute-start | bytes 2211848 | tf_op jit(solution)/shard_map/ppermute | solution.py:513
  225.3 28.6 %collective-permute-start.29 = (bf16[1,40,4608]{2,1,0:T(8,128)(2,1)S(1)}, bf16[1,40,4608]{2,1,0:T(8,128)(2,1)}, u32[]{:S(2)}, u32[]{:S(2)}) collective-permute-start(bf16[1,40,4608]{2,1,0:T(8,128)(2,1)S(1)} %get-tuple-element.221), channel_id=1, source_target_pairs={{0,8},{8,16},{16,24},{24,0},{1,9},{9,17},{17,25},{25,1},{2,10},{10... | collective-permute-start | bytes 1105928 | tf_op jit(solution)/shard_map/ppermute | solution.py:517
  250.4 47.8 %collective-permute-start.33 = (bf16[8,40,2304]{2,1,0:T(8,128)(2,1)}, bf16[8,40,2304]{2,1,0:T(8,128)(2,1)}, u32[]{:S(2)}, u32[]{:S(2)}) collective-permute-start(bf16[8,40,2304]{2,1,0:T(8,128)(2,1)} %pad_maximum_fusion.19), channel_id=1, source_target_pairs={{0,2},{1,3},{2,0},{3,1},{4,6},{5,7},{6,4},{7,5},{8,10},{9,11},{10,... | collective-permute-start | bytes 4423688 | tf_op jit(solution)/shard_map/ppermute | solution.py:513
  252.4 49.4 %collective-permute-start.32 = (bf16[8,40,2304]{2,1,0:T(8,128)(2,1)}, bf16[8,40,2304]{2,1,0:T(8,128)(2,1)}, u32[]{:S(2)}, u32[]{:S(2)}) collective-permute-start(bf16[8,40,2304]{2,1,0:T(8,128)(2,1)} %pad_maximum_fusion.18), channel_id=1, source_target_pairs={{0,4},{1,5},{2,6},{3,7},{4,0},{5,1},{6,2},{7,3},{8,12},{9,13},{10,... | collective-permute-start | bytes 4423688 | tf_op jit(solution)/shard_map/ppermute | solution.py:513
  305.6 28.5 %collective-permute-start.34 = (bf16[640,2304]{1,0:T(8,128)(2,1)}, bf16[640,2304]{1,0:T(8,128)(2,1)}, u32[]{:S(2)}, u32[]{:S(2)}) collective-permute-start(bf16[640,2304]{1,0:T(8,128)(2,1)} %bitcast.56), channel_id=1, source_target_pairs={{0,1},{1,0},{2,3},{3,2},{4,5},{5,4},{6,7},{7,6},{8,9},{9,8},{10,11... | collective-permute-start | bytes 8847368 | tf_op jit(solution)/shard_map/ppermute | solution.py:513
  305.6 28.6 %collective-permute-start.35 = (bf16[640,2304]{1,0:T(8,128)(2,1)}, bf16[640,2304]{1,0:T(8,128)(2,1)}, u32[]{:S(2)}, u32[]{:S(2)}) collective-permute-start(bf16[640,2304]{1,0:T(8,128)(2,1)} %bitcast.57), channel_id=1, source_target_pairs={{0,1},{1,0},{2,3},{3,2},{4,5},{5,4},{6,7},{7,6},{8,9},{9,8},{10,11... | collective-permute-start | bytes 8847368 | tf_op jit(solution)/shard_map/ppermute | solution.py:513
  349.5 831.0 %reduce-scatter.2.cloned.1.call-start = ((), (), s32[]{:S(2)}) async-start(), calls=%async_computation.5 | async-start | bytes 663552 | tf_op jit(solution)/shard_map/reduce_scatter | solution.py:980
  350.8 46.2 %collective-permute-start.42 = (bf16[8,40,2304]{2,1,0:T(8,128)(2,1)}, bf16[8,40,2304]{2,1,0:T(8,128)(2,1)}, u32[]{:S(2)}, u32[]{:S(2)}) collective-permute-start(bf16[8,40,2304]{2,1,0:T(8,128)(2,1)} %pad_maximum_fusion.21), channel_id=1, source_target_pairs={{0,2},{1,3},{2,0},{3,1},{4,6},{5,7},{6,4},{7,5},{8,10},{9,11},{10,... | collective-permute-start | bytes 4423688 | tf_op jit(solution)/shard_map/ppermute | solution.py:513
  352.7 46.8 %collective-permute-start.41 = (bf16[8,40,2304]{2,1,0:T(8,128)(2,1)}, bf16[8,40,2304]{2,1,0:T(8,128)(2,1)}, u32[]{:S(2)}, u32[]{:S(2)}) collective-permute-start(bf16[8,40,2304]{2,1,0:T(8,128)(2,1)} %pad_maximum_fusion.20), channel_id=1, source_target_pairs={{0,4},{1,5},{2,6},{3,7},{4,0},{5,1},{6,2},{7,3},{8,12},{9,13},{10,... | collective-permute-start | bytes 4423688 | tf_op jit(solution)/shard_map/ppermute | solution.py:513
  420.5 31.2 %collective-permute-start.48 = (bf16[4,2,1,1,72,1152]{5,4,3,2,1,0:T(8,128)(2,1)S(1)}, bf16[4,2,1,1,72,1152]{5,4,3,2,1,0:T(8,128)(2,1)S(1)}, u32[]{:S(2)}, u32[]{:S(2)}) collective-permute-start(bf16[4,2,1,1,72,1152]{5,4,3,2,1,0:T(8,128)(2,1)S(1)} %pad_maximum_fusion.29), channel_id=1, source_target_pairs={{0,2},{1,3},{2,0},{3,1},{4,6},{5,7},{6,4},{7,5},{8,10},{9,11},{10,... | collective-permute-start | bytes 3981320 | tf_op jit(solution)/shard_map/ppermute | solution.py:513
  422.2 31.5 %collective-permute-start.47 = (bf16[4,1,2,1,72,1152]{5,4,3,2,1,0:T(8,128)(2,1)S(1)}, bf16[4,1,2,1,72,1152]{5,4,3,2,1,0:T(8,128)(2,1)S(1)}, u32[]{:S(2)}, u32[]{:S(2)}) collective-permute-start(bf16[4,1,2,1,72,1152]{5,4,3,2,1,0:T(8,128)(2,1)S(1)} %pad_maximum_fusion.28), channel_id=1, source_target_pairs={{0,4},{1,5},{2,6},{3,7},{4,0},{5,1},{6,2},{7,3},{8,12},{9,13},{10,... | collective-permute-start | bytes 3981320 | tf_op jit(solution)/shard_map/ppermute | solution.py:513
  472.9 40.9 %collective-permute-start.81 = (bf16[512,1280]{1,0:T(8,128)(2,1)}, bf16[512,1280]{1,0:T(8,128)(2,1)}, u32[]{:S(2)}, u32[]{:S(2)}) collective-permute-start(bf16[512,1280]{1,0:T(8,128)(2,1)} %bitcast.186), channel_id=1, source_target_pairs={{0,1},{1,0},{2,3},{3,2},{4,5},{5,4},{6,7},{7,6},{8,9},{9,8},{10,11... | collective-permute-start | bytes 3932168 | tf_op jit(solution)/shard_map/ppermute | solution.py:513
  473.1 43.2 %collective-permute-start.61 = (bf16[512,1280]{1,0:T(8,128)(2,1)}, bf16[512,1280]{1,0:T(8,128)(2,1)}, u32[]{:S(2)}, u32[]{:S(2)}) collective-permute-start(bf16[512,1280]{1,0:T(8,128)(2,1)} %bitcast.143), channel_id=1, source_target_pairs={{0,1},{1,0},{2,3},{3,2},{4,5},{5,4},{6,7},{7,6},{8,9},{9,8},{10,11... | collective-permute-start | bytes 3932168 | tf_op jit(solution)/shard_map/ppermute | solution.py:513
  476.6 42.3 %collective-permute-start.53 = (bf16[512,1280]{1,0:T(8,128)(2,1)}, bf16[512,1280]{1,0:T(8,128)(2,1)}, u32[]{:S(2)}, u32[]{:S(2)}) collective-permute-start(bf16[512,1280]{1,0:T(8,128)(2,1)} %bitcast.109), channel_id=1, source_target_pairs={{0,1},{1,0},{2,3},{3,2},{4,5},{5,4},{6,7},{7,6},{8,9},{9,8},{10,11... | collective-permute-start | bytes 3932168 | tf_op jit(solution)/shard_map/ppermute | solution.py:513
  492.4 29.0 %collective-permute-start.62 = (bf16[512,1280]{1,0:T(8,128)(2,1)}, bf16[512,1280]{1,0:T(8,128)(2,1)S(1)}, u32[]{:S(2)}, u32[]{:S(2)}) collective-permute-start(bf16[512,1280]{1,0:T(8,128)(2,1)} %bitcast.144), channel_id=1, source_target_pairs={{0,1},{1,0},{2,3},{3,2},{4,5},{5,4},{6,7},{7,6},{8,9},{9,8},{10,11... | collective-permute-start | bytes 3932168 | tf_op jit(solution)/shard_map/ppermute | solution.py:513
  513.5 59.0 %collective-permute-start.54 = (bf16[512,4608]{1,0:T(8,128)(2,1)}, bf16[512,4608]{1,0:T(8,128)(2,1)}, u32[]{:S(2)}, u32[]{:S(2)}) collective-permute-start(bf16[512,4608]{1,0:T(8,128)(2,1)} %bitcast.110), channel_id=1, source_target_pairs={{0,1},{1,0},{2,3},{3,2},{4,5},{5,4},{6,7},{7,6},{8,9},{9,8},{10,11... | collective-permute-start | bytes 14155784 | tf_op jit(solution)/shard_map/ppermute | solution.py:513
  525.0 45.4 %collective-permute-start.55 = (bf16[4,2,2,144,384]{4,3,2,1,0:T(8,128)(2,1)}, bf16[4,2,2,144,384]{4,3,2,1,0:T(8,128)(2,1)}, u32[]{:S(2)}, u32[]{:S(2)}) collective-permute-start(bf16[4,2,2,144,384]{4,3,2,1,0:T(8,128)(2,1)} %dynamic-slice_bitcast_fusion), channel_id=1, source_target_pairs={{0,4},{1,5},{2,6},{3,7},{4,0},{5,1},{6,2},{7,3},{8,12},{9,13},{10,... | collective-permute-start | bytes 5308424 | tf_op jit(solution)/shard_map/ppermute | solution.py:513
  590.0 87.1 %collective-permute-start.60 = (bf16[2,2,4,40,1152]{4,3,0,2,1:T(8,128)(2,1)}, bf16[2,2,4,40,1152]{4,3,0,2,1:T(8,128)(2,1)}, u32[]{:S(2)}, u32[]{:S(2)}) collective-permute-start(bf16[2,2,4,40,1152]{4,3,0,2,1:T(8,128)(2,1)} %bitcast.806), channel_id=1, source_target_pairs={{0,2},{1,3},{2,0},{3,1},{4,6},{5,7},{6,4},{7,5},{8,10},{9,11},{10,... | collective-permute-start | bytes 4423688 | tf_op jit(solution)/shard_map/ppermute | solution.py:513
  593.9 84.9 %collective-permute-start.59 = (bf16[2,2,4,40,1152]{4,3,0,2,1:T(8,128)(2,1)}, bf16[2,2,4,40,1152]{4,3,0,2,1:T(8,128)(2,1)}, u32[]{:S(2)}, u32[]{:S(2)}) collective-permute-start(bf16[2,2,4,40,1152]{4,3,0,2,1:T(8,128)(2,1)} %bitcast.807), channel_id=1, source_target_pairs={{0,4},{1,5},{2,6},{3,7},{4,0},{5,1},{6,2},{7,3},{8,12},{9,13},{10,... | collective-permute-start | bytes 4423688 | tf_op jit(solution)/shard_map/ppermute | solution.py:513
  595.9 47.0 %collective-permute-start.57 = (bf16[4,2,144,384]{3,2,1,0:T(8,128)(2,1)}, bf16[4,2,144,384]{3,2,1,0:T(8,128)(2,1)}, u32[]{:S(2)}, u32[]{:S(2)}) collective-permute-start(bf16[4,2,144,384]{3,2,1,0:T(8,128)(2,1)} %dynamic-slice_bitcast_fusion.2), channel_id=1, source_target_pairs={{0,2},{1,3},{2,0},{3,1},{4,6},{5,7},{6,4},{7,5},{8,10},{9,11},{10,... | collective-permute-start | bytes 2654216 | tf_op jit(solution)/shard_map/ppermute | solution.py:513
  597.7 42.2 %collective-permute-start.58 = (bf16[4,2,144,256]{3,2,1,0:T(8,128)(2,1)}, bf16[4,2,144,256]{3,2,1,0:T(8,128)(2,1)}, u32[]{:S(2)}, u32[]{:S(2)}) collective-permute-start(bf16[4,2,144,256]{3,2,1,0:T(8,128)(2,1)} %dynamic-slice_bitcast_fusion.3), channel_id=1, source_target_pairs={{0,4},{1,5},{2,6},{3,7},{4,0},{5,1},{6,2},{7,3},{8,12},{9,13},{10,... | collective-permute-start | bytes 1769480 | tf_op jit(solution)/shard_map/ppermute | solution.py:513
  662.9 56.4 %collective-permute-start.64 = (bf16[512,1152]{1,0:T(8,128)(2,1)}, bf16[512,1152]{1,0:T(8,128)(2,1)}, u32[]{:S(2)}, u32[]{:S(2)}) collective-permute-start(bf16[512,1152]{1,0:T(8,128)(2,1)} %get-tuple-element.400), channel_id=1, source_target_pairs={{0,1},{1,0},{2,3},{3,2},{4,5},{5,4},{6,7},{7,6},{8,9},{9,8},{10,11... | collective-permute-start | bytes 3538952 | tf_op jit(solution)/shard_map/ppermute | solution.py:513
  732.4 104.5 %collective-permute-start.77 = (bf16[2,2,4,40,1152]{4,3,0,2,1:T(8,128)(2,1)}, bf16[2,2,4,40,1152]{4,3,0,2,1:T(8,128)(2,1)}, u32[]{:S(2)}, u32[]{:S(2)}) collective-permute-start(bf16[2,2,4,40,1152]{4,3,0,2,1:T(8,128)(2,1)} %bitcast.804), channel_id=1, source_target_pairs={{0,2},{1,3},{2,0},{3,1},{4,6},{5,7},{6,4},{7,5},{8,10},{9,11},{10,... | collective-permute-start | bytes 4423688 | tf_op jit(solution)/shard_map/ppermute | solution.py:513
  736.1 102.5 %collective-permute-start.76 = (bf16[2,2,4,40,1152]{4,3,0,2,1:T(8,128)(2,1)}, bf16[2,2,4,40,1152]{4,3,0,2,1:T(8,128)(2,1)}, u32[]{:S(2)}, u32[]{:S(2)}) collective-permute-start(bf16[2,2,4,40,1152]{4,3,0,2,1:T(8,128)(2,1)} %bitcast.805), channel_id=1, source_target_pairs={{0,4},{1,5},{2,6},{3,7},{4,0},{5,1},{6,2},{7,3},{8,12},{9,13},{10,... | collective-permute-start | bytes 4423688 | tf_op jit(solution)/shard_map/ppermute | solution.py:513
  744.1 36.6 %collective-permute-start.74 = (bf16[2,40,2304]{2,1,0:T(8,128)(2,1)}, bf16[2,40,2304]{2,1,0:T(8,128)(2,1)}, u32[]{:S(2)}, u32[]{:S(2)}) collective-permute-start(bf16[2,40,2304]{2,1,0:T(8,128)(2,1)} %get-tuple-element.454), channel_id=1, source_target_pairs={{0,16},{8,24},{16,0},{24,8},{1,17},{9,25},{17,1},{25,9},{2,18},{10... | collective-permute-start | bytes 1105928 | tf_op jit(solution)/shard_map/ppermute | solution.py:517
  750.0 34.0 %all-to-all-start.2 = ((bf16[1,2,256,1152]{3,1,0,2:T(2,128)(2,1)}), bf16[1,2,256,1152]{3,1,0,2:T(2,128)(2,1)}, u32[]{:S(2)}, u32[]{:S(2)}) async-start(bf16[1,2,256,1152]{3,1,0,2:T(2,128)(2,1)} %copy.230), calls=%async_computation.2 | async-start | bytes 2359296 | tf_op jit(solution)/shard_map/all_to_all | solution.py:912
  836.6 42.6 %collective-permute-start.83 = (bf16[512,1152]{1,0:T(8,128)(2,1)}, bf16[512,1152]{1,0:T(8,128)(2,1)S(1)}, u32[]{:S(2)}, u32[]{:S(2)}) collective-permute-start(bf16[512,1152]{1,0:T(8,128)(2,1)} %bitcast.903), channel_id=1, source_target_pairs={{0,1},{1,0},{2,3},{3,2},{4,5},{5,4},{6,7},{7,6},{8,9},{9,8},{10,11... | collective-permute-start | bytes 3538952 | tf_op jit(solution)/shard_map/ppermute | solution.py:513
  849.6 29.6 %collective-permute-start.82 = (bf16[512,1152]{1,0:T(8,128)(2,1)S(1)}, bf16[512,1152]{1,0:T(8,128)(2,1)S(1)}, u32[]{:S(2)}, u32[]{:S(2)}) collective-permute-start(bf16[512,1152]{1,0:T(8,128)(2,1)S(1)} %bitcast.899), channel_id=1, source_target_pairs={{0,1},{1,0},{2,3},{3,2},{4,5},{5,4},{6,7},{7,6},{8,9},{9,8},{10,11... | collective-permute-start | bytes 3538952 | tf_op jit(solution)/shard_map/ppermute | solution.py:513
  887.1 67.4 %collective-permute-start.88 = (bf16[2,2,4,40,1152]{4,3,0,2,1:T(8,128)(2,1)}, bf16[2,2,4,40,1152]{4,3,0,2,1:T(8,128)(2,1)}, u32[]{:S(2)}, u32[]{:S(2)}) collective-permute-start(bf16[2,2,4,40,1152]{4,3,0,2,1:T(8,128)(2,1)} %bitcast.802), channel_id=1, source_target_pairs={{0,2},{1,3},{2,0},{3,1},{4,6},{5,7},{6,4},{7,5},{8,10},{9,11},{10,... | collective-permute-start | bytes 4423688 | tf_op jit(solution)/shard_map/ppermute | solution.py:513
  891.3 46.3 %all-to-all-start.3 = ((bf16[1,16,32,1152]{3,2,0,1:T(8,128)(2,1)}), bf16[1,16,32,1152]{3,2,0,1:T(8,128)(2,1)S(1)}, u32[]{:S(2)}, u32[]{:S(2)}) async-start(bf16[1,16,32,1152]{3,2,0,1:T(8,128)(2,1)} %bitcast.912), calls=%async_computation.3 | async-start | bytes 2359296 | tf_op jit(solution)/shard_map/all_to_all | solution.py:938
  901.3 35.3 %collective-permute-start.90 = (bf16[2,40,2304]{2,1,0:T(8,128)(2,1)S(1)}, bf16[2,40,2304]{2,1,0:T(8,128)(2,1)S(1)}, u32[]{:S(2)}, u32[]{:S(2)}) collective-permute-start(bf16[2,40,2304]{2,1,0:T(8,128)(2,1)S(1)} %get-tuple-element.451), channel_id=1, source_target_pairs={{0,16},{8,24},{16,0},{24,8},{1,17},{9,25},{17,1},{25,9},{2,18},{10... | collective-permute-start | bytes 1105928 | tf_op jit(solution)/shard_map/ppermute | solution.py:517
  904.0 32.6 %collective-permute-start.91 = (bf16[2,40,2304]{2,1,0:T(8,128)(2,1)S(1)}, bf16[2,40,2304]{2,1,0:T(8,128)(2,1)S(1)}, u32[]{:S(2)}, u32[]{:S(2)}) collective-permute-start(bf16[2,40,2304]{2,1,0:T(8,128)(2,1)S(1)} %get-tuple-element.450), channel_id=1, source_target_pairs={{0,8},{8,16},{16,24},{24,0},{1,9},{9,17},{17,25},{25,1},{2,10},{10... | collective-permute-start | bytes 1105928 | tf_op jit(solution)/shard_map/ppermute | solution.py:517
  908.5 48.3 %collective-permute-start.87 = (bf16[2,2,4,40,1152]{4,3,0,2,1:T(8,128)(2,1)}, bf16[2,2,4,40,1152]{4,3,0,2,1:T(8,128)(2,1)}, u32[]{:S(2)}, u32[]{:S(2)}) collective-permute-start(bf16[2,2,4,40,1152]{4,3,0,2,1:T(8,128)(2,1)} %bitcast.803), channel_id=1, source_target_pairs={{0,4},{1,5},{2,6},{3,7},{4,0},{5,1},{6,2},{7,3},{8,12},{9,13},{10,... | collective-permute-start | bytes 4423688 | tf_op jit(solution)/shard_map/ppermute | solution.py:513
  943.2 102.3 %collective-permute-start.99 = (bf16[512,1152]{1,0:T(8,128)(2,1)}, bf16[512,1152]{1,0:T(8,128)(2,1)}, u32[]{:S(2)}, u32[]{:S(2)}) collective-permute-start(bf16[512,1152]{1,0:T(8,128)(2,1)} %get-tuple-element.403), channel_id=1, source_target_pairs={{0,1},{1,0},{2,3},{3,2},{4,5},{5,4},{6,7},{7,6},{8,9},{9,8},{10,11... | collective-permute-start | bytes 3538952 | tf_op jit(solution)/shard_map/ppermute | solution.py:513
  994.5 51.0 %collective-permute-start.98 = (bf16[512,1152]{1,0:T(8,128)(2,1)}, bf16[512,1152]{1,0:T(8,128)(2,1)}, u32[]{:S(2)}, u32[]{:S(2)}) collective-permute-start(bf16[512,1152]{1,0:T(8,128)(2,1)} %bitcast.906), channel_id=1, source_target_pairs={{0,1},{1,0},{2,3},{3,2},{4,5},{5,4},{6,7},{7,6},{8,9},{9,8},{10,11... | collective-permute-start | bytes 3538952 | tf_op jit(solution)/shard_map/ppermute | solution.py:513
  1002.8 35.4 %collective-permute-start.101 = (bf16[2,40,2304]{2,1,0:T(8,128)(2,1)S(1)}, bf16[2,40,2304]{2,1,0:T(8,128)(2,1)S(1)}, u32[]{:S(2)}, u32[]{:S(2)}) collective-permute-start(bf16[2,40,2304]{2,1,0:T(8,128)(2,1)S(1)} %get-tuple-element.448), channel_id=1, source_target_pairs={{0,16},{8,24},{16,0},{24,8},{1,17},{9,25},{17,1},{25,9},{2,18},{10... | collective-permute-start | bytes 1105928 | tf_op jit(solution)/shard_map/ppermute | solution.py:517
  1005.5 32.7 %collective-permute-start.102 = (bf16[2,40,2304]{2,1,0:T(8,128)(2,1)S(1)}, bf16[2,40,2304]{2,1,0:T(8,128)(2,1)S(1)}, u32[]{:S(2)}, u32[]{:S(2)}) collective-permute-start(bf16[2,40,2304]{2,1,0:T(8,128)(2,1)S(1)} %get-tuple-element.447), channel_id=1, source_target_pairs={{0,8},{8,16},{16,24},{24,0},{1,9},{9,17},{17,25},{25,1},{2,10},{10... | collective-permute-start | bytes 1105928 | tf_op jit(solution)/shard_map/ppermute | solution.py:517
  1061.9 34.6 %collective-permute-start.104 = (bf16[2,2,4,40,1152]{4,3,0,2,1:T(8,128)(2,1)}, bf16[2,2,4,40,1152]{4,3,0,2,1:T(8,128)(2,1)}, u32[]{:S(2)}, u32[]{:S(2)}) collective-permute-start(bf16[2,2,4,40,1152]{4,3,0,2,1:T(8,128)(2,1)} %bitcast.800), channel_id=1, source_target_pairs={{0,2},{1,3},{2,0},{3,1},{4,6},{5,7},{6,4},{7,5},{8,10},{9,11},{10,... | collective-permute-start | bytes 4423688 | tf_op jit(solution)/shard_map/ppermute | solution.py:513
  1070.1 34.4 %collective-permute-start.103 = (bf16[2,2,4,40,1152]{4,3,0,2,1:T(8,128)(2,1)}, bf16[2,2,4,40,1152]{4,3,0,2,1:T(8,128)(2,1)}, u32[]{:S(2)}, u32[]{:S(2)}) collective-permute-start(bf16[2,2,4,40,1152]{4,3,0,2,1:T(8,128)(2,1)} %bitcast.801), channel_id=1, source_target_pairs={{0,4},{1,5},{2,6},{3,7},{4,0},{5,1},{6,2},{7,3},{8,12},{9,13},{10,... | collective-permute-start | bytes 4423688 | tf_op jit(solution)/shard_map/ppermute | solution.py:513
  1136.1 37.3 %collective-permute-start.115 = (bf16[2,40,2304]{2,1,0:T(8,128)(2,1)S(1)}, bf16[2,40,2304]{2,1,0:T(8,128)(2,1)S(1)}, u32[]{:S(2)}, u32[]{:S(2)}) collective-permute-start(bf16[2,40,2304]{2,1,0:T(8,128)(2,1)S(1)} %get-tuple-element.445), channel_id=1, source_target_pairs={{0,16},{8,24},{16,0},{24,8},{1,17},{9,25},{17,1},{25,9},{2,18},{10... | collective-permute-start | bytes 1105928 | tf_op jit(solution)/shard_map/ppermute | solution.py:517
  1136.2 37.2 %collective-permute-start.116 = (bf16[2,40,2304]{2,1,0:T(8,128)(2,1)S(1)}, bf16[2,40,2304]{2,1,0:T(8,128)(2,1)S(1)}, u32[]{:S(2)}, u32[]{:S(2)}) collective-permute-start(bf16[2,40,2304]{2,1,0:T(8,128)(2,1)S(1)} %get-tuple-element.444), channel_id=1, source_target_pairs={{0,8},{8,16},{16,24},{24,0},{1,9},{9,17},{17,25},{25,1},{2,10},{10... | collective-permute-start | bytes 1105928 | tf_op jit(solution)/shard_map/ppermute | solution.py:517
  1146.2 29.5 %collective-permute-start.112 = (f32[1,20,1152]{2,1,0:T(8,128)S(1)}, f32[1,20,1152]{2,1,0:T(8,128)S(1)}, u32[]{:S(2)}, u32[]{:S(2)}) collective-permute-start(f32[1,20,1152]{2,1,0:T(8,128)S(1)} %bitcast.919), channel_id=1, source_target_pairs={{0,16},{8,24},{16,0},{24,8},{1,17},{9,25},{17,1},{25,9},{2,18},{10... | collective-permute-start | bytes 276488 | tf_op jit(solution)/shard_map/ppermute | solution.py:517
  (284 other events, 3707.8 us)
Sparse Core Ops, SparseCore 0:
  704.4 40.6 reduce-scatter.1

commit v4 on v3

--- a/solution.py
+++ b/solution.py
@@ -861,6 +861,10 @@
     def choose(low, high):
         return jnp.where(k == 0, low, high)
 
+    def pair_half(low, high):
+        low, high = (part.reshape(-1, part.shape[-1]) for part in (low, high))
+        return jnp.concatenate([choose(low, high), swap(choose(high, low), "k")], axis=0)
+
     def sums_of(left, right):
         return lax.dot_general(left, right, (((0,), (0,)), ((), ())), preferred_element_type=jnp.float32).astype(
             jnp.bfloat16
@@ -868,15 +872,14 @@
 
     grad_mlp = (out_rows * gate_two).astype(jnp.bfloat16)
     grad_gate_two = jnp.sum(out_rows * mlp_branch, axis=1)
-    pair_mlp = pair(grad_mlp)
-    sum_out = sums_of(pair(gelu_out), choose(pair_mlp[:, :640], pair_mlp[:, 512:]))
+    mlp_rows = grad_mlp.reshape(rows, width)
+    sum_out = sums_of(pair(gelu_out), pair_half(mlp_rows[:, :640], mlp_rows[:, 512:]))
     bias_out = column_sum(grad_mlp)
     grad_gelu, sum_out = lax.optimization_barrier((product_back(grad_mlp, w_out), sum_out))
     own_out = mover.add(scatter_out_steps(at), sum_out)
     gelu_pull = jax.vjp(partial(jax.nn.gelu, approximate=True), inner_act)[1]
     grad_inner = mover.tick(gelu_pull(grad_gelu)[0].astype(jnp.bfloat16))
-    pair_inner = pair(grad_inner)
-    pair_two, inner_half = pair_packed(normed_two), choose(pair_inner[:, :HALF], pair_inner[:, HALF:])
+    pair_two, inner_half = pair_packed(normed_two), pair_half(grad_inner[..., :HALF], grad_inner[..., HALF:])
     sum_in = (sums_of(pair_two, inner_half[:, :width]), sums_of(pair_two, inner_half[:, width:]))
     bias_in = column_sum(grad_inner)
     norm_pull = jax.vjp(modulate, hidden_three, mod_table[:, 3], mod_table[:, 4])[1]
@@ -902,8 +905,8 @@
     bias_cvalue = column_sum(grad_value)
     text_part = unpacked_float(packed_back(grad_key, w_ckey) + packed_back(grad_value, w_cvalue))
     text_two = jnp.concatenate([text_packed[0], text_packed[0]], axis=0)
-    sum_kv = sums_of(text_two, choose(pair(grad_key), pair(grad_value)))
-    sum_side = sums_of(choose(pair_packed(cross_in), pair_packed(c_flat)), choose(pair(grad_cquery), pair(grad_cross)))
+    sum_kv = sums_of(text_two, pair_half(grad_key, grad_value))
+    sum_side = sums_of(choose(pair_packed(cross_in), pair_packed(c_flat)), pair_half(grad_cquery, grad_cross))
     sum_cross = (choose(sum_side, sum_kv), choose(sum_kv, sum_side))
     grad_temporal = (grad_two * gate_one).astype(jnp.bfloat16).reshape(1, frame_count, patch_count, width)
     grad_temporal, sum_cross = mover.tick((grad_temporal, sum_cross))
@@ -917,8 +920,8 @@
     def stage_sums(grads, inputs, flat, proj_grad, task):
         query, key, value = mover.tick(tuple(merge_heads(part).astype(jnp.bfloat16) for part in grads))
         pair_in = pair_packed(inputs)
-        low = sums_of(pair_in, choose(pair(query), pair(value)))
-        high = sums_of(choose(pair_in, pair_packed(flat)), choose(pair(key), pair(proj_grad)))
+        low = sums_of(pair_in, pair_half(query, value))
+        high = sums_of(choose(pair_in, pair_packed(flat)), pair_half(key, proj_grad))
         w_low, w_high = task.state
         if task is s_task:
             query, key, value, low, high = lax.optimization_barrier((query, key, value, low, high))

time: 1200 us -> 1200 us (level)
    ppermute x83 -> x77, waiting for transfers between devices: 180 us -> 186 us  [swap(): return lax.ppermute(arr, 'seq', SWAP[axis])]
    unnamed x435 -> x437, local copies, waits for them, and re-layouts: 34.7 us -> 36.4 us
    ppermute x83 -> x77, starting transfers between devices: 62.9 us -> 63 us  [swap(): return lax.ppermute(arr, 'seq', SWAP[axis])]
  transfers between devices with their start and end apart: 124 -> 118, of which waited for: 52 -> 49; matrix products, arithmetic and copies ran while one was open for 49% -> 45% of each run, Pallas kernels for 0% -> 0%
where the time goes in v4:
time: 1200 us; the launch traced here: 1190 us
  waiting for transfers between devices  387 us (32%)
  matrix products  302 us (25%)
  local copies, waits for them, and re-layouts  177 us (15%)
  starting transfers between devices  159 us (13%)
  other arithmetic  143 us (12%)
  between operations  19 us (2%)
    ppermute x36, waiting for transfers between devices, turn(): return lax.ppermute(arr, 'clip', [(i, (i + d) % 4) for i in range(4)])  194 us
    ppermute x77, waiting for transfers between devices, swap(): return lax.ppermute(arr, 'seq', SWAP[axis])  186 us
    dot_general x34, matrix products, product(): lax.dot_general(left_arr, right_arr, (((left_arr.ndim - 1,), (0,)), ((),...  92.8 us
    ppermute x36, starting transfers between devices, turn(): return lax.ppermute(arr, 'clip', [(i, (i + d) % 4) for i in range(4)])  78.8 us
    dot_general x25, matrix products, product_back(): lax.dot_general(grad_arr, weight, (((grad_arr.ndim - 1,), (1,)), ((), ())...  76.6 us
    ppermute x77, starting transfers between devices, swap(): return lax.ppermute(arr, 'seq', SWAP[axis])  63 us
    dot_general x9, matrix products, sums_of(): lax.dot_general(left, right, (((0,), (0,)), ((), ())), preferred_element_...  57.8 us
    unnamed x437, local copies, waits for them, and re-layouts  36.4 us
  transfers between devices with their start and end apart: 118, of which 49 were waited for; matrix products, arithmetic and copies ran while one was open for 45% of the time, Pallas kernels for 0%

profile of v4, /device:TPU:0, one launch (start us, length us, event | category | flops | bytes accessed | tf_op | source)
XLA Modules:
  0.0 1187.5 jit_solution(10133015848047570003)
XLA Ops:
  26.0 7.1 collective-permute-done.2
  34.6 17.4 %collective-permute-done.5 = bf16[1,40,4608]{2,1,0:T(8,128)(2,1)S(1)} collective-permute-done((bf16[1,40,4608]{2,1,0:T(8,128)(2,1)S(1)}, bf16[1,40,4608]{2,1,0:T(8,128)(2,1)S(1)}, u32[]{:S(2)}, u32[]{:S(2)}) %collective-permute-start.5) | collective-permute-done | bytes 368672 | tf_op jit(solution)/shard_map/ppermute | solution.py:517
  55.9 17.9 %collective-permute-done.7 = f32[26,1152]{1,0:T(8,128)S(1)} collective-permute-done((f32[26,1152]{1,0:T(8,128)S(1)}, f32[26,1152]{1,0:T(8,128)S(1)}, u32[]{:S(2)}, u32[]{:S(2)}) %collective-permute-start.7) | collective-permute-done | bytes 119840 | tf_op jit(solution)/shard_map/ppermute | solution.py:513
  74.0 8.5 collective-permute-start.11
  92.2 13.1 %collective-permute-done.12 = bf16[1,40,4608]{2,1,0:T(8,128)(2,1)S(1)} collective-permute-done((bf16[1,40,4608]{2,1,0:T(8,128)(2,1)S(1)}, bf16[1,40,4608]{2,1,0:T(8,128)(2,1)S(1)}, u32[]{:S(2)}, u32[]{:S(2)}) %collective-permute-start.12) | collective-permute-done | bytes 368672 | tf_op jit(solution)/shard_map/ppermute | solution.py:517
  105.7 13.5 %collective-permute-done.15 = bf16[8,40,2304]{2,1,0:T(8,128)(2,1)S(1)} collective-permute-done((bf16[8,40,2304]{2,1,0:T(8,128)(2,1)S(1)}, bf16[8,40,2304]{2,1,0:T(8,128)(2,1)S(1)}, u32[]{:S(2)}, u32[]{:S(2)}) %collective-permute-start.15) | collective-permute-done | bytes 1474592 | tf_op jit(solution)/shard_map/ppermute | solution.py:513
  131.9 11.7 collective-permute-done.18
  158.4 14.0 %collective-permute-done.21 = bf16[1,40,4608]{2,1,0:T(8,128)(2,1)S(1)} collective-permute-done((bf16[1,40,4608]{2,1,0:T(8,128)(2,1)S(1)}, bf16[1,40,4608]{2,1,0:T(8,128)(2,1)S(1)}, u32[]{:S(2)}, u32[]{:S(2)}) %collective-permute-start.21) | collective-permute-done | bytes 368672 | tf_op jit(solution)/shard_map/ppermute | solution.py:517
  223.7 7.5 collective-permute-start.29
  259.1 5.8 all-to-all-done
  284.8 5.7 reshape.1822
  290.5 5.8 reshape.1820
  296.3 5.7 reshape.1821
  316.6 5.3 multiply_reduce_fusion.4
  384.5 16.8 %collective-permute-done.42 = bf16[8,40,2304]{2,1,0:T(8,128)(2,1)} collective-permute-done((bf16[8,40,2304]{2,1,0:T(8,128)(2,1)}, bf16[8,40,2304]{2,1,0:T(8,128)(2,1)}, u32[]{:S(2)}, u32[]{:S(2)}) %collective-permute-start.42) | collective-permute-done | bytes 1474592 | tf_op jit(solution)/shard_map/ppermute | solution.py:513
  413.8 9.6 collective-permute-done.45
  448.6 7.1 collective-permute-done.48
  480.4 6.9 maximum_maximum_fusion
  487.3 12.9 %convolution_bitcast_fusion = f32[1,512,4608]{2,1,0:T(8,128)} fusion(bf16[512,1152]{1,0:T(8,128)(2,1)S(1)} %fusion.182, bf16[4608,1152]{1,0:T(8,128)(2,1)} %bitcast.867), kind=kOutput, calls=%fused_computation.21 | convolution fusion | flops 5435817984 | bytes 21233664 | tf_op jit(solution)/shard_map/dot_general | solution.py:29
  500.3 10.4 fusion.11
  510.6 8.7 fusion.6
  542.6 19.3 %collective-permute-done.56 = bf16[4,2,2,144,256]{4,3,2,1,0:T(8,128)(2,1)} collective-permute-done((bf16[4,2,2,144,256]{4,3,2,1,0:T(8,128)(2,1)S(1)}, bf16[4,2,2,144,256]{4,3,2,1,0:T(8,128)(2,1)}, u32[]{:S(2)}, u32[]{:S(2)}) %collective-permute-start.56) | collective-permute-done | bytes 1179680 | tf_op jit(solution)/shard_map/ppermute | solution.py:513
  563.4 8.9 collective-permute-done.55
  574.1 9.8 convolution_convert_fusion.6
  604.2 10.0 fusion.183
  628.8 12.2 %collective-permute-done.58 = bf16[4,2,144,256]{3,2,1,0:T(8,128)(2,1)} collective-permute-done((bf16[4,2,144,256]{3,2,1,0:T(8,128)(2,1)}, bf16[4,2,144,256]{3,2,1,0:T(8,128)(2,1)}, u32[]{:S(2)}, u32[]{:S(2)}) %collective-permute-start.58) | collective-permute-done | bytes 589856 | tf_op jit(solution)/shard_map/ppermute | solution.py:513
  656.9 7.9 collective-permute-done.65
  664.7 13.7 %collective-permute-done.66 = bf16[2,144,640]{2,1,0:T(8,128)(2,1)S(1)} collective-permute-done((bf16[2,144,640]{2,1,0:T(8,128)(2,1)S(1)}, bf16[2,144,640]{2,1,0:T(8,128)(2,1)S(1)}, u32[]{:S(2)}, u32[]{:S(2)}) %collective-permute-start.66) | collective-permute-done | bytes 368672 | tf_op jit(solution)/shard_map/ppermute | solution.py:517
  711.4 5.2 multiply_convert_fusion.9
  738.7 7.1 collective-permute-start.71
  756.6 25.0 %collective-permute-done.72 = bf16[2,40,2304]{2,1,0:T(8,128)(2,1)} collective-permute-done((bf16[2,40,2304]{2,1,0:T(8,128)(2,1)}, bf16[2,40,2304]{2,1,0:T(8,128)(2,1)}, u32[]{:S(2)}, u32[]{:S(2)}) %collective-permute-start.72) | collective-permute-done | bytes 368672 | tf_op jit(solution)/shard_map/ppermute | solution.py:517
  792.0 6.3 reshape.1871
  798.3 8.9 multiply_reduce_fusion.2
  856.6 13.1 %collective-permute-done.81 = bf16[2,4,40,1152]{3,2,0,1:T(8,128)(2,1)S(1)} collective-permute-done((bf16[2,4,40,1152]{3,2,0,1:T(8,128)(2,1)S(1)}, bf16[2,4,40,1152]{3,2,0,1:T(8,128)(2,1)S(1)}, u32[]{:S(2)}, u32[]{:S(2)}) %collective-permute-start.81) | collective-permute-done | bytes 737312 | tf_op jit(solution)/shard_map/ppermute | solution.py:513
  871.3 6.7 convolution_convert_fusion.3
  877.9 5.2 convolution_convert_fusion.2
  893.6 7.3 collective-permute-start.85
  910.6 24.9 %collective-permute-done.86 = bf16[2,40,2304]{2,1,0:T(8,128)(2,1)S(1)} collective-permute-done((bf16[2,40,2304]{2,1,0:T(8,128)(2,1)S(1)}, bf16[2,40,2304]{2,1,0:T(8,128)(2,1)S(1)}, u32[]{:S(2)}, u32[]{:S(2)}) %collective-permute-start.86) | collective-permute-done | bytes 368672 | tf_op jit(solution)/shard_map/ppermute | solution.py:517
  956.8 6.2 convolution_convert_fusion.8
  976.6 8.0 collective-permute-done.88
  1005.6 7.6 collective-permute-done.94
  1013.2 22.8 %collective-permute-done.95 = bf16[2,40,2304]{2,1,0:T(8,128)(2,1)S(1)} collective-permute-done((bf16[2,40,2304]{2,1,0:T(8,128)(2,1)S(1)}, bf16[2,40,2304]{2,1,0:T(8,128)(2,1)S(1)}, u32[]{:S(2)}, u32[]{:S(2)}) %collective-permute-start.95) | collective-permute-done | bytes 368672 | tf_op jit(solution)/shard_map/ppermute | solution.py:517
  1037.1 8.0 convolution_convert_fusion.1
  1045.2 5.4 convolution_convert_fusion
  1082.1 12.4 %collective-permute-done.98 = bf16[2,2,4,40,1152]{4,3,0,2,1:T(8,128)(2,1)} collective-permute-done((bf16[2,2,4,40,1152]{4,3,0,2,1:T(8,128)(2,1)}, bf16[2,2,4,40,1152]{4,3,0,2,1:T(8,128)(2,1)}, u32[]{:S(2)}, u32[]{:S(2)}) %collective-permute-start.98) | collective-permute-done | bytes 1474592 | tf_op jit(solution)/shard_map/ppermute | solution.py:513
  1096.1 6.0 collective-permute-done.97
  1111.5 8.8 collective-permute-done.100
  1149.2 24.0 %collective-permute-done.109 = bf16[2,40,2304]{2,1,0:T(8,128)(2,1)S(1)} collective-permute-done((bf16[2,40,2304]{2,1,0:T(8,128)(2,1)S(1)}, bf16[2,40,2304]{2,1,0:T(8,128)(2,1)S(1)}, u32[]{:S(2)}, u32[]{:S(2)}) %collective-permute-start.109) | collective-permute-done | bytes 368672 | tf_op jit(solution)/shard_map/ppermute | solution.py:517
  (1005 shorter events, 656.7 us)
Async XLA Ops:
  18.3 33.6 %collective-permute-start.5 = (bf16[1,40,4608]{2,1,0:T(8,128)(2,1)S(1)}, bf16[1,40,4608]{2,1,0:T(8,128)(2,1)S(1)}, u32[]{:S(2)}, u32[]{:S(2)}) collective-permute-start(bf16[1,40,4608]{2,1,0:T(8,128)(2,1)S(1)} %get-tuple-element.167), channel_id=1, source_target_pairs={{0,16},{8,24},{16,0},{24,8},{1,17},{9,25},{17,1},{25,9},{2,18},{10... | collective-permute-start | bytes 1105928 | tf_op jit(solution)/shard_map/ppermute | solution.py:517
  19.6 32.4 %collective-permute-start.6 = (bf16[1,40,4608]{2,1,0:T(8,128)(2,1)S(1)}, bf16[1,40,4608]{2,1,0:T(8,128)(2,1)S(1)}, u32[]{:S(2)}, u32[]{:S(2)}) collective-permute-start(bf16[1,40,4608]{2,1,0:T(8,128)(2,1)S(1)} %get-tuple-element.167), channel_id=1, source_target_pairs={{0,24},{8,0},{16,8},{24,16},{1,25},{9,1},{17,9},{25,17},{2,26},{10... | collective-permute-start | bytes 1105928 | tf_op jit(solution)/shard_map/ppermute | solution.py:517
  86.6 32.6 %collective-permute-start.15 = (bf16[8,40,2304]{2,1,0:T(8,128)(2,1)S(1)}, bf16[8,40,2304]{2,1,0:T(8,128)(2,1)S(1)}, u32[]{:S(2)}, u32[]{:S(2)}) collective-permute-start(bf16[8,40,2304]{2,1,0:T(8,128)(2,1)S(1)} %pad_maximum_fusion.16), channel_id=1, source_target_pairs={{0,2},{1,3},{2,0},{3,1},{4,6},{5,7},{6,4},{7,5},{8,10},{9,11},{10,... | collective-permute-start | bytes 4423688 | tf_op jit(solution)/shard_map/ppermute | solution.py:513
  90.1 31.9 %collective-permute-start.14 = (bf16[8,40,2304]{2,1,0:T(8,128)(2,1)S(1)}, bf16[8,40,2304]{2,1,0:T(8,128)(2,1)S(1)}, u32[]{:S(2)}, u32[]{:S(2)}) collective-permute-start(bf16[8,40,2304]{2,1,0:T(8,128)(2,1)S(1)} %pad_maximum_fusion.15), channel_id=1, source_target_pairs={{0,4},{1,5},{2,6},{3,7},{4,0},{5,1},{6,2},{7,3},{8,12},{9,13},{10,... | collective-permute-start | bytes 4423688 | tf_op jit(solution)/shard_map/ppermute | solution.py:513
  150.2 48.9 %collective-permute-start.24 = (bf16[8,40,2304]{2,1,0:T(8,128)(2,1)}, bf16[8,40,2304]{2,1,0:T(8,128)(2,1)}, u32[]{:S(2)}, u32[]{:S(2)}) collective-permute-start(bf16[8,40,2304]{2,1,0:T(8,128)(2,1)} %pad_maximum_fusion.18), channel_id=1, source_target_pairs={{0,2},{1,3},{2,0},{3,1},{4,6},{5,7},{6,4},{7,5},{8,10},{9,11},{10,... | collective-permute-start | bytes 4423688 | tf_op jit(solution)/shard_map/ppermute | solution.py:513
  151.7 49.7 %collective-permute-start.23 = (bf16[8,40,2304]{2,1,0:T(8,128)(2,1)}, bf16[8,40,2304]{2,1,0:T(8,128)(2,1)}, u32[]{:S(2)}, u32[]{:S(2)}) collective-permute-start(bf16[8,40,2304]{2,1,0:T(8,128)(2,1)} %pad_maximum_fusion.17), channel_id=1, source_target_pairs={{0,4},{1,5},{2,6},{3,7},{4,0},{5,1},{6,2},{7,3},{8,12},{9,13},{10,... | collective-permute-start | bytes 4423688 | tf_op jit(solution)/shard_map/ppermute | solution.py:513
  174.5 32.2 %collective-permute-start.27 = (bf16[4,40,2304]{2,1,0:T(8,128)(2,1)}, bf16[4,40,2304]{2,1,0:T(8,128)(2,1)}, u32[]{:S(2)}, u32[]{:S(2)}) collective-permute-start(bf16[4,40,2304]{2,1,0:T(8,128)(2,1)} %pad_maximum_fusion.39), channel_id=1, source_target_pairs={{0,2},{1,3},{2,0},{3,1},{4,6},{5,7},{6,4},{7,5},{8,10},{9,11},{10,... | collective-permute-start | bytes 2211848 | tf_op jit(solution)/shard_map/ppermute | solution.py:513
  223.7 28.6 %collective-permute-start.29 = (bf16[1,40,4608]{2,1,0:T(8,128)(2,1)S(1)}, bf16[1,40,4608]{2,1,0:T(8,128)(2,1)}, u32[]{:S(2)}, u32[]{:S(2)}) collective-permute-start(bf16[1,40,4608]{2,1,0:T(8,128)(2,1)S(1)} %get-tuple-element.221), channel_id=1, source_target_pairs={{0,8},{8,16},{16,24},{24,0},{1,9},{9,17},{17,25},{25,1},{2,10},{10... | collective-permute-start | bytes 1105928 | tf_op jit(solution)/shard_map/ppermute | solution.py:517
  248.8 53.2 %collective-permute-start.33 = (bf16[8,40,2304]{2,1,0:T(8,128)(2,1)}, bf16[8,40,2304]{2,1,0:T(8,128)(2,1)}, u32[]{:S(2)}, u32[]{:S(2)}) collective-permute-start(bf16[8,40,2304]{2,1,0:T(8,128)(2,1)} %pad_maximum_fusion.20), channel_id=1, source_target_pairs={{0,2},{1,3},{2,0},{3,1},{4,6},{5,7},{6,4},{7,5},{8,10},{9,11},{10,... | collective-permute-start | bytes 4423688 | tf_op jit(solution)/shard_map/ppermute | solution.py:513
  250.7 54.8 %collective-permute-start.32 = (bf16[8,40,2304]{2,1,0:T(8,128)(2,1)}, bf16[8,40,2304]{2,1,0:T(8,128)(2,1)}, u32[]{:S(2)}, u32[]{:S(2)}) collective-permute-start(bf16[8,40,2304]{2,1,0:T(8,128)(2,1)} %pad_maximum_fusion.19), channel_id=1, source_target_pairs={{0,4},{1,5},{2,6},{3,7},{4,0},{5,1},{6,2},{7,3},{8,12},{9,13},{10,... | collective-permute-start | bytes 4423688 | tf_op jit(solution)/shard_map/ppermute | solution.py:513
  309.3 30.4 %collective-permute-start.34 = (bf16[640,2304]{1,0:T(8,128)(2,1)}, bf16[640,2304]{1,0:T(8,128)(2,1)}, u32[]{:S(2)}, u32[]{:S(2)}) collective-permute-start(bf16[640,2304]{1,0:T(8,128)(2,1)} %bitcast.56), channel_id=1, source_target_pairs={{0,1},{1,0},{2,3},{3,2},{4,5},{5,4},{6,7},{7,6},{8,9},{9,8},{10,11... | collective-permute-start | bytes 8847368 | tf_op jit(solution)/shard_map/ppermute | solution.py:513
  309.3 30.4 %collective-permute-start.35 = (bf16[640,2304]{1,0:T(8,128)(2,1)}, bf16[640,2304]{1,0:T(8,128)(2,1)}, u32[]{:S(2)}, u32[]{:S(2)}) collective-permute-start(bf16[640,2304]{1,0:T(8,128)(2,1)} %bitcast.57), channel_id=1, source_target_pairs={{0,1},{1,0},{2,3},{3,2},{4,5},{5,4},{6,7},{7,6},{8,9},{9,8},{10,11... | collective-permute-start | bytes 8847368 | tf_op jit(solution)/shard_map/ppermute | solution.py:513
  315.5 143.7 %collective-permute-start.90 = (bf16[512,1280]{1,0:T(8,128)(2,1)}, bf16[512,1280]{1,0:T(8,128)(2,1)}, u32[]{:S(2)}, u32[]{:S(2)}) collective-permute-start(bf16[512,1280]{1,0:T(8,128)(2,1)} %bitcast.908), channel_id=1, source_target_pairs={{0,1},{1,0},{2,3},{3,2},{4,5},{5,4},{6,7},{7,6},{8,9},{9,8},{10,11... | collective-permute-start | bytes 3932168 | tf_op jit(solution)/shard_map/ppermute | solution.py:513
  353.8 826.6 %reduce-scatter.2.cloned.1.call-start = ((), (), s32[]{:S(2)}) async-start(), calls=%async_computation.5 | async-start | bytes 663552 | tf_op jit(solution)/shard_map/reduce_scatter | solution.py:983
  355.1 46.2 %collective-permute-start.42 = (bf16[8,40,2304]{2,1,0:T(8,128)(2,1)}, bf16[8,40,2304]{2,1,0:T(8,128)(2,1)}, u32[]{:S(2)}, u32[]{:S(2)}) collective-permute-start(bf16[8,40,2304]{2,1,0:T(8,128)(2,1)} %pad_maximum_fusion.22), channel_id=1, source_target_pairs={{0,2},{1,3},{2,0},{3,1},{4,6},{5,7},{6,4},{7,5},{8,10},{9,11},{10,... | collective-permute-start | bytes 4423688 | tf_op jit(solution)/shard_map/ppermute | solution.py:513
  364.7 38.9 %collective-permute-start.41 = (bf16[8,40,2304]{2,1,0:T(8,128)(2,1)}, bf16[8,40,2304]{2,1,0:T(8,128)(2,1)}, u32[]{:S(2)}, u32[]{:S(2)}) collective-permute-start(bf16[8,40,2304]{2,1,0:T(8,128)(2,1)} %pad_maximum_fusion.21), channel_id=1, source_target_pairs={{0,4},{1,5},{2,6},{3,7},{4,0},{5,1},{6,2},{7,3},{8,12},{9,13},{10,... | collective-permute-start | bytes 4423688 | tf_op jit(solution)/shard_map/ppermute | solution.py:513
  423.4 37.0 %collective-permute-start.92 = (bf16[512,1280]{1,0:T(8,128)(2,1)}, bf16[512,1280]{1,0:T(8,128)(2,1)}, u32[]{:S(2)}, u32[]{:S(2)}) collective-permute-start(bf16[512,1280]{1,0:T(8,128)(2,1)} %bitcast.226), channel_id=1, source_target_pairs={{0,1},{1,0},{2,3},{3,2},{4,5},{5,4},{6,7},{7,6},{8,9},{9,8},{10,11... | collective-permute-start | bytes 3932168 | tf_op jit(solution)/shard_map/ppermute | solution.py:513
  423.5 37.4 %collective-permute-start.76 = (bf16[512,1280]{1,0:T(8,128)(2,1)}, bf16[512,1280]{1,0:T(8,128)(2,1)}, u32[]{:S(2)}, u32[]{:S(2)}) collective-permute-start(bf16[512,1280]{1,0:T(8,128)(2,1)} %bitcast.182), channel_id=1, source_target_pairs={{0,1},{1,0},{2,3},{3,2},{4,5},{5,4},{6,7},{7,6},{8,9},{9,8},{10,11... | collective-permute-start | bytes 3932168 | tf_op jit(solution)/shard_map/ppermute | solution.py:513
  424.5 31.2 %collective-permute-start.48 = (bf16[4,2,1,1,72,1152]{5,4,3,2,1,0:T(8,128)(2,1)S(1)}, bf16[4,2,1,1,72,1152]{5,4,3,2,1,0:T(8,128)(2,1)S(1)}, u32[]{:S(2)}, u32[]{:S(2)}) collective-permute-start(bf16[4,2,1,1,72,1152]{5,4,3,2,1,0:T(8,128)(2,1)S(1)} %pad_maximum_fusion.30), channel_id=1, source_target_pairs={{0,2},{1,3},{2,0},{3,1},{4,6},{5,7},{6,4},{7,5},{8,10},{9,11},{10,... | collective-permute-start | bytes 3981320 | tf_op jit(solution)/shard_map/ppermute | solution.py:513
  425.8 31.3 %collective-permute-start.47 = (bf16[4,1,2,1,72,1152]{5,4,3,2,1,0:T(8,128)(2,1)S(1)}, bf16[4,1,2,1,72,1152]{5,4,3,2,1,0:T(8,128)(2,1)S(1)}, u32[]{:S(2)}, u32[]{:S(2)}) collective-permute-start(bf16[4,1,2,1,72,1152]{5,4,3,2,1,0:T(8,128)(2,1)S(1)} %pad_maximum_fusion.29), channel_id=1, source_target_pairs={{0,4},{1,5},{2,6},{3,7},{4,0},{5,1},{6,2},{7,3},{8,12},{9,13},{10,... | collective-permute-start | bytes 3981320 | tf_op jit(solution)/shard_map/ppermute | solution.py:513
  470.1 30.1 %collective-permute-start.52 = (bf16[512,640]{1,0:T(8,128)(2,1)}, bf16[512,640]{1,0:T(8,128)(2,1)}, u32[]{:S(2)}, u32[]{:S(2)}) collective-permute-start(bf16[512,640]{1,0:T(8,128)(2,1)} %get-tuple-element.501), channel_id=1, source_target_pairs={{0,1},{1,0},{2,3},{3,2},{4,5},{5,4},{6,7},{7,6},{8,9},{9,8},{10,11... | collective-permute-start | bytes 1966088 | tf_op jit(solution)/shard_map/ppermute | solution.py:513
  528.8 45.2 %collective-permute-start.54 = (bf16[512,2304]{1,0:T(8,128)(2,1)}, bf16[512,2304]{1,0:T(8,128)(2,1)}, u32[]{:S(2)}, u32[]{:S(2)}) collective-permute-start(bf16[512,2304]{1,0:T(8,128)(2,1)} %get-tuple-element.415), channel_id=1, source_target_pairs={{0,1},{1,0},{2,3},{3,2},{4,5},{5,4},{6,7},{7,6},{8,9},{9,8},{10,11... | collective-permute-start | bytes 7077896 | tf_op jit(solution)/shard_map/ppermute | solution.py:513
  530.9 41.4 %collective-permute-start.55 = (bf16[4,2,2,144,384]{4,3,2,1,0:T(8,128)(2,1)}, bf16[4,2,2,144,384]{4,3,2,1,0:T(8,128)(2,1)}, u32[]{:S(2)}, u32[]{:S(2)}) collective-permute-start(bf16[4,2,2,144,384]{4,3,2,1,0:T(8,128)(2,1)} %dynamic-slice_bitcast_fusion), channel_id=1, source_target_pairs={{0,4},{1,5},{2,6},{3,7},{4,0},{5,1},{6,2},{7,3},{8,12},{9,13},{10,... | collective-permute-start | bytes 5308424 | tf_op jit(solution)/shard_map/ppermute | solution.py:513
  533.6 28.3 %collective-permute-start.56 = (bf16[4,2,2,144,256]{4,3,2,1,0:T(8,128)(2,1)S(1)}, bf16[4,2,2,144,256]{4,3,2,1,0:T(8,128)(2,1)}, u32[]{:S(2)}, u32[]{:S(2)}) collective-permute-start(bf16[4,2,2,144,256]{4,3,2,1,0:T(8,128)(2,1)S(1)} %dynamic-slice_bitcast_fusion.1), channel_id=1, source_target_pairs={{0,2},{1,3},{2,0},{3,1},{4,6},{5,7},{6,4},{7,5},{8,10},{9,11},{10,... | collective-permute-start | bytes 3538952 | tf_op jit(solution)/shard_map/ppermute | solution.py:513
  591.4 88.1 %collective-permute-start.60 = (bf16[2,2,4,40,1152]{4,3,0,2,1:T(8,128)(2,1)}, bf16[2,2,4,40,1152]{4,3,0,2,1:T(8,128)(2,1)}, u32[]{:S(2)}, u32[]{:S(2)}) collective-permute-start(bf16[2,2,4,40,1152]{4,3,0,2,1:T(8,128)(2,1)} %bitcast.825), channel_id=1, source_target_pairs={{0,2},{1,3},{2,0},{3,1},{4,6},{5,7},{6,4},{7,5},{8,10},{9,11},{10,... | collective-permute-start | bytes 4423688 | tf_op jit(solution)/shard_map/ppermute | solution.py:513
  594.7 86.5 %collective-permute-start.59 = (bf16[2,2,4,40,1152]{4,3,0,2,1:T(8,128)(2,1)}, bf16[2,2,4,40,1152]{4,3,0,2,1:T(8,128)(2,1)}, u32[]{:S(2)}, u32[]{:S(2)}) collective-permute-start(bf16[2,2,4,40,1152]{4,3,0,2,1:T(8,128)(2,1)} %bitcast.826), channel_id=1, source_target_pairs={{0,4},{1,5},{2,6},{3,7},{4,0},{5,1},{6,2},{7,3},{8,12},{9,13},{10,... | collective-permute-start | bytes 4423688 | tf_op jit(solution)/shard_map/ppermute | solution.py:513
  597.2 47.4 %collective-permute-start.57 = (bf16[4,2,144,384]{3,2,1,0:T(8,128)(2,1)}, bf16[4,2,144,384]{3,2,1,0:T(8,128)(2,1)}, u32[]{:S(2)}, u32[]{:S(2)}) collective-permute-start(bf16[4,2,144,384]{3,2,1,0:T(8,128)(2,1)} %dynamic-slice_bitcast_fusion.2), channel_id=1, source_target_pairs={{0,2},{1,3},{2,0},{3,1},{4,6},{5,7},{6,4},{7,5},{8,10},{9,11},{10,... | collective-permute-start | bytes 2654216 | tf_op jit(solution)/shard_map/ppermute | solution.py:513
  599.4 41.6 %collective-permute-start.58 = (bf16[4,2,144,256]{3,2,1,0:T(8,128)(2,1)}, bf16[4,2,144,256]{3,2,1,0:T(8,128)(2,1)}, u32[]{:S(2)}, u32[]{:S(2)}) collective-permute-start(bf16[4,2,144,256]{3,2,1,0:T(8,128)(2,1)} %dynamic-slice_bitcast_fusion.3), channel_id=1, source_target_pairs={{0,4},{1,5},{2,6},{3,7},{4,0},{5,1},{6,2},{7,3},{8,12},{9,13},{10,... | collective-permute-start | bytes 1769480 | tf_op jit(solution)/shard_map/ppermute | solution.py:513
  733.0 102.8 %collective-permute-start.75 = (bf16[2,2,4,40,1152]{4,3,0,2,1:T(8,128)(2,1)}, bf16[2,2,4,40,1152]{4,3,0,2,1:T(8,128)(2,1)}, u32[]{:S(2)}, u32[]{:S(2)}) collective-permute-start(bf16[2,2,4,40,1152]{4,3,0,2,1:T(8,128)(2,1)} %bitcast.823), channel_id=1, source_target_pairs={{0,2},{1,3},{2,0},{3,1},{4,6},{5,7},{6,4},{7,5},{8,10},{9,11},{10,... | collective-permute-start | bytes 4423688 | tf_op jit(solution)/shard_map/ppermute | solution.py:513
  736.2 101.8 %collective-permute-start.74 = (bf16[2,2,4,40,1152]{4,3,0,2,1:T(8,128)(2,1)}, bf16[2,2,4,40,1152]{4,3,0,2,1:T(8,128)(2,1)}, u32[]{:S(2)}, u32[]{:S(2)}) collective-permute-start(bf16[2,2,4,40,1152]{4,3,0,2,1:T(8,128)(2,1)} %bitcast.824), channel_id=1, source_target_pairs={{0,4},{1,5},{2,6},{3,7},{4,0},{5,1},{6,2},{7,3},{8,12},{9,13},{10,... | collective-permute-start | bytes 4423688 | tf_op jit(solution)/shard_map/ppermute | solution.py:513
  745.8 35.8 %collective-permute-start.72 = (bf16[2,40,2304]{2,1,0:T(8,128)(2,1)}, bf16[2,40,2304]{2,1,0:T(8,128)(2,1)}, u32[]{:S(2)}, u32[]{:S(2)}) collective-permute-start(bf16[2,40,2304]{2,1,0:T(8,128)(2,1)} %get-tuple-element.466), channel_id=1, source_target_pairs={{0,16},{8,24},{16,0},{24,8},{1,17},{9,25},{17,1},{25,9},{2,18},{10... | collective-permute-start | bytes 1105928 | tf_op jit(solution)/shard_map/ppermute | solution.py:517
  750.8 32.8 %all-to-all-start.2 = ((bf16[1,2,256,1152]{3,1,0,2:T(2,128)(2,1)}), bf16[1,2,256,1152]{3,1,0,2:T(2,128)(2,1)}, u32[]{:S(2)}, u32[]{:S(2)}) async-start(bf16[1,2,256,1152]{3,1,0,2:T(2,128)(2,1)} %copy.232), calls=%async_computation.2 | async-start | bytes 2359296 | tf_op jit(solution)/shard_map/all_to_all | solution.py:915
  885.7 66.8 %collective-permute-start.84 = (bf16[2,2,4,40,1152]{4,3,0,2,1:T(8,128)(2,1)}, bf16[2,2,4,40,1152]{4,3,0,2,1:T(8,128)(2,1)}, u32[]{:S(2)}, u32[]{:S(2)}) collective-permute-start(bf16[2,2,4,40,1152]{4,3,0,2,1:T(8,128)(2,1)} %bitcast.821), channel_id=1, source_target_pairs={{0,2},{1,3},{2,0},{3,1},{4,6},{5,7},{6,4},{7,5},{8,10},{9,11},{10,... | collective-permute-start | bytes 4423688 | tf_op jit(solution)/shard_map/ppermute | solution.py:513
  889.9 46.6 %all-to-all-start.3 = ((bf16[1,16,32,1152]{3,2,0,1:T(8,128)(2,1)}), bf16[1,16,32,1152]{3,2,0,1:T(8,128)(2,1)S(1)}, u32[]{:S(2)}, u32[]{:S(2)}) async-start(bf16[1,16,32,1152]{3,2,0,1:T(8,128)(2,1)} %bitcast.923), calls=%async_computation.3 | async-start | bytes 2359296 | tf_op jit(solution)/shard_map/all_to_all | solution.py:941
  900.9 34.6 %collective-permute-start.86 = (bf16[2,40,2304]{2,1,0:T(8,128)(2,1)S(1)}, bf16[2,40,2304]{2,1,0:T(8,128)(2,1)S(1)}, u32[]{:S(2)}, u32[]{:S(2)}) collective-permute-start(bf16[2,40,2304]{2,1,0:T(8,128)(2,1)S(1)} %get-tuple-element.463), channel_id=1, source_target_pairs={{0,16},{8,24},{16,0},{24,8},{1,17},{9,25},{17,1},{25,9},{2,18},{10... | collective-permute-start | bytes 1105928 | tf_op jit(solution)/shard_map/ppermute | solution.py:517
  902.9 32.6 %collective-permute-start.87 = (bf16[2,40,2304]{2,1,0:T(8,128)(2,1)S(1)}, bf16[2,40,2304]{2,1,0:T(8,128)(2,1)S(1)}, u32[]{:S(2)}, u32[]{:S(2)}) collective-permute-start(bf16[2,40,2304]{2,1,0:T(8,128)(2,1)S(1)} %get-tuple-element.462), channel_id=1, source_target_pairs={{0,8},{8,16},{16,24},{24,0},{1,9},{9,17},{17,25},{25,1},{2,10},{10... | collective-permute-start | bytes 1105928 | tf_op jit(solution)/shard_map/ppermute | solution.py:517
  907.3 47.4 %collective-permute-start.83 = (bf16[2,2,4,40,1152]{4,3,0,2,1:T(8,128)(2,1)}, bf16[2,2,4,40,1152]{4,3,0,2,1:T(8,128)(2,1)}, u32[]{:S(2)}, u32[]{:S(2)}) collective-permute-start(bf16[2,2,4,40,1152]{4,3,0,2,1:T(8,128)(2,1)} %bitcast.822), channel_id=1, source_target_pairs={{0,4},{1,5},{2,6},{3,7},{4,0},{5,1},{6,2},{7,3},{8,12},{9,13},{10,... | collective-permute-start | bytes 4423688 | tf_op jit(solution)/shard_map/ppermute | solution.py:513
  994.6 50.5 %collective-permute-start.93 = (bf16[512,1152]{1,0:T(8,128)(2,1)}, bf16[512,1152]{1,0:T(8,128)(2,1)}, u32[]{:S(2)}, u32[]{:S(2)}) collective-permute-start(bf16[512,1152]{1,0:T(8,128)(2,1)} %get-tuple-element.442), channel_id=1, source_target_pairs={{0,1},{1,0},{2,3},{3,2},{4,5},{5,4},{6,7},{7,6},{8,9},{9,8},{10,11... | collective-permute-start | bytes 3538952 | tf_op jit(solution)/shard_map/ppermute | solution.py:513
  1001.3 35.8 %collective-permute-start.91 = (bf16[512,1152]{1,0:T(8,128)(2,1)S(1)}, bf16[512,1152]{1,0:T(8,128)(2,1)S(1)}, u32[]{:S(2)}, u32[]{:S(2)}) collective-permute-start(bf16[512,1152]{1,0:T(8,128)(2,1)S(1)} %bitcast.921), channel_id=1, source_target_pairs={{0,1},{1,0},{2,3},{3,2},{4,5},{5,4},{6,7},{7,6},{8,9},{9,8},{10,11... | collective-permute-start | bytes 3538952 | tf_op jit(solution)/shard_map/ppermute | solution.py:513
  1002.2 33.7 %collective-permute-start.95 = (bf16[2,40,2304]{2,1,0:T(8,128)(2,1)S(1)}, bf16[2,40,2304]{2,1,0:T(8,128)(2,1)S(1)}, u32[]{:S(2)}, u32[]{:S(2)}) collective-permute-start(bf16[2,40,2304]{2,1,0:T(8,128)(2,1)S(1)} %get-tuple-element.460), channel_id=1, source_target_pairs={{0,16},{8,24},{16,0},{24,8},{1,17},{9,25},{17,1},{25,9},{2,18},{10... | collective-permute-start | bytes 1105928 | tf_op jit(solution)/shard_map/ppermute | solution.py:517
  1003.6 32.4 %collective-permute-start.96 = (bf16[2,40,2304]{2,1,0:T(8,128)(2,1)S(1)}, bf16[2,40,2304]{2,1,0:T(8,128)(2,1)S(1)}, u32[]{:S(2)}, u32[]{:S(2)}) collective-permute-start(bf16[2,40,2304]{2,1,0:T(8,128)(2,1)S(1)} %get-tuple-element.459), channel_id=1, source_target_pairs={{0,8},{8,16},{16,24},{24,0},{1,9},{9,17},{17,25},{25,1},{2,10},{10... | collective-permute-start | bytes 1105928 | tf_op jit(solution)/shard_map/ppermute | solution.py:517
  1060.5 34.0 %collective-permute-start.98 = (bf16[2,2,4,40,1152]{4,3,0,2,1:T(8,128)(2,1)}, bf16[2,2,4,40,1152]{4,3,0,2,1:T(8,128)(2,1)}, u32[]{:S(2)}, u32[]{:S(2)}) collective-permute-start(bf16[2,2,4,40,1152]{4,3,0,2,1:T(8,128)(2,1)} %bitcast.819), channel_id=1, source_target_pairs={{0,2},{1,3},{2,0},{3,1},{4,6},{5,7},{6,4},{7,5},{8,10},{9,11},{10,... | collective-permute-start | bytes 4423688 | tf_op jit(solution)/shard_map/ppermute | solution.py:513
  1068.7 33.4 %collective-permute-start.97 = (bf16[2,2,4,40,1152]{4,3,0,2,1:T(8,128)(2,1)}, bf16[2,2,4,40,1152]{4,3,0,2,1:T(8,128)(2,1)}, u32[]{:S(2)}, u32[]{:S(2)}) collective-permute-start(bf16[2,2,4,40,1152]{4,3,0,2,1:T(8,128)(2,1)} %bitcast.820), channel_id=1, source_target_pairs={{0,4},{1,5},{2,6},{3,7},{4,0},{5,1},{6,2},{7,3},{8,12},{9,13},{10,... | collective-permute-start | bytes 4423688 | tf_op jit(solution)/shard_map/ppermute | solution.py:513
  1132.7 40.5 %collective-permute-start.109 = (bf16[2,40,2304]{2,1,0:T(8,128)(2,1)S(1)}, bf16[2,40,2304]{2,1,0:T(8,128)(2,1)S(1)}, u32[]{:S(2)}, u32[]{:S(2)}) collective-permute-start(bf16[2,40,2304]{2,1,0:T(8,128)(2,1)S(1)} %get-tuple-element.457), channel_id=1, source_target_pairs={{0,16},{8,24},{16,0},{24,8},{1,17},{9,25},{17,1},{25,9},{2,18},{10... | collective-permute-start | bytes 1105928 | tf_op jit(solution)/shard_map/ppermute | solution.py:517
  1135.4 37.8 %collective-permute-start.110 = (bf16[2,40,2304]{2,1,0:T(8,128)(2,1)S(1)}, bf16[2,40,2304]{2,1,0:T(8,128)(2,1)S(1)}, u32[]{:S(2)}, u32[]{:S(2)}) collective-permute-start(bf16[2,40,2304]{2,1,0:T(8,128)(2,1)S(1)} %get-tuple-element.456), channel_id=1, source_target_pairs={{0,8},{8,16},{16,24},{24,0},{1,9},{9,17},{17,25},{25,1},{2,10},{10... | collective-permute-start | bytes 1105928 | tf_op jit(solution)/shard_map/ppermute | solution.py:517
  1144.1 29.4 %collective-permute-start.105 = (f32[1,20,1152]{2,1,0:T(8,128)S(1)}, f32[1,20,1152]{2,1,0:T(8,128)S(1)}, u32[]{:S(2)}, u32[]{:S(2)}) collective-permute-start(f32[1,20,1152]{2,1,0:T(8,128)S(1)} %bitcast.936), channel_id=1, source_target_pairs={{0,8},{8,16},{16,24},{24,0},{1,9},{9,17},{17,25},{25,1},{2,10},{10... | collective-permute-start | bytes 276488 | tf_op jit(solution)/shard_map/ppermute | solution.py:517
  1144.4 31.2 %collective-permute-start.106 = (f32[1,20,1152]{2,1,0:T(8,128)S(1)}, f32[1,20,1152]{2,1,0:T(8,128)S(1)}, u32[]{:S(2)}, u32[]{:S(2)}) collective-permute-start(f32[1,20,1152]{2,1,0:T(8,128)S(1)} %bitcast.937), channel_id=1, source_target_pairs={{0,16},{8,24},{16,0},{24,8},{1,17},{9,25},{17,1},{25,9},{2,18},{10... | collective-permute-start | bytes 276488 | tf_op jit(solution)/shard_map/ppermute | solution.py:517
  1146.6 29.0 %collective-permute-start.107 = (f32[1,20,1152]{2,1,0:T(8,128)S(1)}, f32[1,20,1152]{2,1,0:T(8,128)S(1)}, u32[]{:S(2)}, u32[]{:S(2)}) collective-permute-start(f32[1,20,1152]{2,1,0:T(8,128)S(1)} %bitcast.938), channel_id=1, source_target_pairs={{0,24},{8,0},{16,8},{24,16},{1,25},{9,1},{17,9},{25,17},{2,26},{10... | collective-permute-start | bytes 276488 | tf_op jit(solution)/shard_map/ppermute | solution.py:517
  (279 other events, 3412.1 us)
Sparse Core Ops, SparseCore 0:
  708.7 40.4 reduce-scatter.1
